TPU v7x, 32 devices: a whole 2x2x4 slice. The times are simulated.
32 devices in a mesh: shard: 8 (over y, x, core), seq: 4 (over z).
Axes of the slice: x: 2, y: 2, z: 4, core: 2. Of those that a mesh axis runs over, the one named last changes fastest.
Arguments:
- hidden_in: bfloat16 [16, 1024, 1024], P('shard', 'seq'), may hold values from -6 to 6
- condition: bfloat16 [16, 1024], P('shard'), may hold values from -6 to 6
- out_grad: bfloat16 [16, 1024, 1024], P('shard', 'seq'), may hold values from -6 to 6
- ada_weight: bfloat16 [1024, 6144], P(('shard', 'seq')), may hold values from -0.1875 to 0.1875
- qkv_weight: bfloat16 [1024, 3072], P(('shard', 'seq')), may hold values from -0.1875 to 0.1875
- proj_weight: bfloat16 [1024, 1024], P(('shard', 'seq')), may hold values from -1.5 to 1.5
- up_weight: bfloat16 [1024, 4096], P(('shard', 'seq')), may hold values from -0.1875 to 0.1875
- down_weight: bfloat16 [4096, 1024], P(('shard', 'seq')), may hold values from -0.09375 to 0.09375
- ada_bias: bfloat16 [6144], P(('shard', 'seq')), may hold values from -3 to 3
- qv_bias: bfloat16 [2048], P(('shard', 'seq')), may hold values from -3 to 3
- proj_bias: bfloat16 [1024], P(('shard', 'seq')), may hold values from -3 to 3
- up_bias: bfloat16 [4096], P(('shard', 'seq')), may hold values from -3 to 3
- down_bias: bfloat16 [1024], P(('shard', 'seq')), may hold values from -3 to 3
Outputs:
- block_out: bfloat16 [16, 1024, 1024], P('shard', 'seq')
- hidden_grad: float32 [16, 1024, 1024], P('shard', 'seq')
- condition_grad: float32 [16, 1024], P('shard')
- ada_grad: float32 [1024, 6144], P(('shard', 'seq'))
- qkv_grad: float32 [1024, 3072], P(('shard', 'seq'))
- proj_grad: float32 [1024, 1024], P(('shard', 'seq'))
- up_grad: float32 [1024, 4096], P(('shard', 'seq'))
- down_grad: float32 [4096, 1024], P(('shard', 'seq'))
- adabias_grad: float32 [6144], P(('shard', 'seq'))
- qvbias_grad: float32 [2048], P(('shard', 'seq'))
- projbias_grad: float32 [1024], P(('shard', 'seq'))
- upbias_grad: float32 [4096], P(('shard', 'seq'))
- downbias_grad: float32 [1024], P(('shard', 'seq'))
All inputs are finite; a program needn't handle non-finite values.
Results may differ from a plain program's by a relative error of at most 0.013.
The roundings to bfloat16 on the way count: a program that leaves them out, or rounds other values in their place, can miss the bound.
Values may be sent and summed in bfloat16 or wider, within the bound.
No kernel may reach another device: no remote copies, remote signals or barrier semaphores. Data moves between devices by JAX's collectives and lax.ppermute only.
A program may use at most 256 MiB of HBM per device.

v0:
```python
from functools import partial

import jax
import jax.numpy as jnp
from jax import lax
from jax.sharding import PartitionSpec as P

HD = 64


EPS = 1e-06


def shortened(shard):

    def short(part):
        return part.astype(jnp.bfloat16) if part.dtype == jnp.float32 else part

    return jax.tree.map(short, shard)


def modulate(tokens, shift_by, scale_by):
    average = jnp.mean(tokens, axis=-1, keepdims=True)
    centered = tokens - average
    variance = jnp.mean(centered * centered, axis=-1, keepdims=True)
    return centered * lax.rsqrt(variance + EPS) * (1.0 + scale_by) + shift_by


def cross_rows(left, right):
    return lax.dot_general(
        left, right, (((0,), (0,)), ((), ())), preferred_element_type=jnp.float32
    )


def along_cols(left, right):
    return lax.dot_general(
        left, right, (((1,), (1,)), ((), ())), preferred_element_type=jnp.float32
    )


def flat_rows(matrix):
    return matrix.reshape(-1, 128)


def own_rows(received, like, devices):
    return received.reshape(like.shape[0] // devices, like.shape[1])


def split_heads(latent_item):
    length = latent_item.shape[0]
    head_count = latent_item.shape[-1] // HD
    return [latent_item[:, member, 0].reshape(length, head_count, HD) for member in range(3)]


def attend_forward(packed):
    factor = HD ** (-0.5)

    def one_latent(latent_item):
        queries, key_rows, value_rows = split_heads(latent_item)
        length = queries.shape[0]
        block = min(512, length)
        outputs = []
        log_parts = []
        for begin in range(0, length, block):
            query_block = queries[begin : begin + block]
            scores = factor * jnp.einsum(
                "qhd,khd->hqk", query_block, key_rows, preferred_element_type=jnp.float32
            )
            highest = jnp.max(scores, axis=-1, keepdims=True)
            expon = jnp.exp(scores - highest)
            summed = jnp.sum(expon, axis=-1, keepdims=True)
            probs = (expon / summed).astype(jnp.bfloat16)
            mixed = jnp.einsum(
                "hqk,khd->qhd", probs, value_rows, preferred_element_type=jnp.float32
            )
            outputs.append(mixed.astype(jnp.bfloat16).reshape(block, 1, -1))
            log_parts.append((highest + jnp.log(summed))[..., 0])
        return (jnp.concatenate(outputs, 0), jnp.concatenate(log_parts, 1))

    mixed_all, log_sums = lax.map(one_latent, packed)
    return (mixed_all, log_sums, packed)


def attend_backward(packed, log_sums, grad_mixed):
    factor = HD ** (-0.5)

    def one_latent(operands):
        latent_item, log_rows, grad_item = operands
        queries, key_rows, value_rows = split_heads(latent_item)
        grad_rows = grad_item[:, 0].reshape(queries.shape)
        length = queries.shape[0]
        block = min(512, length)
        grad_keys = jnp.zeros(key_rows.shape, jnp.float32)
        grad_values = jnp.zeros(value_rows.shape, jnp.float32)
        grad_queries = []
        for begin in range(0, length, block):
            query_block = queries[begin : begin + block]
            grad_block = grad_rows[begin : begin + block]
            scores = factor * jnp.einsum(
                "qhd,khd->hqk", query_block, key_rows, preferred_element_type=jnp.float32
            )
            probs = jnp.exp(scores - log_rows[:, begin : begin + block, None])
            grad_probs = jnp.einsum(
                "qhd,khd->hqk", grad_block, value_rows, preferred_element_type=jnp.float32
            )
            inner = jnp.sum(probs * grad_probs, axis=-1, keepdims=True)
            grad_scores = (probs * (grad_probs - inner)).astype(jnp.bfloat16)
            grad_values = grad_values + jnp.einsum(
                "hqk,qhd->khd",
                probs.astype(jnp.bfloat16),
                grad_block,
                preferred_element_type=jnp.float32,
            )
            grad_queries.append(
                factor
                * jnp.einsum(
                    "hqk,khd->qhd", grad_scores, key_rows, preferred_element_type=jnp.float32
                )
            )
            grad_keys = grad_keys + factor * jnp.einsum(
                "hqk,qhd->khd", grad_scores, query_block, preferred_element_type=jnp.float32
            )
        stacked = jnp.stack([jnp.concatenate(grad_queries, 0), grad_keys, grad_values], 1).astype(
            jnp.bfloat16
        )
        return stacked.reshape(length, 3, 1, -1)

    return lax.map(one_latent, (packed, log_sums, grad_mixed))


def shards(
    hidden_in,
    condition,
    out_grad,
    ada_weight,
    qkv_weight,
    proj_weight,
    up_weight,
    down_weight,
    ada_bias,
    qv_bias,
    proj_bias,
    up_bias,
    down_bias,
):
    sharded = (
        ada_weight,
        qkv_weight,
        proj_weight,
        up_weight,
        down_weight,
        ada_bias,
        qv_bias,
        proj_bias,
        up_bias,
        down_bias,
    )
    gathered = (
        lax.all_gather(sharded[0], ("shard", "seq"), axis=0, tiled=True),
        lax.all_gather(sharded[1], ("shard", "seq"), axis=0, tiled=True),
        lax.all_gather(sharded[2], ("shard", "seq"), axis=0, tiled=True),
        lax.all_gather(sharded[3], ("shard", "seq"), axis=0, tiled=True),
        lax.all_gather(sharded[4], ("shard", "seq"), axis=0, tiled=True),
        lax.all_gather(sharded[5], ("shard", "seq"), axis=0, tiled=True),
        lax.all_gather(sharded[6], ("shard", "seq"), axis=0, tiled=True),
        lax.all_gather(sharded[7], ("shard", "seq"), axis=0, tiled=True),
        lax.all_gather(sharded[8], ("shard", "seq"), axis=0, tiled=True),
        lax.all_gather(sharded[9], ("shard", "seq"), axis=0, tiled=True),
    )
    w_ada, w_qkv, w_proj, w_up, w_down, b_ada, b_qv, b_proj, b_up, b_down = gathered
    latents, local_len, model_width = hidden_in.shape
    row_count = latents * local_len
    groups = lax.axis_size("seq")
    devices = lax.axis_size("shard") * groups
    silu_low = jax.nn.silu(condition.astype(jnp.float32)).astype(jnp.bfloat16)
    modulation = jnp.dot(silu_low, w_ada, preferred_element_type=jnp.float32) + b_ada.astype(
        jnp.float32
    )
    pieces = modulation.reshape(latents, 6, 1, model_width)
    shift_a, scale_a, gate_a, shift_m, scale_m, gate_m = [pieces[:, member] for member in range(6)]
    tokens = hidden_in.astype(jnp.float32)
    normed = modulate(tokens, shift_a, scale_a).astype(jnp.bfloat16).reshape(row_count, model_width)
    qv_float = b_qv.astype(jnp.float32)
    full_bias = jnp.concatenate(
        [qv_float[:model_width], jnp.zeros((model_width,), jnp.float32), qv_float[model_width:]]
    )
    projected = (jnp.dot(normed, w_qkv, preferred_element_type=jnp.float32) + full_bias).astype(
        jnp.bfloat16
    )
    projected = projected.reshape(latents, local_len, 3, groups, model_width // groups)
    mixed_heads, log_sums, packed = attend_forward(
        lax.all_to_all(projected, "seq", split_axis=3, concat_axis=1, tiled=True)
    )
    mixed = jax.tree.map(
        lambda part, own: part.astype(own.dtype),
        lax.all_to_all(shortened(mixed_heads), "seq", split_axis=1, concat_axis=2, tiled=True),
        mixed_heads,
    ).reshape(row_count, model_width)
    attn_out = (
        jnp.dot(mixed, w_proj, preferred_element_type=jnp.float32) + b_proj.astype(jnp.float32)
    ).reshape(latents, local_len, model_width)
    middle = tokens + gate_a * attn_out
    normed_two = (
        modulate(middle, shift_m, scale_m).astype(jnp.bfloat16).reshape(row_count, model_width)
    )
    pre_act = jnp.dot(normed_two, w_up, preferred_element_type=jnp.float32) + b_up.astype(
        jnp.float32
    )
    hidden = jax.nn.gelu(pre_act, approximate=True).astype(jnp.bfloat16)
    mlp_out = (
        jnp.dot(hidden, w_down, preferred_element_type=jnp.float32) + b_down.astype(jnp.float32)
    ).reshape(latents, local_len, model_width)
    block_out = (middle + gate_m * mlp_out).astype(jnp.bfloat16)
    w_ada, w_qkv, w_proj, w_up, w_down = (
        lax.all_gather(ada_weight, ("shard", "seq"), axis=0, tiled=True),
        lax.all_gather(qkv_weight, ("shard", "seq"), axis=0, tiled=True),
        lax.all_gather(proj_weight, ("shard", "seq"), axis=0, tiled=True),
        lax.all_gather(up_weight, ("shard", "seq"), axis=0, tiled=True),
        lax.all_gather(down_weight, ("shard", "seq"), axis=0, tiled=True),
    )
    cotangent = out_grad.astype(jnp.float32)
    grad_gate_m = jnp.sum(cotangent * mlp_out, axis=1)
    grad_mlp = (gate_m * cotangent).astype(jnp.bfloat16).reshape(row_count, model_width)
    grad_down = cross_rows(hidden, grad_mlp)
    grad_bdown = jnp.sum(grad_mlp.astype(jnp.float32), axis=0)
    grad_hidden = along_cols(grad_mlp, w_down)
    _, gelu_back = jax.vjp(partial(jax.nn.gelu, approximate=True), pre_act)
    grad_pre = gelu_back(grad_hidden)[0].astype(jnp.bfloat16)
    grad_up = cross_rows(normed_two, grad_pre)
    grad_bup = jnp.sum(grad_pre.astype(jnp.float32), axis=0)
    grad_normed_two = along_cols(grad_pre, w_up).reshape(latents, local_len, model_width)
    _, second_back = jax.vjp(modulate, middle, shift_m, scale_m)
    grad_middle, grad_shift_m, grad_scale_m = second_back(grad_normed_two)
    grad_middle = grad_middle + cotangent
    grad_gate_a = jnp.sum(grad_middle * attn_out, axis=1)
    grad_attn = (gate_a * grad_middle).astype(jnp.bfloat16).reshape(row_count, model_width)
    grad_proj = cross_rows(mixed, grad_attn)
    grad_bproj = jnp.sum(grad_attn.astype(jnp.float32), axis=0)
    grad_mixed = (
        along_cols(grad_attn, w_proj)
        .astype(jnp.bfloat16)
        .reshape(latents, local_len, groups, model_width // groups)
    )
    heads_grad = lax.all_to_all(grad_mixed, "seq", split_axis=2, concat_axis=1, tiled=True)
    grad_packed = attend_backward(packed, log_sums, heads_grad)
    grad_rows = lax.all_to_all(grad_packed, "seq", split_axis=1, concat_axis=3, tiled=True).reshape(
        row_count, 3 * model_width
    )
    grad_qkv = cross_rows(normed, grad_rows)
    column_sums = jnp.sum(grad_rows.astype(jnp.float32), axis=0)
    grad_bqv = jnp.concatenate([column_sums[:model_width], column_sums[2 * model_width :]])
    grad_normed = along_cols(grad_rows, w_qkv).reshape(latents, local_len, model_width)
    _, first_back = jax.vjp(modulate, tokens, shift_a, scale_a)
    grad_tokens, grad_shift_a, grad_scale_a = first_back(grad_normed)
    hidden_grad = grad_tokens + grad_middle
    partial_mod = jnp.concatenate(
        [
            grad_shift_a[:, 0],
            grad_scale_a[:, 0],
            grad_gate_a,
            grad_shift_m[:, 0],
            grad_scale_m[:, 0],
            grad_gate_m,
        ],
        axis=-1,
    )
    grad_mod = lax.psum(partial_mod.astype(jnp.bfloat16), "seq")
    grad_silu = along_cols(grad_mod, w_ada)
    _, silu_back = jax.vjp(jax.nn.silu, condition.astype(jnp.float32))
    condition_grad = silu_back(grad_silu)[0]
    leading = (lax.axis_index("seq") == 0).astype(jnp.float32)
    grad_ada = cross_rows(silu_low, grad_mod) * leading
    grad_bada = jnp.sum(grad_mod.astype(jnp.float32), axis=0) * leading
    ada_flat, adabias_share = (
        lax.psum_scatter(flat_rows(grad_ada), ("shard", "seq"), scatter_dimension=0, tiled=True),
        lax.psum_scatter(grad_bada, ("shard", "seq"), scatter_dimension=0, tiled=True),
    )
    ada_share = own_rows(ada_flat, grad_ada, devices)
    shares = (
        lax.psum_scatter(flat_rows(grad_qkv), ("shard", "seq"), scatter_dimension=0, tiled=True),
        lax.psum_scatter(flat_rows(grad_proj), ("shard", "seq"), scatter_dimension=0, tiled=True),
        lax.psum_scatter(flat_rows(grad_up), ("shard", "seq"), scatter_dimension=0, tiled=True),
        lax.psum_scatter(flat_rows(grad_down), ("shard", "seq"), scatter_dimension=0, tiled=True),
        lax.psum_scatter(grad_bqv, ("shard", "seq"), scatter_dimension=0, tiled=True),
        lax.psum_scatter(grad_bproj, ("shard", "seq"), scatter_dimension=0, tiled=True),
        lax.psum_scatter(grad_bup, ("shard", "seq"), scatter_dimension=0, tiled=True),
        lax.psum_scatter(grad_bdown, ("shard", "seq"), scatter_dimension=0, tiled=True),
    )
    qkv_share = own_rows(shares[0], grad_qkv, devices)
    proj_share = own_rows(shares[1], grad_proj, devices)
    up_share = own_rows(shares[2], grad_up, devices)
    down_share = own_rows(shares[3], grad_down, devices)
    return (
        block_out,
        hidden_grad,
        condition_grad,
        ada_share,
        qkv_share,
        proj_share,
        up_share,
        down_share,
        adabias_share,
        shares[4],
        shares[5],
        shares[6],
        shares[7],
    )


def solution(mesh):
    in_specs = (
        P("shard", "seq", None),
        P("shard", None),
        P("shard", "seq", None),
        P(("shard", "seq"), None),
        P(("shard", "seq"), None),
        P(("shard", "seq"), None),
        P(("shard", "seq"), None),
        P(("shard", "seq"), None),
        P(("shard", "seq")),
        P(("shard", "seq")),
        P(("shard", "seq")),
        P(("shard", "seq")),
        P(("shard", "seq")),
    )
    out_specs = (
        P("shard", "seq", None),
        P("shard", "seq", None),
        P("shard", None),
        P(("shard", "seq"), None),
        P(("shard", "seq"), None),
        P(("shard", "seq"), None),
        P(("shard", "seq"), None),
        P(("shard", "seq"), None),
        P(("shard", "seq")),
        P(("shard", "seq")),
        P(("shard", "seq")),
        P(("shard", "seq")),
        P(("shard", "seq")),
    )
    return jax.shard_map(shards, mesh=mesh, in_specs=in_specs, out_specs=out_specs, check_vma=False)
```

profile of v0, /device:TPU:0, one launch (start us, length us, event | category | flops | bytes accessed | tf_op | source)
XLA Modules:
  0.0 1905.2 jit_solution(10022754701015661519)
XLA Ops:
  13.4 43.3 %all-reduce.10 = (bf16[6144]{0:T(1024)(128)(2,1)S(1)}, bf16[2048]{0:T(1024)(128)(2,1)S(1)}, bf16[1024]{0:T(1024)(128)(2,1)}, bf16[1024]{0:T(1024)(128)(2,1)}) all-reduce(bf16[6144]{0:T(1024)(128)(2,1)S(1)} %dynamic-update-slice, bf16[2048]{0:T(1024)(128)(2,1)S(1)} %dynamic-update-slice.1, ...), channel_id=1, replica_groups=mesh['shard'=8,'seq'=4] {'shard','seq'}, use_global_device_ids=true, to_apply=%add | all-reduce | flops 10240 | bytes 40960
  59.9 50.7 %all-gather.7.cloned.1.call-done = bf16[1024,6144]{1,0:T(8,128)(2,1)} async-done(((bf16[32,6144]{1,0:T(8,128)(2,1)}), bf16[1024,6144]{1,0:T(8,128)(2,1)}) %all-gather.7.cloned.1.call-update) | async-done | bytes 12582928 | tf_op jit(solution)/shard_map/all_gather | solution.py:159
  110.5 6.3 convolution_add_fusion.1
  118.7 62.6 %all-gather.9.cloned.1.call-done = bf16[1024,3072]{1,0:T(8,128)(2,1)} async-done(((bf16[32,3072]{1,0:T(8,128)(2,1)}), bf16[1024,3072]{1,0:T(8,128)(2,1)}) %all-gather.9.cloned.1.call-update) | async-done | bytes 6291472 | tf_op jit(solution)/shard_map/all_gather | solution.py:160
  181.2 7.5 add_convert_fusion
  188.8 5.5 reshape.258
  196.5 3.7 all-to-all-start
  200.9 79.3 %all-to-all-done = bf16[2,256,3,4,256]{4,1,2,0,3:T(8,128)(2,1)S(1)} async-done(((bf16[2,256,3,4,256]{4,1,2,0,3:T(8,128)(2,1)}), bf16[2,256,3,4,256]{4,1,2,0,3:T(8,128)(2,1)S(1)}, u32[]{:S(2)}, u32[]{:S(2)}) %all-to-all-start) | async-done | bytes 3145760 | tf_op jit(solution)/shard_map/all_to_all | solution.py:192
  282.1 3.2 copy.82
  285.3 24.6 %while.22 = (s32[]{:T(128)}, bf16[2,1024,1,256]{1,3,2,0:T(8,128)(2,1)}, f32[2,4,1024]{2,1,0:T(4,128)S(1)}, bf16[2,1024,3,1,256]{1,4,2,3,0:T(8,128)(2,1)S(1)}, s32[]{:T(128)}) while((s32[]{:T(128)}, bf16[2,1024,1,256]{1,3,2,0:T(8,128)(2,1)}, f32[2,4,1024]{2,1,0:T(4,128)S(1)}, bf16[2,1024,3,1,256]{1,4,2,3,0:T(8,128)(2,1)S(1)}, s32[]{:T(128)}) %tuple.102), condition=%wide.region_7.8_spmd, body=%wide.region_2.7_spmd.sunk | while | flops 1112801280 | bytes 60981828 | solution.py:80
  292.0 2.3 fusion.194
  294.4 2.3 fusion.192
  306.7 2.3 fusion.192
  309.9 3.7 copy.83
  313.6 4.3 all-to-all-start.1
  317.9 104.1 %all-gather = bf16[32,1,128]{2,1,0:T(2,128)(2,1)S(1)} all-gather(bf16[1,1,128]{2,1,0:T(2,128)(2,1)S(1)} %bitcast.304), channel_id=1, replica_groups=mesh['shard'=8,'seq'=4] {'shard','seq'}, dimensions={0}, use_global_device_ids=true | all-gather | bytes 8448 | tf_op jit(solution)/shard_map/all_gather | solution.py:167
  422.1 3.1 convert_reduce_fusion.3
  428.7 3.2 convolution_add_fusion.2
  436.1 11.5 fusion.84
  447.6 14.4 convert_reduce_fusion
  462.0 4.5 fusion.85
  468.0 21.9 %convolution_add_fusion.3 = f32[512,1024]{1,0:T(8,128)S(1)} fusion(bf16[4096,1024]{1,0:T(8,128)(2,1)} %all-gather.15.cloned.1.call-done, f32[1024]{0:T(1024)S(1)} %convert_element_type.126, f32[512,4096]{1,0:T(8,128)} %fusion.84, f32[4096]{0:T(1024)S(1)} %bitcast.300), kind=kOutput, calls=%fused_computation.105 | convolution fusion | flops 4316463104 | bytes 18894848 | tf_op jit(solution)/shard_map/dot_general | solution.py:211
  489.8 2.4 add_add_fusion.1
  494.1 3.1 convert_reduce_fusion.4
  500.4 2.7 reshape.266
  503.1 2.4 copy.86
  505.4 4.3 all-to-all-start.2
  509.8 4.8 fusion.87
  514.6 4.9 reshape.272
  519.6 25.8 %all-to-all-done.2 = bf16[2,256,4,256]{3,1,0,2:T(8,128)(2,1)} async-done(((bf16[2,256,4,256]{3,1,0,2:T(8,128)(2,1)}), bf16[2,256,4,256]{3,1,0,2:T(8,128)(2,1)}, u32[]{:S(2)}, u32[]{:S(2)}) %all-to-all-start.2) | async-done | bytes 1048608 | tf_op jit(solution)/shard_map/all_to_all | solution.py:244
  547.7 94.3 %while.23 = (s32[]{:T(128)}, bf16[2,1024,3,1,256]{1,4,3,2,0:T(8,128)(2,1)}, bf16[2,1024,3,1,256]{1,4,2,3,0:T(8,128)(2,1)S(1)}, f32[2,4,1024]{2,1,0:T(4,128)S(1)}...) while((s32[]{:T(128)}, bf16[2,1024,3,1,256]{1,4,3,2,0:T(8,128)(2,1)}, ...), condition=%wide.region_15.16_spmd, body=%wide.region_12.15_spmd.sunk | while | flops 2742284288 | bytes 237650704 | solution.py:128
  549.6 4.5 fusion.222
  554.4 6.7 multiply_reduce_fusion.14
  561.0 4.5 fusion.219
  565.7 7.6 multiply_reduce_fusion.13
  574.6 2.4 copy-done
  577.0 8.2 multiply_convert_fusion.8
  596.8 4.5 fusion.222
  601.6 6.6 multiply_reduce_fusion.14
  608.2 4.5 fusion.219
  612.9 7.6 multiply_reduce_fusion.13
  621.8 2.4 copy-done
  624.2 8.2 multiply_convert_fusion.8
  642.0 7.6 copy.90
  649.6 75.9 %all_to_all.66 = bf16[2,1024,3,1,256]{4,0,3,2,1:T(2,128)(2,1)S(1)} all-to-all(bf16[2,1024,3,1,256]{4,0,3,2,1:T(2,128)(2,1)S(1)} %copy.90), channel_id=1, replica_groups=mesh['shard'=8,'seq'=4] {'seq'}, dimensions={1} | all-to-all | bytes 6291456 | tf_op jit(solution)/shard_map/all_to_all | solution.py:246
  727.6 2.4 copy.92
  730.0 3.9 reshape.269
  733.9 10.2 fusion.86
  744.2 13.9 reshape.270
  759.3 10.8 fusion.88
  770.1 18.6 reshape.274
  790.0 16.2 fusion.70
  806.2 18.0 reshape.276
  824.3 6.5 dot_general.97
  831.0 7.0 fusion.53
  839.6 2.3 fusion.55
  842.0 19.8 %psum.7 = bf16[2,6144]{1,0:T(2,128)(2,1)S(1)} all-reduce(bf16[2,6144]{1,0:T(2,128)(2,1)S(1)} %constant_dynamic-update-slice_fusion), channel_id=1, replica_groups=mesh['shard'=8,'seq'=4] {'seq'}, use_global_device_ids=true, to_apply=%region_24.25 | all-reduce | flops 12288 | bytes 49152 | tf_op jit(solution)/shard_map/psum | solution.py:267
  861.8 10.5 broadcast_multiply_fusion
  872.4 26.3 %reshape.267 = f32[49152,128]{1,0:T(8,128)} reshape(f32[1024,6144]{1,0:T(8,128)} %broadcast_multiply_fusion) | data formatting | bytes 50331648 | tf_op jit(solution)/shard_map/reshape | solution.py:42
  901.2 39.0 %all-reduce.9 = (f32[6144]{0:T(1024)S(1)}, f32[2048]{0:T(1024)S(1)}, f32[1024]{0:T(1024)S(1)}, f32[4096]{0:T(1024)S(1)}, f32[1024]{0:T(1024)S(1)}) all-reduce(f32[6144]{0:T(1024)S(1)} %broadcast_multiply_fusion.1, f32[2048]{0:T(1024)S(1)} %pad_maximum_fusion.2, ...), channel_id=7, replica_groups=mesh['shard'=8,'seq'=4] {'shard','seq'}, use_global_device_ids=true, to_apply=%region_31.32.clone | all-reduce | flops 14336 | bytes 114688
  943.2 8.6 fusion.63
  955.2 325.5 %reduce-scatter.12.cloned.1.call-done = f32[1024,128]{1,0:T(8,128)} async-done(((f32[32768,128]{1,0:T(8,128)}), f32[1024,128]{1,0:T(8,128)}) %reduce-scatter.12.cloned.1.call-update) | async-done | bytes 524304 | tf_op jit(solution)/shard_map/reduce_scatter | solution.py:282
  1282.6 362.6 %reduce-scatter.14.cloned.1.call-done = f32[1024,128]{1,0:T(8,128)} async-done(((f32[32768,128]{1,0:T(8,128)}), f32[1024,128]{1,0:T(8,128)}) %reduce-scatter.14.cloned.1.call-update) | async-done | bytes 524304 | tf_op jit(solution)/shard_map/reduce_scatter | solution.py:283
  1647.1 248.9 %reduce-scatter.6.cloned.1.call-done = f32[1536,128]{1,0:T(8,128)} async-done(((f32[49152,128]{1,0:T(8,128)}), f32[1536,128]{1,0:T(8,128)}) %reduce-scatter.6.cloned.1.call-update) | async-done | bytes 786448 | tf_op jit(solution)/shard_map/reduce_scatter | solution.py:275
  (267 shorter events, 97.1 us)
Async XLA Ops:
  7.2 103.3 %all-gather.7.cloned.1.call-start = ((), (), s32[]{:S(2)}) async-start(), calls=%async_computation.9 | async-start | bytes 12976128 | tf_op jit(solution)/shard_map/all_gather | solution.py:159
  7.9 173.3 %all-gather.9.cloned.1.call-start = ((), (), s32[]{:S(2)}) async-start(), calls=%async_computation.10 | async-start | bytes 6488064 | tf_op jit(solution)/shard_map/all_gather | solution.py:160
  8.7 420.0 %all-gather.11.cloned.1.call-start = ((), (), s32[]{:S(2)}) async-start(), calls=%async_computation.11 | async-start | bytes 2162688 | tf_op jit(solution)/shard_map/all_gather | solution.py:161
  9.4 426.7 %all-gather.13.cloned.1.call-start = ((), (), s32[]{:S(2)}) async-start(), calls=%async_computation.12 | async-start | bytes 8650752 | tf_op jit(solution)/shard_map/all_gather | solution.py:162
  58.2 60.0 %copy-start.25 = (f32[2,256]{1,0:T(2,128)}, f32[2,256]{1,0:T(2,128)S(1)}, u32[]{:S(2)}) copy-start(f32[2,256]{1,0:T(2,128)S(1)} %broadcast_multiply_fusion.3) | copy-start | bytes 6148
  59.8 50.7 %copy-start.36 = (f32[2,256]{1,0:T(2,128)}, f32[2,256]{1,0:T(2,128)S(1)}, u32[]{:S(2)}) copy-start(f32[2,256]{1,0:T(2,128)S(1)} %fusion.52) | copy-start | bytes 6148
  59.8 58.3 %copy-start.32 = (f32[2,256]{1,0:T(2,128)}, f32[2,256]{1,0:T(2,128)S(1)}, u32[]{:S(2)}) copy-start(f32[2,256]{1,0:T(2,128)S(1)} %fusion.64) | copy-start | bytes 6148
  59.8 58.3 %copy-start.5 = (bf16[2,256,1024]{2,1,0:T(8,128)(2,1)S(1)}, bf16[2,256,1024]{2,1,0:T(8,128)(2,1)}, u32[]{:S(2)}) copy-start(bf16[2,256,1024]{2,1,0:T(8,128)(2,1)} %param.17) | copy-start | bytes 3145732
  118.7 62.6 %copy-start.21 = (bf16[2,256,1024]{2,1,0:T(8,128)(2,1)}, bf16[2,256,1024]{2,1,0:T(8,128)(2,1)S(1)}, u32[]{:S(2)}) copy-start(bf16[2,256,1024]{2,1,0:T(8,128)(2,1)S(1)} %fusion.50) | copy-start | bytes 3145732
  196.5 83.6 %all-to-all-start = ((bf16[2,256,3,4,256]{4,1,2,0,3:T(8,128)(2,1)}), bf16[2,256,3,4,256]{4,1,2,0,3:T(8,128)(2,1)S(1)}, u32[]{:S(2)}, u32[]{:S(2)}) async-start(bf16[2,256,3,4,256]{4,1,2,0,3:T(8,128)(2,1)} %copy.80), calls=%async_computation | async-start | bytes 6291456 | tf_op jit(solution)/shard_map/all_to_all | solution.py:192
  200.2 247.3 %all-gather.15.cloned.1.call-start = ((), (), s32[]{:S(2)}) async-start(), calls=%async_computation.13 | async-start | bytes 8650752 | tf_op jit(solution)/shard_map/all_gather | solution.py:163
  309.9 8.0 copy-start.46
  309.9 8.0 copy-start.47
  309.9 112.1 %copy-start.45 = (bf16[1024]{0:T(1024)(128)(2,1)S(1)}, bf16[1024]{0:T(1024)(128)(2,1)}, u32[]{:S(2)}) copy-start(bf16[1024]{0:T(1024)(128)(2,1)} %get-tuple-element.136) | copy-start | bytes 6148
  309.9 112.1 %copy-start.29 = (f32[2,1,1,1024]{3,1,0,2:T(1,128)S(1)}, f32[2,1,1,1024]{3,1,0,2:T(1,128)}, u32[]{:S(2)}) copy-start(f32[2,1,1,1024]{3,1,0,2:T(1,128)} %get-tuple-element.177) | copy-start | bytes 24580
  309.9 112.2 %copy-start.30 = (f32[2,1,1,1024]{3,1,0,2:T(1,128)S(1)}, f32[2,1,1,1024]{3,1,0,2:T(1,128)}, u32[]{:S(2)}) copy-start(f32[2,1,1,1024]{3,1,0,2:T(1,128)} %get-tuple-element.172) | copy-start | bytes 24580
  309.9 112.2 %copy-start.31 = (f32[2,1,1,1024]{3,1,0,2:T(1,128)S(1)}, f32[2,1,1,1024]{3,1,0,2:T(1,128)}, u32[]{:S(2)}) copy-start(f32[2,1,1,1024]{3,1,0,2:T(1,128)} %get-tuple-element.174) | copy-start | bytes 24580
  313.6 111.6 %all-to-all-start.1 = ((bf16[2,1024,1,256]{3,0,2,1:T(2,128)(2,1)}), bf16[2,1024,1,256]{3,0,2,1:T(2,128)(2,1)}, u32[]{:S(2)}, u32[]{:S(2)}) async-start(bf16[2,1024,1,256]{3,0,2,1:T(2,128)(2,1)} %copy.83), calls=%async_computation.1 | async-start | bytes 2097152 | tf_op jit(solution)/shard_map/all_to_all | solution.py:196
  422.0 46.0 %copy-start.43 = (f32[32,1,128]{2,1,0:T(1,128)}, f32[32,1,128]{2,1,0:T(1,128)S(1)}, u32[]{:S(2)}) copy-start(f32[32,1,128]{2,1,0:T(1,128)S(1)} %convert_element_type.139) | copy-start | bytes 49156
  428.7 3.3 copy-start.6
  431.9 2.7 copy-start.28
  447.6 14.4 copy-start.48
  462.0 4.6 copy-start.18
  462.0 4.6 copy-start.4
  489.8 2.4 copy-start.14
  494.0 4.1 copy-start.49
  494.0 6.4 copy-start.34
  505.4 40.0 %all-to-all-start.2 = ((bf16[2,256,4,256]{3,1,0,2:T(8,128)(2,1)}), bf16[2,256,4,256]{3,1,0,2:T(8,128)(2,1)}, u32[]{:S(2)}, u32[]{:S(2)}) async-start(bf16[2,256,4,256]{3,1,0,2:T(8,128)(2,1)} %copy.86), calls=%async_computation.2 | async-start | bytes 2097152 | tf_op jit(solution)/shard_map/all_to_all | solution.py:244
  509.7 442.1 %reduce-scatter.10.cloned.1.call-start = ((), (), s32[]{:S(2)}) async-start(), calls=%async_computation.16 | async-start | bytes 4325376 | tf_op jit(solution)/shard_map/reduce_scatter | solution.py:281
  519.5 433.9 %reduce-scatter.8.cloned.1.call-start = ((), (), s32[]{:S(2)}) async-start(), calls=%async_computation.15 | async-start | bytes 12976128 | tf_op jit(solution)/shard_map/reduce_scatter | solution.py:280
  547.7 1.7 copy-start.1
  549.6 4.6 copy-start.12
  565.7 7.6 slice-start
  565.7 8.9 slice-start.1
  565.7 11.3 copy-start
  591.6 3.2 copy-start.2
  594.9 1.7 copy-start.1
  596.8 4.6 copy-start.12
  612.9 7.6 slice-start
  612.9 8.9 slice-start.1
  612.9 11.3 copy-start
  638.8 3.2 copy-start.2
  725.9 1.7 copy-start.9
  730.0 14.2 copy-start.11
  758.1 522.6 %reduce-scatter.12.cloned.1.call-start = ((), (), s32[]{:S(2)}) async-start(), calls=%async_computation.17 | async-start | bytes 17301504 | tf_op jit(solution)/shard_map/reduce_scatter | solution.py:282
  788.7 856.5 %reduce-scatter.14.cloned.1.call-start = ((), (), s32[]{:S(2)}) async-start(), calls=%async_computation.18 | async-start | bytes 17301504 | tf_op jit(solution)/shard_map/reduce_scatter | solution.py:283
  824.2 6.6 copy-start.7
  824.3 6.6 copy-start.24
  824.3 6.6 copy-start.26
  824.3 1071.7 %reduce-scatter.6.cloned.1.call-start = ((), (), s32[]{:S(2)}) async-start(), calls=%async_computation.14 | async-start | bytes 25952256 | tf_op jit(solution)/shard_map/reduce_scatter | solution.py:275
  830.9 7.1 copy-start.37
  830.9 7.1 copy-start.33
  830.9 8.3 copy-start.13
  830.9 8.3 copy-start.15
  830.9 8.3 copy-start.17
  830.9 8.3 copy-start.35
  837.9 1.6 copy-start.8
  839.6 2.4 copy-start.41
  839.6 2.4 copy-start.40
  839.6 22.2 %copy-start.27 = (bf16[2,1024]{1,0:T(2,128)(2,1)S(1)}, bf16[2,1024]{1,0:T(2,128)(2,1)}, u32[]{:S(2)}) copy-start(bf16[2,1024]{1,0:T(2,128)(2,1)} %param.18) | copy-start | bytes 12292
  898.7 1.9 copy-start.10
  898.7 2.5 copy-start.38
  898.7 2.5 copy-start.39
  898.7 2.5 copy-start.42
  (7 other events, 8.1 us)
Sparse Core Ops, SparseCore 0:
  10.9 99.5 all-gather.6
  113.4 67.7 all-gather.8
  184.2 81.8 all-gather.10
  268.8 97.9 all-gather.12
  369.6 76.8 all-gather.14
  519.6 153.5 reduce-scatter.9
  758.2 155.5 reduce-scatter.7
  916.2 364.4 reduce-scatter.11
  1283.1 362.0 reduce-scatter.13
  1652.6 243.3 reduce-scatter.5
where the time goes:
time: 1910 us
  waiting for transfers between devices  1160 us (61%)
  blocking collectives  282 us (15%)
  matrix products  218 us (11%)
  local copies, waits for them, and re-layouts  168 us (9%)
  other arithmetic  50.4 us (3%)
    reduce_scatter x1, waiting for transfers between devices, shards(): lax.psum_scatter(flat_rows(grad_down), ('shard', 'seq'), scatter_dimensio...  363 us
    reduce_scatter x1, waiting for transfers between devices, shards(): lax.psum_scatter(flat_rows(grad_up), ('shard', 'seq'), scatter_dimension=...  325 us
    reduce_scatter x1, waiting for transfers between devices, shards(): lax.psum_scatter(flat_rows(grad_ada), ('shard', 'seq'), scatter_dimension...  249 us
    all_gather x1, blocking collectives, shards(): lax.all_gather(sharded[8], ('shard', 'seq'), axis=0, tiled=True)  104 us
    unnamed x2, blocking collectives  82.3 us
    reshape x5, local copies, waits for them, and re-layouts, flat_rows(): return matrix.reshape(-1, 128)  81.7 us
    all_to_all x1, waiting for transfers between devices, shards(): lax.all_to_all(projected, 'seq', split_axis=3, concat_axis=1, tiled=True)  79.3 us
    all_to_all x1, blocking collectives, shards(): lax.all_to_all(grad_packed, 'seq', split_axis=1, concat_axis=3, tiled=True)  75.9 us
  transfers between devices with their start and end apart: 13, of which 7 were waited for; matrix products, arithmetic and copies ran while one was open for 19% of the time, Pallas kernels for 0%

commit v1 on v0

v1 whole, which is shorter than its diff:
```python
from functools import partial

import jax
import jax.numpy as jnp
from jax import lax
from jax.sharding import PartitionSpec as P

HD = 64


EPS = 1e-06

AXES = ("shard", "seq")

bf16 = jnp.bfloat16
f32 = jnp.float32


def modulate(tokens, shift_by, scale_by):
    average = jnp.mean(tokens, axis=-1, keepdims=True)
    centered = tokens - average
    variance = jnp.mean(centered * centered, axis=-1, keepdims=True)
    return centered * lax.rsqrt(variance + EPS) * (1.0 + scale_by) + shift_by


def cross_rows(left, right):
    return lax.dot_general(left, right, (((0,), (0,)), ((), ())), preferred_element_type=f32)


def along_cols(left, right):
    return lax.dot_general(left, right, (((1,), (1,)), ((), ())), preferred_element_type=f32)


def plain(left, right):
    return jnp.dot(left, right, preferred_element_type=f32)


def attend_forward(queries, key_rows, value_rows):
    factor = HD ** (-0.5)
    count = queries.shape[0]
    queries = queries.reshape(count, -1, HD)
    key_rows = key_rows.reshape(key_rows.shape[0], -1, HD)
    value_rows = value_rows.reshape(value_rows.shape[0], -1, HD)
    scores = factor * jnp.einsum("qhd,khd->hqk", queries, key_rows, preferred_element_type=f32)
    highest = jnp.max(scores, axis=-1, keepdims=True)
    expon = jnp.exp(scores - highest)
    summed = jnp.sum(expon, axis=-1, keepdims=True)
    probs = (expon / summed).astype(bf16)
    mixed = jnp.einsum("hqk,khd->qhd", probs, value_rows, preferred_element_type=f32)
    return mixed.astype(bf16).reshape(count, -1), (highest + jnp.log(summed))[..., 0]


def attend_backward(queries, key_rows, value_rows, log_sums, grad_mixed):
    factor = HD ** (-0.5)
    count = queries.shape[0]
    length = key_rows.shape[0]
    queries = queries.reshape(count, -1, HD)
    grad_rows = grad_mixed.reshape(count, -1, HD)
    key_rows = key_rows.reshape(length, -1, HD)
    value_rows = value_rows.reshape(length, -1, HD)
    scores = factor * jnp.einsum("qhd,khd->hqk", queries, key_rows, preferred_element_type=f32)
    probs = jnp.exp(scores - log_sums[..., None])
    grad_probs = jnp.einsum("qhd,khd->hqk", grad_rows, value_rows, preferred_element_type=f32)
    inner = jnp.sum(probs * grad_probs, axis=-1, keepdims=True)
    grad_scores = (probs * (grad_probs - inner)).astype(bf16)
    grad_values = jnp.einsum("hqk,qhd->khd", probs.astype(bf16), grad_rows, preferred_element_type=f32)
    grad_queries = factor * jnp.einsum("hqk,khd->qhd", grad_scores, key_rows, preferred_element_type=f32)
    grad_keys = factor * jnp.einsum("hqk,qhd->khd", grad_scores, queries, preferred_element_type=f32)
    return (
        grad_queries.reshape(count, -1),
        grad_keys.reshape(length, -1),
        grad_values.reshape(length, -1),
    )


class Places:
    def __init__(self, latents):
        self.shards = lax.axis_size("shard")
        self.groups = lax.axis_size("seq")
        self.devices = self.shards * self.groups
        self.latents = latents
        assert 2 * latents == self.groups
        self.shard = lax.axis_index("shard")
        self.seq = lax.axis_index("seq")
        self.flat = self.shard * self.groups + self.seq
        self.core = self.shard % 2
        self.slot = self.seq % latents
        self.moves = []
        for turn in range(latents):
            move = []
            for source in range(self.devices):
                pair, core = divmod(source // self.groups, 2)
                half, place = divmod(source % self.groups, latents)
                member = (place + turn) % latents
                target = (2 * pair + half) * self.groups + core * latents + member
                move.append((source, target))
            self.moves.append(move)

    def to_pairs(self, blocks):
        parts = []
        for turn, move in enumerate(self.moves):
            member = (self.slot + turn) % self.latents
            block = lax.dynamic_index_in_dim(blocks, member, 0, keepdims=False)
            parts.append(lax.ppermute(block, AXES, move))
        return jnp.concatenate(parts, axis=0)

    def from_pairs(self, rows):
        tokens = rows.shape[0] // self.latents
        parts = []
        for turn, move in enumerate(self.moves):
            block = rows[turn * tokens : (turn + 1) * tokens]
            parts.append(lax.ppermute(block, AXES, [(b, a) for a, b in move]))
        twice = jnp.stack(parts + parts)
        start = (self.latents - self.slot) % self.latents
        return lax.dynamic_slice_in_dim(twice, start, self.latents, axis=0)

    def across(self, array, bit):
        swaps = [(s, s ^ (1 << bit)) for s in range(self.shards)]
        return lax.ppermute(array, "shard", swaps)

    def order(self, bits):
        order = [0]
        for bit in reversed(bits):
            order = order + [near ^ (1 << bit) for near in order]
        return order

    def arranged(self, matrix, bits):
        width = matrix.shape[1] // self.shards
        return jnp.concatenate(
            [
                lax.dynamic_slice_in_dim(matrix, (self.shard ^ near) * width, width, axis=1)
                for near in self.order(bits)
            ],
            axis=1,
        )

    def reduced(self, left, right, bits):
        columns = self.arranged(left, bits)
        width = columns.shape[1] // self.shards
        received = []

        def piece(low, high):
            total = cross_rows(columns[:, low * width : high * width], right)
            for part in received:
                total = total + part[low * width : high * width].astype(f32)
            return total

        for step, bit in enumerate(bits):
            low, high = self.shards >> (step + 1), self.shards >> step
            received.append(self.across(piece(low, high).astype(bf16), bit))
        own = piece(0, 1)
        rows = width // self.groups

        def block(away):
            begin = ((self.seq + away) % self.groups) * rows
            return lax.dynamic_slice_in_dim(own, begin, rows, axis=0)

        total = block(0)
        for away in range(1, self.groups):
            shift = [(q, (q + away) % self.groups) for q in range(self.groups)]
            total = total + lax.ppermute(block(away).astype(bf16), "seq", shift).astype(f32)
        return total


def shards(
    hidden_in,
    condition,
    out_grad,
    ada_weight,
    qkv_weight,
    proj_weight,
    up_weight,
    down_weight,
    ada_bias,
    qv_bias,
    proj_bias,
    up_bias,
    down_bias,
):
    latents, local_len, width = hidden_in.shape
    at = Places(latents)
    bits = list(range(at.shards.bit_length() - 1))
    bits_back = bits[:1] + bits[:0:-1]
    pairs = at.shards // 2
    total_latents = pairs * at.groups
    depth = ada_weight.shape[0]

    w_qkv = lax.all_gather(qkv_weight, AXES, axis=0, tiled=True)
    w_proj = lax.all_gather(proj_weight, AXES, axis=0, tiled=True)
    w_up = lax.all_gather(up_weight, AXES, axis=0, tiled=True)
    w_down = lax.all_gather(down_weight, AXES, axis=0, tiled=True)

    tokens = at.to_pairs(hidden_in).astype(f32)
    cotangent = at.to_pairs(out_grad).astype(f32)

    every_condition = lax.all_gather(condition, "shard", axis=0, tiled=True).astype(f32)
    silu_rows = lax.dynamic_slice_in_dim(every_condition, at.flat * depth, depth, axis=1)
    silu_rows = jax.nn.silu(silu_rows).astype(bf16)
    share = plain(silu_rows, ada_weight)
    wide = share.shape[1]
    share = share.reshape(pairs, at.groups, 2, wide // 2).transpose(0, 2, 1, 3)
    share = share.reshape(at.devices, wide // 2)
    biases = jnp.concatenate([ada_bias, qv_bias, proj_bias, up_bias, down_bias]).astype(f32)
    cuts = [ada_bias.shape[0], qv_bias.shape[0], proj_bias.shape[0], up_bias.shape[0], down_bias.shape[0]]
    sent = jnp.concatenate([share, jnp.broadcast_to(biases, (at.devices, biases.shape[0]))], axis=1)
    came = lax.all_to_all(sent, AXES, 0, 0, tiled=True)
    mine = jnp.sum(came[:, : wide // 2], axis=0)
    other = at.across(mine, 0)
    modulation = jnp.where(
        at.core == 0, jnp.concatenate([mine, other]), jnp.concatenate([other, mine])
    )
    whole = []
    begin = wide // 2
    for cut in cuts:
        whole.append(came[:, begin : begin + cut].reshape(-1))
        begin += cut
    b_ada, b_qv, b_proj, b_up, b_down = whole
    modulation = (modulation + b_ada).reshape(6, width)
    shift_a, scale_a, gate_a, shift_m, scale_m, gate_m = [modulation[member] for member in range(6)]

    normed = modulate(tokens, shift_a, scale_a).astype(bf16)
    kv_bias = jnp.concatenate([jnp.zeros((width,), f32), b_qv[width:]])
    kv_own = (plain(normed, w_qkv[:, width:]) + kv_bias).astype(bf16)
    kv_other = at.across(kv_own, 0)
    queries = (plain(normed, w_qkv[:, :width]) + b_qv[:width]).astype(bf16)
    kv_all = jnp.concatenate([kv_own, kv_other], axis=0)
    key_rows, value_rows = kv_all[:, :width], kv_all[:, width:]
    mixed, log_sums = attend_forward(queries, key_rows, value_rows)
    attn_out = plain(mixed, w_proj) + b_proj
    middle = tokens + gate_a * attn_out
    normed_two = modulate(middle, shift_m, scale_m).astype(bf16)
    pre_act = plain(normed_two, w_up) + b_up
    hidden = jax.nn.gelu(pre_act, approximate=True).astype(bf16)
    mlp_out = plain(hidden, w_down) + b_down
    block_out = at.from_pairs((middle + gate_m * mlp_out).astype(bf16))

    grad_gate_m = jnp.sum(cotangent * mlp_out, axis=0)
    grad_mlp = (gate_m * cotangent).astype(bf16)
    grad_bdown = jnp.sum(grad_mlp.astype(f32), axis=0)
    grad_hidden = along_cols(grad_mlp, w_down)
    _, gelu_back = jax.vjp(partial(jax.nn.gelu, approximate=True), pre_act)
    grad_pre = gelu_back(grad_hidden)[0].astype(bf16)
    grad_bup = jnp.sum(grad_pre.astype(f32), axis=0)
    down_share = at.reduced(hidden, grad_mlp, bits_back)
    up_share = at.reduced(normed_two, grad_pre, bits)
    grad_normed_two = along_cols(grad_pre, w_up)
    _, second_back = jax.vjp(modulate, middle, shift_m, scale_m)
    grad_middle, grad_shift_m, grad_scale_m = second_back(grad_normed_two)
    grad_middle = grad_middle + cotangent

    grad_gate_a = jnp.sum(grad_middle * attn_out, axis=0)
    grad_attn = (gate_a * grad_middle).astype(bf16)
    grad_bproj = jnp.sum(grad_attn.astype(f32), axis=0)
    grad_mixed = along_cols(grad_attn, w_proj).astype(bf16)
    proj_share = at.reduced(mixed, grad_attn, bits)
    grad_queries, grad_keys, grad_values = attend_backward(
        queries, key_rows, value_rows, log_sums, grad_mixed
    )
    count = tokens.shape[0]
    grad_kv = jnp.concatenate([grad_keys, grad_values], axis=1)
    kv_came = at.across(grad_kv[count:].astype(bf16), 0)
    grad_kv = (grad_kv[:count] + kv_came.astype(f32)).astype(bf16)
    grad_rows = jnp.concatenate([grad_queries.astype(bf16), grad_kv], axis=1)
    qkv_share = at.reduced(normed, grad_rows, bits)
    column_sums = jnp.sum(grad_rows.astype(f32), axis=0)
    grad_bqv = jnp.concatenate([column_sums[:width], column_sums[2 * width :]])
    grad_normed = along_cols(grad_rows, w_qkv)
    _, first_back = jax.vjp(modulate, tokens, shift_a, scale_a)
    grad_tokens, grad_shift_a, grad_scale_a = first_back(grad_normed)
    hidden_grad = at.from_pairs((grad_tokens + grad_middle).astype(bf16)).astype(f32)

    part_mod = jnp.concatenate(
        [grad_shift_a, grad_scale_a, grad_gate_a, grad_shift_m, grad_scale_m, grad_gate_m]
    )
    grad_mod = (part_mod + at.across(part_mod, 0)).astype(bf16)
    half_mod = lax.dynamic_slice_in_dim(grad_mod, at.core * (wide // 2), wide // 2).astype(f32)
    bias_parts = [
        part.reshape(at.devices, -1) for part in (grad_bqv, grad_bproj, grad_bup, grad_bdown)
    ]
    sent = jnp.concatenate(
        [jnp.broadcast_to(half_mod, (at.devices, wide // 2))] + bias_parts, axis=1
    )
    came = lax.all_to_all(sent, AXES, 0, 0, tiled=True)
    every_mod = came[:, : wide // 2].reshape(pairs, 2, at.groups, wide // 2)
    every_mod = every_mod.transpose(0, 2, 1, 3).reshape(total_latents, wide).astype(bf16)
    bias_sums = jnp.sum(came[:, wide // 2 :], axis=0)
    bias_shares = []
    begin = 0
    for part in bias_parts:
        bias_shares.append(bias_sums[begin : begin + part.shape[1]])
        begin += part.shape[1]
    ada_share = cross_rows(silu_rows, every_mod)
    own_bias = ada_bias.shape[0]
    adabias_share = jnp.sum(
        lax.dynamic_slice_in_dim(every_mod, at.flat * own_bias, own_bias, axis=1).astype(f32), axis=0
    )
    grad_silu = along_cols(every_mod, ada_weight).reshape(at.shards, 1, latents * depth)
    sent = jnp.broadcast_to(grad_silu, (at.shards, at.groups, latents * depth))
    came = lax.all_to_all(sent.reshape(at.devices, latents * depth), AXES, 0, 0, tiled=True)
    grad_silu = came.reshape(at.devices, latents, depth).transpose(1, 0, 2).reshape(latents, width)
    _, silu_back = jax.vjp(jax.nn.silu, condition.astype(f32))
    condition_grad = silu_back(grad_silu)[0]
    return (
        block_out,
        hidden_grad,
        condition_grad,
        ada_share,
        qkv_share,
        proj_share,
        up_share,
        down_share,
        adabias_share,
        bias_shares[0],
        bias_shares[1],
        bias_shares[2],
        bias_shares[3],
    )


def solution(mesh):
    in_specs = (
        P("shard", "seq", None),
        P("shard", None),
        P("shard", "seq", None),
        P(("shard", "seq"), None),
        P(("shard", "seq"), None),
        P(("shard", "seq"), None),
        P(("shard", "seq"), None),
        P(("shard", "seq"), None),
        P(("shard", "seq")),
        P(("shard", "seq")),
        P(("shard", "seq")),
        P(("shard", "seq")),
        P(("shard", "seq")),
    )
    out_specs = (
        P("shard", "seq", None),
        P("shard", "seq", None),
        P("shard", None),
        P(("shard", "seq"), None),
        P(("shard", "seq"), None),
        P(("shard", "seq"), None),
        P(("shard", "seq"), None),
        P(("shard", "seq"), None),
        P(("shard", "seq")),
        P(("shard", "seq")),
        P(("shard", "seq")),
        P(("shard", "seq")),
        P(("shard", "seq")),
    )
    return jax.shard_map(shards, mesh=mesh, in_specs=in_specs, out_specs=out_specs, check_vma=False)
```

time: 1910 us -> 736 us (0.39)
  waiting for transfers between devices: 1160 us -> 281 us
  blocking collectives: 282 us -> 11.9 us
  local copies, waits for them, and re-layouts: 168 us -> 52.7 us
  starting transfers between devices: 12.9 us -> 75.4 us
  other arithmetic: 50.4 us -> 83.7 us
    reduce_scatter x5 -> x0, waiting for transfers between devices: 937 us -> none  [the longest x1 363 us: shards(): lax.psum_scatter(flat_rows(grad_down), ('shard', 'seq'), scatter_dimensio...]
    reshape x16 -> x8, local copies, waits for them, and re-layouts: 108 us -> 3.58 us  [the longest x2 1.54 us: shards(): came.reshape(at.devices, latents, depth).transpose(1, 0, 2)]
    all_gather x1, blocking collectives: 104 us -> 11.9 us  [shards(): lax.all_gather(condition, 'shard', axis=0, tiled=True).astype(f32)]
    unnamed x2 -> x0, blocking collectives: 82.3 us -> none
    all_to_all x1 -> x0, blocking collectives: 75.9 us -> none  [shards(): lax.all_to_all(grad_packed, 'seq', split_axis=1, concat_axis=3, tiled=True)]
    ppermute x0 -> x36, waiting for transfers between devices: none -> 74.7 us  [the longest x16 36.4 us: across(): return lax.ppermute(array, 'shard', swaps)]
    ppermute x0 -> x36, starting transfers between devices: none -> 65.1 us  [the longest x12 30.2 us: reduced(): lax.ppermute(block(away).astype(bf16), 'seq', shift).astype(f32)]
    all_to_all x3, waiting for transfers between devices: 105 us -> 51.8 us  [the longest x2 51.8 us: shards(): came = lax.all_to_all(sent, AXES, 0, 0, tiled=True)]
  transfers between devices with their start and end apart: 13 -> 43, of which waited for: 7 -> 14; matrix products, arithmetic and copies ran while one was open for 19% -> 34% of each run, Pallas kernels for 0% -> 0%
where the time goes in v1:
time: 736 us; the launch traced here: 728 us
  waiting for transfers between devices  281 us (38%)
  matrix products  208 us (28%)
  other arithmetic  83.7 us (11%)
  starting transfers between devices  75.4 us (10%)
  local copies, waits for them, and re-layouts  52.7 us (7%)
  between operations  15.7 us (2%)
  blocking collectives  11.9 us (2%)
    all_gather x1, waiting for transfers between devices, shards(): w_down = lax.all_gather(down_weight, AXES, axis=0, tiled=True)  66.1 us
    all_gather x1, waiting for transfers between devices, shards(): w_up = lax.all_gather(up_weight, AXES, axis=0, tiled=True)  60.9 us
    dot_general x17, matrix products, cross_rows(): lax.dot_general(left, right, (((0,), (0,)), ((), ())), preferred_element_...  56.4 us
    all_to_all x2, waiting for transfers between devices, shards(): came = lax.all_to_all(sent, AXES, 0, 0, tiled=True)  51.8 us
    dot_general x6, matrix products, plain(): return jnp.dot(left, right, preferred_element_type=f32)  37.8 us
    ppermute x16, waiting for transfers between devices, across(): return lax.ppermute(array, 'shard', swaps)  36.4 us
    ppermute x12, waiting for transfers between devices, reduced(): lax.ppermute(block(away).astype(bf16), 'seq', shift).astype(f32)  35.7 us
    ppermute x12, starting transfers between devices, reduced(): lax.ppermute(block(away).astype(bf16), 'seq', shift).astype(f32)  30.2 us
  transfers between devices with their start and end apart: 43, of which 14 were waited for; matrix products, arithmetic and copies ran while one was open for 34% of the time, Pallas kernels for 0%

profile of v1, /device:TPU:0, one launch (start us, length us, event | category | flops | bytes accessed | tf_op | source)
XLA Modules:
  0.0 728.3 jit_solution(3764457456033537662)
XLA Ops:
  11.7 3.1 collective-permute-start.1
  14.8 11.9 %all-gather = bf16[8,2,1024]{2,1,0:T(2,128)(2,1)S(1)} all-gather(bf16[1,2,1024]{2,1,0:T(2,128)(2,1)S(1)} %bitcast.124), channel_id=1, replica_groups=mesh['shard'=8,'seq'=4] {'shard'}, dimensions={0}, use_global_device_ids=true | all-gather | bytes 36864 | tf_op jit(solution)/shard_map/all_gather | solution.py:196
  29.7 4.3 all-to-all-start
  34.7 27.6 %all-to-all-done = f32[32,1,3520]{2,1,0:T(1,128)S(1)} async-done(((f32[32,1,3520]{2,1,0:T(1,128)}), f32[32,1,3520]{2,1,0:T(1,128)S(1)}, u32[]{:S(2)}, u32[]{:S(2)}) %all-to-all-start) | async-done | bytes 450592 | tf_op jit(solution)/shard_map/all_to_all | solution.py:206
  62.3 2.2 collective-permute-start.2
  67.1 24.9 %all-gather.6.cloned.1.call-done = bf16[1024,3072]{1,0:T(8,128)(2,1)} async-done(((bf16[32,3072]{1,0:T(8,128)(2,1)}), bf16[1024,3072]{1,0:T(8,128)(2,1)}) %all-gather.6.cloned.1.call-update) | async-done | bytes 6291472 | tf_op jit(solution)/shard_map/all_gather | solution.py:188
  92.0 5.9 add_convert_fusion.2
  99.2 5.4 collective-permute-start.6
  108.6 2.8 add_convert_fusion.9
  112.2 4.3 pad_maximum_fusion.2
  116.6 2.9 copy.50
  119.4 4.6 copy.48
  124.0 13.2 %multiply_reduce_fusion.1 = (f32[16,512]{1,0:T(8,128)S(1)}, f32[16,512,1024]{2,1,0:T(8,128)}) fusion(bf16[512,16,64]{0,2,1:T(8,128)(2,1)S(1)} %bitcast.91, bf16[1024,16,64]{0,2,1:T(8,128)(2,1)S(1)} %bitcast.89), kind=kOutput, calls=%fused_computation.6 | convolution fusion | flops 1090510848 | bytes 36732928 | tf_op jit(solution)/shard_map/qhd,khd->hqk/dot_general | solution.py:44
  137.2 14.6 %fusion = f32[16,512]{1,0:T(8,128)S(1)} fusion(f32[16,512,1024]{2,1,0:T(8,128)} %get-tuple-element.92, f32[16,512]{1,0:T(8,128)S(1)} %get-tuple-element.91), kind=kLoop, calls=%fused_computation.5 | loop fusion | flops 25157632 | bytes 33619968 | tf_op jit(solution)/shard_map/reduce_sum | solution.py:47
  151.9 13.6 %fusion.47 = bf16[16,64,512]{2,1,0:T(8,128)(2,1)S(1)} fusion(bf16[1024,16,64]{0,2,1:T(8,128)(2,1)S(1)} %bitcast.93, f32[16,512,1024]{2,1,0:T(8,128)} %get-tuple-element.92, f32[16,512]{1,0:T(8,128)S(1)} %fusion, f32[16,512]{1,0:T(8,128)S(1)} %get-tuple-element.91), kind=kOutput, calls=%fused_computation.104 | convolution fusion | flops 1107820544 | bytes 36765696 | tf_op jit(solution)/shard_map/hqk,khd->qhd/dot_general | solution.py:49
  167.3 4.6 fusion.165
  174.9 60.9 %all-gather.10.cloned.1.call-done = bf16[1024,4096]{1,0:T(8,128)(2,1)} async-done(((bf16[32,4096]{1,0:T(8,128)(2,1)}), bf16[1024,4096]{1,0:T(8,128)(2,1)}) %all-gather.10.cloned.1.call-update) | async-done | bytes 8388624 | tf_op jit(solution)/shard_map/all_gather | solution.py:190
  235.7 12.7 %multiply_convert_fusion.1 = (bf16[512,4096]{1,0:T(8,128)(2,1)}, f32[512,4096]{1,0:T(8,128)}) fusion(f32[4096]{0:T(1024)} %slice_bitcast_fusion, bf16[512,1024]{1,0:T(8,128)(2,1)S(1)} %add_convert_fusion.8, bf16[1024,4096]{1,0:T(8,128)(2,1)} %all-gather.10.cloned.1.call-done), kind=kOutput, calls=%fused_computation.24 | convolution fusion | flops 4315938816 | bytes 22036480 | tf_op jit(solution)/shard_map/dot_general | solution.py:35
  248.4 66.1 %all-gather.12.cloned.1.call-done = bf16[4096,1024]{1,0:T(8,128)(2,1)} async-done(((bf16[128,1024]{1,0:T(8,128)(2,1)}), bf16[4096,1024]{1,0:T(8,128)(2,1)}) %all-gather.12.cloned.1.call-update) | async-done | bytes 8388624 | tf_op jit(solution)/shard_map/all_gather | solution.py:191
  314.6 14.3 %convert_reduce_fusion = (f32[4096]{0:T(1024)}, bf16[512,4096]{1,0:T(8,128)(2,1)S(1)}) fusion(f32[512,4096]{1,0:T(8,128)} %get-tuple-element.95, f32[4096]{0:T(1024)} %slice_bitcast_fusion, bf16[4096,1024]{1,0:T(8,128)(2,1)} %all-gather.12.cloned.1.call-done, f32[1024]{0:T(1024)} %get-tuple-element.81, bf16[256,1024]{1,0:T(8,128)(2,1)} %collective-permute-done.7, ...), kind=kOutput, calls=%fused_computation.23 | convolution fusion | flops 4346343424 | bytes 22056960 | tf_op jit(solution)/shard_map/dot_general | solution.py:31
  328.9 5.5 multiply_reduce_fusion.2
  335.1 2.2 copy-done.33
  338.0 11.5 %convert_reduce_fusion.3 = (f32[1024]{0:T(1024)S(1)}, f32[1024]{0:T(1024)}, f32[1024]{0:T(1024)S(1)}, f32[1024]{0:T(1024)S(1)}, bf16[512,1024]{1,0:T(8,128)(2,1)S(1)}, /*index=5*/bf16[512,1024]{1,0:T(8,128)(2,1)}) fusion(f32[1024]{0:T(1024)S(1)} %copy-done.85, bf16[256,1024]{1,0:T(8,128)(2,1)} %collective-permute-done.7, ...), kind=kOutput, calls=%fused_computation.88 | convolution fusion | flops 4307021824 | bytes 22054912 | tf_op jit(solution)/shard_map/dot_general | solution.py:35
  350.5 2.3 convolution_convert_fusion.3
  354.7 23.2 %multiply_reduce_fusion = (f32[16,512]{1,0:T(8,128)}, f32[16,512,1024]{2,1,0:T(8,128)}) fusion(f32[16,512,1024]{2,1,0:T(8,128)} %get-tuple-element.92, f32[16,512]{1,0:T(8,128)} %log_add_fusion, bf16[512,16,64]{0,2,1:T(8,128)(2,1)S(1)} %bitcast.95, bf16[1024,16,64]{0,2,1:T(8,128)(2,1)S(1)} %bitcast.94), kind=kOutput, calls=%fused_computation.1 | convolution fusion | flops 1107288064 | bytes 70320128 | tf_op jit(solution)/shard_map/qhd,khd->hqk/dot_general | solution.py:63
  377.9 15.5 %fusion.2 = f32[16,64,1024]{2,1,0:T(8,128)} fusion(bf16[512,16,64]{0,2,1:T(8,128)(2,1)S(1)} %bitcast.96, f32[16,512,1024]{2,1,0:T(8,128)} %get-tuple-element.92, f32[16,512]{1,0:T(8,128)} %log_add_fusion), kind=kOutput, calls=%fused_computation.8 | convolution fusion | flops 1098907648 | bytes 38830080 | tf_op jit(solution)/shard_map/hqk,qhd->khd/dot_general | solution.py:66
  394.7 5.8 convolution_convert_fusion.2
  400.8 3.1 fusion.118
  406.0 28.1 %multiply_convert_fusion = bf16[16,512,1024]{2,1,0:T(8,128)(2,1)} fusion(f32[16,512,1024]{2,1,0:T(8,128)} %get-tuple-element.98, f32[16,512,1024]{2,1,0:T(8,128)} %get-tuple-element.92, f32[16,512]{1,0:T(8,128)S(1)} %copy-done.53, f32[16,512]{1,0:T(8,128)S(1)} %copy-done.40), kind=kLoop, calls=%fused_computation | loop fusion | flops 41943040 | bytes 83951616 | tf_op jit(solution)/shard_map/convert_element_type | solution.py:65
  434.1 8.9 %convolution_multiply_fusion = f32[16,64,1024]{2,1,0:T(8,128)S(1)} fusion(bf16[512,16,64]{0,2,1:T(8,128)(2,1)S(1)} %bitcast.92, bf16[16,512,1024]{2,1,0:T(8,128)(2,1)} %multiply_convert_fusion), kind=kOutput, calls=%fused_computation.57 | convolution fusion | flops 1074790400 | bytes 22020096 | tf_op jit(solution)/shard_map/hqk,qhd->khd/dot_general | solution.py:68
  447.0 5.3 collective-permute-start.4
  453.9 11.0 %multiply_convert_fusion.2 = bf16[16,64,512]{2,1,0:T(8,128)(2,1)S(1)} fusion(bf16[1024,16,64]{0,2,1:T(8,128)(2,1)S(1)} %bitcast.90, bf16[16,512,1024]{2,1,0:T(8,128)(2,1)} %multiply_convert_fusion), kind=kOutput, calls=%fused_computation.93 | convolution fusion | flops 1074790400 | bytes 19922944 | tf_op jit(solution)/shard_map/hqk,khd->qhd/dot_general | solution.py:67
  464.8 2.3 add_convert_fusion.11
  468.7 3.4 fusion.86
  472.2 4.4 convolution_convert_fusion
  476.6 3.5 collective-permute-done.19
  485.5 3.4 fusion.54
  491.0 3.8 collective-permute-start.22
  494.8 3.0 fusion.16
  497.8 3.5 convolution_convert_fusion.1
  501.4 6.5 fusion.32
  518.5 3.1 add_convert_fusion.6
  523.2 4.6 add_convert_fusion
  530.5 3.3 all-to-all-start.1
  533.9 3.6 collective-permute-start.23
  539.5 5.7 add_convert_fusion.1
  548.4 3.3 fusion.130
  551.7 2.6 collective-permute-done.10
  556.4 24.3 %all-to-all-done.1 = f32[32,1,3328]{2,1,0:T(1,128)} async-done(((f32[32,1,3328]{2,1,0:T(1,128)}), f32[32,1,3328]{2,1,0:T(1,128)}, u32[]{:S(2)}, u32[]{:S(2)}) %all-to-all-start.1) | async-done | bytes 426016 | tf_op jit(solution)/shard_map/all_to_all | solution.py:283
  587.6 2.5 all-to-all-start.2
  590.2 3.8 add_convert_fusion.3
  598.4 3.8 add_convert_fusion.4
  610.4 3.9 add_convert_fusion.5
  616.6 14.9 %collective-permute-done.13 = bf16[256,3072]{1,0:T(8,128)(2,1)} collective-permute-done((bf16[256,3072]{1,0:T(8,128)(2,1)}, bf16[256,3072]{1,0:T(8,128)(2,1)}, u32[]{:S(2)}, u32[]{:S(2)}) %collective-permute-start.13) | collective-permute-done | bytes 1572896 | tf_op jit(solution)/shard_map/ppermute | solution.py:119
  631.6 2.6 add_convert_fusion.10
  635.9 17.3 %collective-permute-done.32 = bf16[512,1024]{1,0:T(8,128)(2,1)} collective-permute-done((bf16[512,1024]{1,0:T(8,128)(2,1)}, bf16[512,1024]{1,0:T(8,128)(2,1)}, u32[]{:S(2)}, u32[]{:S(2)}) %collective-permute-start.32) | collective-permute-done | bytes 1048608 | tf_op jit(solution)/shard_map/ppermute | solution.py:119
  653.2 2.8 convert_add_fusion.2
  657.9 2.5 collective-permute-start.34
  668.4 10.2 %collective-permute-done.27 = bf16[32,4096]{1,0:T(8,128)(2,1)S(1)} collective-permute-done((bf16[32,4096]{1,0:T(8,128)(2,1)S(1)}, bf16[32,4096]{1,0:T(8,128)(2,1)S(1)}, u32[]{:S(2)}, u32[]{:S(2)}) %collective-permute-start.27) | collective-permute-done | bytes 262176 | tf_op jit(solution)/shard_map/ppermute | solution.py:161
  678.6 15.3 %collective-permute-done.28 = bf16[32,4096]{1,0:T(8,128)(2,1)S(1)} collective-permute-done((bf16[32,4096]{1,0:T(8,128)(2,1)S(1)}, bf16[32,4096]{1,0:T(8,128)(2,1)S(1)}, u32[]{:S(2)}, u32[]{:S(2)}) %collective-permute-start.28) | collective-permute-done | bytes 262176 | tf_op jit(solution)/shard_map/ppermute | solution.py:161
  693.9 11.1 %collective-permute-start.15 = (bf16[32,3072]{1,0:T(8,128)(2,1)S(1)}, bf16[32,3072]{1,0:T(8,128)(2,1)S(1)}, u32[]{:S(2)}, u32[]{:S(2)}) collective-permute-start(bf16[32,3072]{1,0:T(8,128)(2,1)S(1)} %get-tuple-element.45), channel_id=1, source_target_pairs={{0,1},{1,2},{2,3},{3,0},{4,5},{5,6},{6,7},{7,4},{8,9},{9,10},{10,1... | collective-permute-start | bytes 589832 | tf_op jit(solution)/shard_map/ppermute | solution.py:161
  705.0 3.4 collective-permute-start.16
  710.2 3.5 collective-permute-done.15
  713.7 6.7 collective-permute-done.16
  (370 shorter events, 101.9 us)
Async XLA Ops:
  7.2 20.2 %copy-start = (bf16[32,6144]{1,0:T(8,128)(2,1)S(1)}, bf16[32,6144]{1,0:T(8,128)(2,1)}, u32[]{:S(2)}) copy-start(bf16[32,6144]{1,0:T(8,128)(2,1)} %param.16) | copy-start | bytes 1179652
  7.2 84.8 %all-gather.6.cloned.1.call-start = ((), (), s32[]{:S(2)}) async-start(), calls=%async_computation.3 | async-start | bytes 6488064 | tf_op jit(solution)/shard_map/all_gather | solution.py:188
  7.9 159.4 %all-gather.8.cloned.1.call-start = ((), (), s32[]{:S(2)}) async-start(), calls=%async_computation.4 | async-start | bytes 2162688 | tf_op jit(solution)/shard_map/all_gather | solution.py:189
  8.7 227.1 %all-gather.10.cloned.1.call-start = ((), (), s32[]{:S(2)}) async-start(), calls=%async_computation.5 | async-start | bytes 8650752 | tf_op jit(solution)/shard_map/all_gather | solution.py:190
  9.4 305.1 %all-gather.12.cloned.1.call-start = ((), (), s32[]{:S(2)}) async-start(), calls=%async_computation.6 | async-start | bytes 8650752 | tf_op jit(solution)/shard_map/all_gather | solution.py:191
  10.8 17.5 %copy-start.94 = (bf16[192]{0:T(256)(128)(2,1)S(1)}, bf16[192]{0:T(256)(128)(2,1)}, u32[]{:S(2)}) copy-start(bf16[192]{0:T(256)(128)(2,1)} %param.21) | copy-start | bytes 1156
  10.8 17.5 %copy-start.95 = (bf16[64]{0:T(256)(128)(2,1)S(1)}, bf16[64]{0:T(256)(128)(2,1)}, u32[]{:S(2)}) copy-start(bf16[64]{0:T(256)(128)(2,1)} %param.22) | copy-start | bytes 388
  10.8 17.5 %copy-start.96 = (bf16[32]{0:T(256)(128)(2,1)S(1)}, bf16[32]{0:T(256)(128)(2,1)}, u32[]{:S(2)}) copy-start(bf16[32]{0:T(256)(128)(2,1)} %param.23) | copy-start | bytes 196
  10.8 17.5 %copy-start.97 = (bf16[128]{0:T(256)(128)(2,1)S(1)}, bf16[128]{0:T(256)(128)(2,1)}, u32[]{:S(2)}) copy-start(bf16[128]{0:T(256)(128)(2,1)} %param.24) | copy-start | bytes 772
  10.8 17.5 %copy-start.98 = (bf16[32]{0:T(256)(128)(2,1)S(1)}, bf16[32]{0:T(256)(128)(2,1)}, u32[]{:S(2)}) copy-start(bf16[32]{0:T(256)(128)(2,1)} %param.25) | copy-start | bytes 196
  10.9 23.1 %collective-permute-start = (bf16[256,1024]{1,0:T(8,128)(2,1)S(1)}, bf16[256,1024]{1,0:T(8,128)(2,1)S(1)}, u32[]{:S(2)}, u32[]{:S(2)}) collective-permute-start(bf16[256,1024]{1,0:T(8,128)(2,1)S(1)} %get-tuple-element.72), channel_id=1, source_target_pairs={{0,0},{1,1},{2,4},{3,5},{4,2},{5,3},{6,6},{7,7},{8,8},{9,9},{10,12... | collective-permute-start | bytes 1572872 | tf_op jit(solution)/shard_map/ppermute | solution.py:104
  11.7 22.3 %collective-permute-start.1 = (bf16[256,1024]{1,0:T(8,128)(2,1)S(1)}, bf16[256,1024]{1,0:T(8,128)(2,1)S(1)}, u32[]{:S(2)}, u32[]{:S(2)}) collective-permute-start(bf16[256,1024]{1,0:T(8,128)(2,1)S(1)} %get-tuple-element.73), channel_id=1, source_target_pairs={{0,1},{1,0},{2,5},{3,4},{4,3},{5,2},{6,7},{7,6},{8,9},{9,8},{10,13... | collective-permute-start | bytes 1572872 | tf_op jit(solution)/shard_map/ppermute | solution.py:104
  29.7 32.5 %all-to-all-start = ((f32[32,1,3520]{2,1,0:T(1,128)}), f32[32,1,3520]{2,1,0:T(1,128)S(1)}, u32[]{:S(2)}, u32[]{:S(2)}) async-start(f32[32,1,3520]{2,1,0:T(1,128)} %copy.47), calls=%async_computation | async-start | bytes 917504 | tf_op jit(solution)/shard_map/all_to_all | solution.py:206
  34.0 33.0 %copy-start.13 = (bf16[256,1024]{1,0:T(8,128)(2,1)}, bf16[256,1024]{1,0:T(8,128)(2,1)S(1)}, u32[]{:S(2)}) copy-start(bf16[256,1024]{1,0:T(8,128)(2,1)S(1)} %collective-permute-done) | copy-start | bytes 1572868
  34.0 33.0 %copy-start.16 = (bf16[256,1024]{1,0:T(8,128)(2,1)}, bf16[256,1024]{1,0:T(8,128)(2,1)S(1)}, u32[]{:S(2)}) copy-start(bf16[256,1024]{1,0:T(8,128)(2,1)S(1)} %collective-permute-done.1) | copy-start | bytes 1572868
  34.2 32.8 %copy-start.71 = (f32[512]{0:T(512)}, f32[512]{0:T(512)S(1)}, u32[]{:S(2)}) copy-start(f32[512]{0:T(512)S(1)} %broadcast_multiply_fusion.1) | copy-start | bytes 6148
  34.7 27.7 %copy-start.76 = (f32[512]{0:T(512)}, f32[512]{0:T(512)S(1)}, u32[]{:S(2)}) copy-start(f32[512]{0:T(512)S(1)} %fusion.31) | copy-start | bytes 6148
  34.7 63.2 %copy-start.73 = (f32[512]{0:T(512)}, f32[512]{0:T(512)S(1)}, u32[]{:S(2)}) copy-start(f32[512]{0:T(512)S(1)} %fusion.148) | copy-start | bytes 6148
  62.3 3.0 collective-permute-start.2
  66.0 101.3 %copy-start.88 = (f32[1024]{0:T(1024)}, f32[1024]{0:T(1024)S(1)}, u32[]{:S(2)}) copy-start(f32[1024]{0:T(1024)S(1)} %get-tuple-element.86) | copy-start | bytes 12292
  67.1 41.6 %copy-start.32 = (bf16[512,1024]{1,0:T(8,128)(2,1)}, bf16[512,1024]{1,0:T(8,128)(2,1)S(1)}, u32[]{:S(2)}) copy-start(bf16[512,1024]{1,0:T(8,128)(2,1)S(1)} %fusion.29) | copy-start | bytes 3145732
  97.9 14.3 %collective-permute-start.3 = (bf16[512,2048]{1,0:T(8,128)(2,1)}, bf16[512,2048]{1,0:T(8,128)(2,1)}, u32[]{:S(2)}, u32[]{:S(2)}) collective-permute-start(bf16[512,2048]{1,0:T(8,128)(2,1)} %add_convert_fusion.2), channel_id=1, source_target_pairs={{0,4},{4,0},{8,12},{12,8},{16,20},{20,16},{24,28},{28,24},{1,5},{5... | collective-permute-start | bytes 6291464 | tf_op jit(solution)/shard_map/ppermute | solution.py:119
  99.2 149.2 %collective-permute-start.6 = (bf16[256,1024]{1,0:T(8,128)(2,1)}, bf16[256,1024]{1,0:T(8,128)(2,1)}, u32[]{:S(2)}, u32[]{:S(2)}) collective-permute-start(bf16[256,1024]{1,0:T(8,128)(2,1)} %get-tuple-element.68), channel_id=1, source_target_pairs={{0,0},{1,1},{2,4},{3,5},{4,2},{5,3},{6,6},{7,7},{8,8},{9,9},{10,12... | collective-permute-start | bytes 1572872 | tf_op jit(solution)/shard_map/ppermute | solution.py:104
  104.6 143.8 %collective-permute-start.7 = (bf16[256,1024]{1,0:T(8,128)(2,1)}, bf16[256,1024]{1,0:T(8,128)(2,1)}, u32[]{:S(2)}, u32[]{:S(2)}) collective-permute-start(bf16[256,1024]{1,0:T(8,128)(2,1)} %get-tuple-element.69), channel_id=1, source_target_pairs={{0,1},{1,0},{2,5},{3,4},{4,3},{5,2},{6,7},{7,6},{8,9},{9,8},{10,13... | collective-permute-start | bytes 1572872 | tf_op jit(solution)/shard_map/ppermute | solution.py:104
  106.3 61.0 %copy-start.90 = (f32[1024]{0:T(1024)}, f32[1024]{0:T(1024)S(1)}, u32[]{:S(2)}) copy-start(f32[1024]{0:T(1024)S(1)} %add.460) | copy-start | bytes 12292
  151.8 15.5 %copy-start.14 = (bf16[256,1024]{1,0:T(8,128)(2,1)S(1)}, bf16[256,1024]{1,0:T(8,128)(2,1)}, u32[]{:S(2)}) copy-start(bf16[256,1024]{1,0:T(8,128)(2,1)} %copy-done.13) | copy-start | bytes 1572868
  151.9 15.5 %copy-start.17 = (bf16[256,1024]{1,0:T(8,128)(2,1)S(1)}, bf16[256,1024]{1,0:T(8,128)(2,1)}, u32[]{:S(2)}) copy-start(bf16[256,1024]{1,0:T(8,128)(2,1)} %copy-done.16) | copy-start | bytes 1572868
  173.1 75.4 %copy-start.25 = (bf16[512,1024]{1,0:T(8,128)(2,1)}, bf16[512,1024]{1,0:T(8,128)(2,1)S(1)}, u32[]{:S(2)}) copy-start(bf16[512,1024]{1,0:T(8,128)(2,1)S(1)} %add_convert_fusion.8) | copy-start | bytes 3145732
  377.9 15.5 %copy-start.34 = (bf16[512,4096]{1,0:T(8,128)(2,1)S(1)}, bf16[512,4096]{1,0:T(8,128)(2,1)}, u32[]{:S(2)}) copy-start(bf16[512,4096]{1,0:T(8,128)(2,1)} %get-tuple-element.94) | copy-start | bytes 12582916
  400.5 122.2 %collective-permute-start.30 = (bf16[2048,1024]{1,0:T(8,128)(2,1)}, bf16[2048,1024]{1,0:T(8,128)(2,1)}, u32[]{:S(2)}, u32[]{:S(2)}) collective-permute-start(bf16[2048,1024]{1,0:T(8,128)(2,1)} %convolution_convert_fusion.2), channel_id=1, source_target_pairs={{0,4},{4,0},{8,12},{12,8},{16,20},{20,16},{24,28},{28,24},{1,5},{5... | collective-permute-start | bytes 12582920 | tf_op jit(solution)/shard_map/ppermute | solution.py:119
  405.7 59.2 %collective-permute-start.18 = (bf16[512,1024]{1,0:T(8,128)(2,1)}, bf16[512,1024]{1,0:T(8,128)(2,1)}, u32[]{:S(2)}, u32[]{:S(2)}) collective-permute-start(bf16[512,1024]{1,0:T(8,128)(2,1)} %convolution_convert_fusion.4), channel_id=1, source_target_pairs={{0,4},{4,0},{8,12},{12,8},{16,20},{20,16},{24,28},{28,24},{1,5},{5... | collective-permute-start | bytes 3145736 | tf_op jit(solution)/shard_map/ppermute | solution.py:119
  406.0 28.1 %copy-start.10 = (bf16[512,1024]{0,1:T(8,128)(2,1)S(1)}, bf16[512,1024]{0,1:T(8,128)(2,1)}, u32[]{:S(2)}) copy-start(bf16[512,1024]{0,1:T(8,128)(2,1)} %copy-done.9) | copy-start | bytes 3145732
  445.7 49.0 %collective-permute-start.8 = (bf16[512,2048]{0,1:T(8,128)(2,1)}, bf16[512,2048]{0,1:T(8,128)(2,1)}, u32[]{:S(2)}, u32[]{:S(2)}) collective-permute-start(bf16[512,2048]{0,1:T(8,128)(2,1)} %fusion.17), channel_id=1, source_target_pairs={{0,4},{4,0},{8,12},{12,8},{16,20},{20,16},{24,28},{28,24},{1,5},{5... | collective-permute-start | bytes 6291464 | tf_op jit(solution)/shard_map/ppermute | solution.py:119
  447.0 38.5 %collective-permute-start.4 = (bf16[256,1024]{1,0:T(8,128)(2,1)}, bf16[256,1024]{1,0:T(8,128)(2,1)}, u32[]{:S(2)}, u32[]{:S(2)}) collective-permute-start(bf16[256,1024]{1,0:T(8,128)(2,1)} %get-tuple-element.71), channel_id=1, source_target_pairs={{0,0},{1,1},{4,2},{5,3},{2,4},{3,5},{6,6},{7,7},{8,8},{9,9},{12,10... | collective-permute-start | bytes 1572872 | tf_op jit(solution)/shard_map/ppermute | solution.py:112
  452.4 33.2 %collective-permute-start.5 = (bf16[256,1024]{1,0:T(8,128)(2,1)}, bf16[256,1024]{1,0:T(8,128)(2,1)}, u32[]{:S(2)}, u32[]{:S(2)}) collective-permute-start(bf16[256,1024]{1,0:T(8,128)(2,1)} %get-tuple-element.70), channel_id=1, source_target_pairs={{1,0},{0,1},{5,2},{4,3},{3,4},{2,5},{7,6},{6,7},{9,8},{8,9},{13,10... | collective-permute-start | bytes 1572872 | tf_op jit(solution)/shard_map/ppermute | solution.py:112
  464.8 36.5 %copy-start.26 = (bf16[16,64,512]{2,1,0:T(8,128)(2,1)}, bf16[16,64,512]{2,1,0:T(8,128)(2,1)S(1)}, u32[]{:S(2)}) copy-start(bf16[16,64,512]{2,1,0:T(8,128)(2,1)S(1)} %multiply_convert_fusion.2) | copy-start | bytes 3145732
  467.2 12.9 %collective-permute-start.19 = (bf16[256,1024]{1,0:T(8,128)(2,1)S(1)}, bf16[256,1024]{1,0:T(8,128)(2,1)S(1)}, u32[]{:S(2)}, u32[]{:S(2)}) collective-permute-start(bf16[256,1024]{1,0:T(8,128)(2,1)S(1)} %add_convert_fusion.11), channel_id=1, source_target_pairs={{0,8},{4,12},{8,0},{12,4},{16,24},{20,28},{24,16},{28,20},{1,9},{5... | collective-permute-start | bytes 1572872 | tf_op jit(solution)/shard_map/ppermute | solution.py:119
  481.4 7.5 %collective-permute-start.20 = (bf16[128,1024]{1,0:T(8,128)(2,1)S(1)}, bf16[128,1024]{1,0:T(8,128)(2,1)S(1)}, u32[]{:S(2)}, u32[]{:S(2)}) collective-permute-start(bf16[128,1024]{1,0:T(8,128)(2,1)S(1)} %add_convert_fusion.12), channel_id=1, source_target_pairs={{0,16},{4,20},{8,24},{12,28},{16,0},{20,4},{24,8},{28,12},{1,17},{... | collective-permute-start | bytes 786440 | tf_op jit(solution)/shard_map/ppermute | solution.py:119
  485.5 53.9 %collective-permute-start.24 = (bf16[512,4096]{1,0:T(8,128)(2,1)}, bf16[512,4096]{1,0:T(8,128)(2,1)}, u32[]{:S(2)}, u32[]{:S(2)}) collective-permute-start(bf16[512,4096]{1,0:T(8,128)(2,1)} %convolution_convert_fusion), channel_id=1, source_target_pairs={{0,4},{4,0},{8,12},{12,8},{16,20},{20,16},{24,28},{28,24},{1,5},{5... | collective-permute-start | bytes 12582920 | tf_op jit(solution)/shard_map/ppermute | solution.py:119
  490.8 43.1 %collective-permute-start.21 = (bf16[32,1024]{1,0:T(8,128)(2,1)}, bf16[32,1024]{1,0:T(8,128)(2,1)}, u32[]{:S(2)}, u32[]{:S(2)}) collective-permute-start(bf16[32,1024]{1,0:T(8,128)(2,1)} %get-tuple-element.74), channel_id=1, source_target_pairs={{0,1},{1,2},{2,3},{3,0},{4,5},{5,6},{6,7},{7,4},{8,9},{9,10},{10,1... | collective-permute-start | bytes 196616 | tf_op jit(solution)/shard_map/ppermute | solution.py:161
  491.0 46.5 %collective-permute-start.22 = (bf16[32,1024]{1,0:T(8,128)(2,1)}, bf16[32,1024]{1,0:T(8,128)(2,1)}, u32[]{:S(2)}, u32[]{:S(2)}) collective-permute-start(bf16[32,1024]{1,0:T(8,128)(2,1)} %get-tuple-element.76), channel_id=1, source_target_pairs={{0,2},{1,3},{2,0},{3,1},{4,6},{5,7},{6,4},{7,5},{8,10},{9,11},{10,... | collective-permute-start | bytes 196616 | tf_op jit(solution)/shard_map/ppermute | solution.py:161
  501.3 88.8 %collective-permute-start.12 = (bf16[512,3072]{1,0:T(8,128)(2,1)}, bf16[512,3072]{1,0:T(8,128)(2,1)}, u32[]{:S(2)}, u32[]{:S(2)}) collective-permute-start(bf16[512,3072]{1,0:T(8,128)(2,1)} %convolution_convert_fusion.1), channel_id=1, source_target_pairs={{0,4},{4,0},{8,12},{12,8},{16,20},{20,16},{24,28},{28,24},{1,5},{5... | collective-permute-start | bytes 9437192 | tf_op jit(solution)/shard_map/ppermute | solution.py:119
  522.7 5.1 collective-permute-start.11
  527.8 70.6 %collective-permute-start.31 = (bf16[1024,1024]{1,0:T(8,128)(2,1)}, bf16[1024,1024]{1,0:T(8,128)(2,1)}, u32[]{:S(2)}, u32[]{:S(2)}) collective-permute-start(bf16[1024,1024]{1,0:T(8,128)(2,1)} %add_convert_fusion), channel_id=1, source_target_pairs={{0,16},{4,20},{8,24},{12,28},{16,0},{20,4},{24,8},{28,12},{1,17},{... | collective-permute-start | bytes 6291464 | tf_op jit(solution)/shard_map/ppermute | solution.py:119
  530.5 50.2 %all-to-all-start.1 = ((f32[32,1,3328]{2,1,0:T(1,128)}), f32[32,1,3328]{2,1,0:T(1,128)}, u32[]{:S(2)}, u32[]{:S(2)}) async-start(f32[32,1,3328]{2,1,0:T(1,128)} %all_to_all.25), calls=%async_computation.1 | async-start | bytes 851968 | tf_op jit(solution)/shard_map/all_to_all | solution.py:283
  533.9 11.4 %collective-permute-start.23 = (bf16[32,1024]{1,0:T(8,128)(2,1)}, bf16[32,1024]{1,0:T(8,128)(2,1)S(1)}, u32[]{:S(2)}, u32[]{:S(2)}) collective-permute-start(bf16[32,1024]{1,0:T(8,128)(2,1)} %get-tuple-element.75), channel_id=1, source_target_pairs={{0,3},{1,0},{2,1},{3,2},{4,7},{5,4},{6,5},{7,6},{8,11},{9,8},{10,9... | collective-permute-start | bytes 196616 | tf_op jit(solution)/shard_map/ppermute | solution.py:161
  537.5 14.3 %collective-permute-start.9 = (bf16[256,1024]{1,0:T(8,128)(2,1)}, bf16[256,1024]{1,0:T(8,128)(2,1)S(1)}, u32[]{:S(2)}, u32[]{:S(2)}) collective-permute-start(bf16[256,1024]{1,0:T(8,128)(2,1)} %get-tuple-element.67), channel_id=1, source_target_pairs={{0,0},{1,1},{4,2},{5,3},{2,4},{3,5},{6,6},{7,7},{8,8},{9,9},{12,10... | collective-permute-start | bytes 1572872 | tf_op jit(solution)/shard_map/ppermute | solution.py:112
  539.4 14.9 %collective-permute-start.10 = (bf16[256,1024]{1,0:T(8,128)(2,1)}, bf16[256,1024]{1,0:T(8,128)(2,1)S(1)}, u32[]{:S(2)}, u32[]{:S(2)}) collective-permute-start(bf16[256,1024]{1,0:T(8,128)(2,1)} %get-tuple-element.66), channel_id=1, source_target_pairs={{1,0},{0,1},{5,2},{4,3},{3,4},{2,5},{7,6},{6,7},{9,8},{8,9},{13,10... | collective-permute-start | bytes 1572872 | tf_op jit(solution)/shard_map/ppermute | solution.py:112
  545.2 65.1 %collective-permute-start.25 = (bf16[256,4096]{1,0:T(8,128)(2,1)}, bf16[256,4096]{1,0:T(8,128)(2,1)}, u32[]{:S(2)}, u32[]{:S(2)}) collective-permute-start(bf16[256,4096]{1,0:T(8,128)(2,1)} %add_convert_fusion.1), channel_id=1, source_target_pairs={{0,8},{4,12},{8,0},{12,4},{16,24},{20,28},{24,16},{28,20},{1,9},{5... | collective-permute-start | bytes 6291464 | tf_op jit(solution)/shard_map/ppermute | solution.py:119
  587.6 17.3 %all-to-all-start.2 = ((f32[32,1,64]{2,1,0:T(1,128)}), f32[32,1,64]{2,1,0:T(1,128)S(1)}, u32[]{:S(2)}, u32[]{:S(2)}) async-start(f32[32,1,64]{2,1,0:T(1,128)} %bitcast.26), calls=%async_computation.2 | async-start | bytes 32768 | tf_op jit(solution)/shard_map/all_to_all | solution.py:299
  594.0 37.6 %collective-permute-start.13 = (bf16[256,3072]{1,0:T(8,128)(2,1)}, bf16[256,3072]{1,0:T(8,128)(2,1)}, u32[]{:S(2)}, u32[]{:S(2)}) collective-permute-start(bf16[256,3072]{1,0:T(8,128)(2,1)} %add_convert_fusion.3), channel_id=1, source_target_pairs={{0,8},{4,12},{8,0},{12,4},{16,24},{20,28},{24,16},{28,20},{1,9},{5... | collective-permute-start | bytes 4718600 | tf_op jit(solution)/shard_map/ppermute | solution.py:119
  602.2 51.0 %collective-permute-start.32 = (bf16[512,1024]{1,0:T(8,128)(2,1)}, bf16[512,1024]{1,0:T(8,128)(2,1)}, u32[]{:S(2)}, u32[]{:S(2)}) collective-permute-start(bf16[512,1024]{1,0:T(8,128)(2,1)} %add_convert_fusion.4), channel_id=1, source_target_pairs={{0,8},{4,12},{8,0},{12,4},{16,24},{20,28},{24,16},{28,20},{1,9},{5... | collective-permute-start | bytes 3145736 | tf_op jit(solution)/shard_map/ppermute | solution.py:119
  614.3 46.1 %collective-permute-start.26 = (bf16[128,4096]{1,0:T(8,128)(2,1)S(1)}, bf16[128,4096]{1,0:T(8,128)(2,1)S(1)}, u32[]{:S(2)}, u32[]{:S(2)}) collective-permute-start(bf16[128,4096]{1,0:T(8,128)(2,1)S(1)} %add_convert_fusion.5), channel_id=1, source_target_pairs={{0,16},{4,20},{8,24},{12,28},{16,0},{20,4},{24,8},{28,12},{1,17},{... | collective-permute-start | bytes 3145736 | tf_op jit(solution)/shard_map/ppermute | solution.py:119
  616.6 36.6 %copy-start.35 = (f32[512,1024]{1,0:T(8,128)S(1)}, f32[512,1024]{1,0:T(8,128)}, u32[]{:S(2)}) copy-start(f32[512,1024]{1,0:T(8,128)} %fusion.86) | copy-start | bytes 6291460
  634.2 30.5 %collective-permute-start.14 = (bf16[128,3072]{1,0:T(8,128)(2,1)S(1)}, bf16[128,3072]{1,0:T(8,128)(2,1)S(1)}, u32[]{:S(2)}, u32[]{:S(2)}) collective-permute-start(bf16[128,3072]{1,0:T(8,128)(2,1)S(1)} %add_convert_fusion.10), channel_id=1, source_target_pairs={{0,16},{4,20},{8,24},{12,28},{16,0},{20,4},{24,8},{28,12},{1,17},{... | collective-permute-start | bytes 2359304 | tf_op jit(solution)/shard_map/ppermute | solution.py:119
  656.1 53.1 %collective-permute-start.33 = (bf16[128,1024]{1,0:T(8,128)(2,1)S(1)}, bf16[128,1024]{1,0:T(8,128)(2,1)S(1)}, u32[]{:S(2)}, u32[]{:S(2)}) collective-permute-start(bf16[128,1024]{1,0:T(8,128)(2,1)S(1)} %get-tuple-element.39), channel_id=1, source_target_pairs={{0,1},{1,2},{2,3},{3,0},{4,5},{5,6},{6,7},{7,4},{8,9},{9,10},{10,1... | collective-permute-start | bytes 786440 | tf_op jit(solution)/shard_map/ppermute | solution.py:161
  657.9 51.3 %collective-permute-start.34 = (bf16[128,1024]{1,0:T(8,128)(2,1)S(1)}, bf16[128,1024]{1,0:T(8,128)(2,1)S(1)}, u32[]{:S(2)}, u32[]{:S(2)}) collective-permute-start(bf16[128,1024]{1,0:T(8,128)(2,1)S(1)} %get-tuple-element.41), channel_id=1, source_target_pairs={{0,2},{1,3},{2,0},{3,1},{4,6},{5,7},{6,4},{7,5},{8,10},{9,11},{10,... | collective-permute-start | bytes 786440 | tf_op jit(solution)/shard_map/ppermute | solution.py:161
  662.6 16.0 %collective-permute-start.27 = (bf16[32,4096]{1,0:T(8,128)(2,1)S(1)}, bf16[32,4096]{1,0:T(8,128)(2,1)S(1)}, u32[]{:S(2)}, u32[]{:S(2)}) collective-permute-start(bf16[32,4096]{1,0:T(8,128)(2,1)S(1)} %get-tuple-element.42), channel_id=1, source_target_pairs={{0,1},{1,2},{2,3},{3,0},{4,5},{5,6},{6,7},{7,4},{8,9},{9,10},{10,1... | collective-permute-start | bytes 786440 | tf_op jit(solution)/shard_map/ppermute | solution.py:161
  662.8 31.0 %collective-permute-start.28 = (bf16[32,4096]{1,0:T(8,128)(2,1)S(1)}, bf16[32,4096]{1,0:T(8,128)(2,1)S(1)}, u32[]{:S(2)}, u32[]{:S(2)}) collective-permute-start(bf16[32,4096]{1,0:T(8,128)(2,1)S(1)} %get-tuple-element.44), channel_id=1, source_target_pairs={{0,2},{1,3},{2,0},{3,1},{4,6},{5,7},{6,4},{7,5},{8,10},{9,11},{10,... | collective-permute-start | bytes 786440 | tf_op jit(solution)/shard_map/ppermute | solution.py:161
  664.6 40.3 %collective-permute-start.29 = (bf16[32,4096]{1,0:T(8,128)(2,1)S(1)}, bf16[32,4096]{1,0:T(8,128)(2,1)S(1)}, u32[]{:S(2)}, u32[]{:S(2)}) collective-permute-start(bf16[32,4096]{1,0:T(8,128)(2,1)S(1)} %get-tuple-element.43), channel_id=1, source_target_pairs={{0,3},{1,0},{2,1},{3,2},{4,7},{5,4},{6,5},{7,6},{8,11},{9,8},{10,9... | collective-permute-start | bytes 786440 | tf_op jit(solution)/shard_map/ppermute | solution.py:161
  678.6 30.7 %collective-permute-start.35 = (bf16[128,1024]{1,0:T(8,128)(2,1)S(1)}, bf16[128,1024]{1,0:T(8,128)(2,1)S(1)}, u32[]{:S(2)}, u32[]{:S(2)}) collective-permute-start(bf16[128,1024]{1,0:T(8,128)(2,1)S(1)} %get-tuple-element.40), channel_id=1, source_target_pairs={{0,3},{1,0},{2,1},{3,2},{4,7},{5,4},{6,5},{7,6},{8,11},{9,8},{10,9... | collective-permute-start | bytes 786440 | tf_op jit(solution)/shard_map/ppermute | solution.py:161
  693.9 19.9 %collective-permute-start.15 = (bf16[32,3072]{1,0:T(8,128)(2,1)S(1)}, bf16[32,3072]{1,0:T(8,128)(2,1)S(1)}, u32[]{:S(2)}, u32[]{:S(2)}) collective-permute-start(bf16[32,3072]{1,0:T(8,128)(2,1)S(1)} %get-tuple-element.45), channel_id=1, source_target_pairs={{0,1},{1,2},{2,3},{3,0},{4,5},{5,6},{6,7},{7,4},{8,9},{9,10},{10,1... | collective-permute-start | bytes 589832 | tf_op jit(solution)/shard_map/ppermute | solution.py:161
  705.0 15.5 %collective-permute-start.16 = (bf16[32,3072]{1,0:T(8,128)(2,1)S(1)}, bf16[32,3072]{1,0:T(8,128)(2,1)S(1)}, u32[]{:S(2)}, u32[]{:S(2)}) collective-permute-start(bf16[32,3072]{1,0:T(8,128)(2,1)S(1)} %get-tuple-element.47), channel_id=1, source_target_pairs={{0,2},{1,3},{2,0},{3,1},{4,6},{5,7},{6,4},{7,5},{8,10},{9,11},{10,... | collective-permute-start | bytes 589832 | tf_op jit(solution)/shard_map/ppermute | solution.py:161
  709.2 11.2 %collective-permute-start.17 = (bf16[32,3072]{1,0:T(8,128)(2,1)S(1)}, bf16[32,3072]{1,0:T(8,128)(2,1)S(1)}, u32[]{:S(2)}, u32[]{:S(2)}) collective-permute-start(bf16[32,3072]{1,0:T(8,128)(2,1)S(1)} %get-tuple-element.46), channel_id=1, source_target_pairs={{0,3},{1,0},{2,1},{3,2},{4,7},{5,4},{6,5},{7,6},{8,11},{9,8},{10,9... | collective-permute-start | bytes 589832 | tf_op jit(solution)/shard_map/ppermute | solution.py:161
  (81 other events, 426.3 us)
Sparse Core Ops, SparseCore 0:
  10.9 81.0 all-gather.5
  94.9 61.5 all-gather.7
  159.5 76.2 all-gather.9
  238.5 75.9 all-gather.11

commit v2 on v1

v2 whole, which is shorter than its diff:
```python
from functools import partial

import jax
import jax.numpy as jnp
from jax import lax
from jax.experimental import pallas as pl
from jax.experimental.pallas import tpu as pltpu
from jax.sharding import PartitionSpec as P

HD = 64


EPS = 1e-06

AXES = ("shard", "seq")

bf16 = jnp.bfloat16
f32 = jnp.float32


def modulate(tokens, shift_by, scale_by):
    average = jnp.mean(tokens, axis=-1, keepdims=True)
    centered = tokens - average
    variance = jnp.mean(centered * centered, axis=-1, keepdims=True)
    return centered * lax.rsqrt(variance + EPS) * (1.0 + scale_by) + shift_by


def cross_rows(left, right):
    return lax.dot_general(left, right, (((0,), (0,)), ((), ())), preferred_element_type=f32)


def along_cols(left, right):
    return lax.dot_general(left, right, (((1,), (1,)), ((), ())), preferred_element_type=f32)


def plain(left, right):
    return jnp.dot(left, right, preferred_element_type=f32)


LIMIT = 48 * 1024 * 1024


def call(kernel, flops, **kwargs):
    return pl.pallas_call(
        kernel,
        compiler_params=pltpu.CompilerParams(vmem_limit_bytes=LIMIT),
        cost_estimate=pl.CostEstimate(flops=flops // 50, bytes_accessed=flops // 10000, transcendentals=0),
        **kwargs,
    )


def transposed_dot(left, right):
    return lax.dot_general(left, right, (((1,), (1,)), ((), ())), preferred_element_type=f32)


def project_kernel(x_ref, low_ref, high_ref, bias_ref, out_ref):
    half = low_ref.shape[0]
    total = jnp.dot(x_ref[:, :half], low_ref[...], preferred_element_type=f32)
    total = total + jnp.dot(x_ref[:, half:], high_ref[...], preferred_element_type=f32)
    out_ref[...] = (total + bias_ref[...]).astype(out_ref.dtype)


def project(x, weight, begin, columns, bias, dtype):
    low, high = weight
    rows, depth = x.shape
    tile = 512
    first = begin // tile
    pick = lambda step: (0, first + step)
    return call(
        project_kernel,
        2 * rows * depth * columns,
        grid=(columns // tile,),
        in_specs=[
            pl.BlockSpec((rows, depth), lambda step: (0, 0)),
            pl.BlockSpec((depth // 2, tile), pick),
            pl.BlockSpec((depth // 2, tile), pick),
            pl.BlockSpec((1, tile), lambda step: (0, step)),
        ],
        out_specs=pl.BlockSpec((rows, tile), lambda step: (0, step)),
        out_shape=jax.ShapeDtypeStruct((rows, columns), dtype),
    )(x, low, high, bias.reshape(1, -1))


def unproject_kernel(rows_ref, weight_ref, out_ref):
    width = rows_ref.shape[2]
    total = transposed_dot(rows_ref[0], weight_ref[:, :width])
    total = total + transposed_dot(rows_ref[1], weight_ref[:, width : 2 * width])
    out_ref[...] = total + transposed_dot(rows_ref[2], weight_ref[:, 2 * width :])


def unproject(rows, weight):
    _, count, width = rows.shape
    depth = weight.shape[0]
    tile = 256
    return call(
        unproject_kernel,
        6 * count * depth * width,
        grid=(depth // tile,),
        in_specs=[
            pl.BlockSpec((3, count, width), lambda step: (0, 0, 0)),
            pl.BlockSpec((tile, 3 * width), lambda step: (step, 0)),
        ],
        out_specs=pl.BlockSpec((count, tile), lambda step: (0, step)),
        out_shape=jax.ShapeDtypeStruct((count, depth), f32),
    )(rows, weight)


def attend_forward_kernel(q_ref, *refs):
    keys, values = refs[0:2], refs[2:4]
    out_ref, log_ref = refs[4:]
    count = q_ref.shape[0]
    outputs = []
    for head in range(2):
        cols = slice(head * HD, (head + 1) * HD)
        query = q_ref[:, cols] * jnp.bfloat16(HD ** (-0.5))
        scores = [transposed_dot(query, key[:, cols]) for key in keys]
        highest = jnp.maximum(
            jnp.max(scores[0], axis=1, keepdims=True), jnp.max(scores[1], axis=1, keepdims=True)
        )
        expon = [jnp.exp(score - highest) for score in scores]
        summed = jnp.sum(expon[0], axis=1, keepdims=True) + jnp.sum(expon[1], axis=1, keepdims=True)
        mixed = jnp.dot(expon[0].astype(bf16), values[0][:, cols], preferred_element_type=f32)
        mixed = mixed + jnp.dot(expon[1].astype(bf16), values[1][:, cols], preferred_element_type=f32)
        outputs.append(mixed / summed)
        logs = jnp.broadcast_to(highest + jnp.log(summed), (count, 128))
        log_ref[head] = jnp.transpose(logs)[0:1]
    out_ref[...] = jnp.concatenate(outputs, axis=1).astype(bf16)


def attend_forward(queries, keys, values):
    count, width = queries.shape
    pair = pl.BlockSpec((count, 2 * HD), lambda step: (0, step))
    steps = width // (2 * HD)
    return call(
        attend_forward_kernel,
        16 * count * count * width,
        grid=(steps,),
        in_specs=[pair] * 5,
        out_specs=[pair, pl.BlockSpec((2, 1, count), lambda step: (step, 0, 0))],
        out_shape=[
            jax.ShapeDtypeStruct((count, width), bf16),
            jax.ShapeDtypeStruct((2 * steps, 1, count), f32),
        ],
    )(queries, *keys, *values)


def attend_backward_kernel(q_ref, g_ref, log_ref, *refs):
    keys, values = refs[0:2], refs[2:4]
    own_ref, other_ref = refs[-2:]
    grads = [[], [], [], [], []]
    factor = HD ** (-0.5)
    for head in range(2):
        cols = slice(head * HD, (head + 1) * HD)
        query = q_ref[:, cols] * jnp.bfloat16(factor)
        grad = g_ref[:, cols]
        logs = log_ref[head]
        probs = [jnp.exp(transposed_dot(key[:, cols], query) - logs) for key in keys]
        grad_probs = [transposed_dot(value[:, cols], grad) for value in values]
        inner = jnp.sum(probs[0] * grad_probs[0], axis=0, keepdims=True)
        inner = inner + jnp.sum(probs[1] * grad_probs[1], axis=0, keepdims=True)
        grad_query = 0.0
        for side in range(2):
            grad_scores = (probs[side] * (grad_probs[side] - inner)).astype(bf16)
            grads[1 + 2 * side].append(jnp.dot(grad_scores, query, preferred_element_type=f32))
            grads[2 + 2 * side].append(
                jnp.dot(probs[side].astype(bf16), grad, preferred_element_type=f32)
            )
            grad_query = grad_query + cross_rows(grad_scores, keys[side][:, cols])
        grads[0].append(factor * grad_query)
    joined = [jnp.concatenate(part, axis=1).astype(bf16) for part in grads]
    for place in range(3):
        own_ref[place] = joined[place]
    for place in range(2):
        other_ref[place] = joined[3 + place]


def attend_backward(queries, grad_mixed, logs, keys, values, begin, steps, so_far):
    count, width = queries.shape
    pair = pl.BlockSpec((count, 2 * HD), lambda step: (0, begin + step))
    own = pl.BlockSpec((3, count, 2 * HD), lambda step: (0, 0, begin + step))
    other = pl.BlockSpec((2, count, 2 * HD), lambda step: (0, 0, begin + step))
    log_spec = pl.BlockSpec((2, 1, count), lambda step: (begin + step, 0, 0))
    operands = [queries, grad_mixed, logs, *keys, *values]
    specs = [pair, pair, log_spec] + [pair] * 4
    aliases = {}
    if so_far is not None:
        aliases = {len(operands): 0, len(operands) + 1: 1}
        operands = operands + list(so_far)
        specs = specs + [pl.BlockSpec(memory_space=pl.ANY)] * 2
    return call(
        attend_backward_kernel,
        40 * count * count * 2 * HD * steps,
        grid=(steps,),
        in_specs=specs,
        out_specs=[own, other],
        out_shape=[
            jax.ShapeDtypeStruct((3, count, width), bf16),
            jax.ShapeDtypeStruct((2, count, width), bf16),
        ],
        input_output_aliases=aliases,
    )(*operands)


def mlp_forward_kernel(x_ref, up_ref, down_ref, up_bias_ref, down_bias_ref, hidden_ref, slope_ref, out_ref):
    tile = hidden_ref.shape[1]
    pre = jnp.dot(x_ref[...], up_ref[...].reshape(-1, tile), preferred_element_type=f32)
    pre = pre + up_bias_ref[...]
    root, cubic = 0.7978845608028654, 0.044715
    square = pre * pre
    wave = jnp.tanh(root * pre * (1.0 + cubic * square))
    half = 0.5 * (1.0 + wave)
    slope = half + 0.5 * pre * (1.0 - wave * wave) * (root * (1.0 + 3.0 * cubic * square))
    slope_ref[...] = slope.astype(bf16)
    hidden = (pre * half).astype(bf16)
    hidden_ref[...] = hidden
    down = down_ref[...].reshape(tile, -1)

    @pl.when(pl.program_id(0) == 0)
    def _():
        out_ref[...] = jnp.broadcast_to(down_bias_ref[...], out_ref.shape)

    out_ref[...] += jnp.dot(hidden, down, preferred_element_type=f32)


def mlp_forward(x, mlp, up_bias, down_bias):
    count, width = x.shape
    hidden_width = up_bias.shape[0]
    tile = 512
    whole = pl.BlockSpec((count, width), lambda step: (0, 0))
    part = pl.BlockSpec((count, tile), lambda step: (0, step))
    return call(
        mlp_forward_kernel,
        4 * count * width * hidden_width,
        grid=(hidden_width // tile,),
        in_specs=[whole]
        + mlp.specs(tile)
        + [
            pl.BlockSpec((1, tile), lambda step: (0, step)),
            pl.BlockSpec((1, width), lambda step: (0, 0)),
        ],
        out_specs=[part, part, whole],
        out_shape=[
            jax.ShapeDtypeStruct((count, hidden_width), bf16),
            jax.ShapeDtypeStruct((count, hidden_width), bf16),
            jax.ShapeDtypeStruct((count, width), f32),
        ],
    )(x, *mlp.arrays, up_bias.reshape(1, -1), down_bias.reshape(1, -1))


def mlp_backward_kernel(grad_ref, up_ref, down_ref, slope_ref, grad_pre_ref, sums_ref, out_ref):
    tile = slope_ref.shape[1]
    grad_hidden = transposed_dot(grad_ref[...], down_ref[...].reshape(tile, -1))
    grad_pre = (grad_hidden * slope_ref[...].astype(f32)).astype(bf16)
    grad_pre_ref[...] = grad_pre
    sums_ref[...] = jnp.sum(grad_pre.astype(f32), axis=0, keepdims=True)

    @pl.when(pl.program_id(0) == 0)
    def _():
        out_ref[...] = jnp.zeros(out_ref.shape, f32)

    out_ref[...] += transposed_dot(grad_pre, up_ref[...].reshape(-1, tile))


def mlp_backward(grad, mlp, slope):
    count, width = grad.shape
    hidden_width = slope.shape[1]
    tile = 512
    whole = pl.BlockSpec((count, width), lambda step: (0, 0))
    part = pl.BlockSpec((count, tile), lambda step: (0, step))
    return call(
        mlp_backward_kernel,
        4 * count * width * hidden_width,
        grid=(hidden_width // tile,),
        in_specs=[whole] + mlp.specs(tile) + [part],
        out_specs=[part, pl.BlockSpec((1, tile), lambda step: (0, step)), whole],
        out_shape=[
            jax.ShapeDtypeStruct((count, hidden_width), bf16),
            jax.ShapeDtypeStruct((1, hidden_width), f32),
            jax.ShapeDtypeStruct((count, width), f32),
        ],
    )(grad, *mlp.arrays, slope)


class FeedForward:
    def __init__(self, up, down):
        self.rows_up, hidden_width = up.shape
        self.rows_down, self.width = down.shape
        cut_up = up.reshape(self.rows_up, -1, self.width).transpose(1, 0, 2).reshape(-1, self.width)
        both = lax.all_gather(jnp.concatenate([cut_up, down], axis=0), AXES, axis=0, tiled=False)
        self.in_place = self.rows_up % 16 == 0 and self.rows_down == cut_up.shape[0]
        if self.in_place:
            self.arrays = (both, both)
        else:
            devices = both.shape[0]
            up = both[:, : cut_up.shape[0]].reshape(devices, -1, self.rows_up, self.width)
            up = up.transpose(0, 2, 1, 3).reshape(1, devices * self.rows_up, hidden_width)
            down = both[:, cut_up.shape[0] :].reshape(1, hidden_width, self.width)
            self.arrays = (up, down)

    def specs(self, tile):
        up, down = self.arrays
        if not self.in_place:
            return [
                pl.BlockSpec((1, up.shape[1], tile), lambda step: (0, 0, step)),
                pl.BlockSpec((1, tile, self.width), lambda step: (0, step, 0)),
            ]
        across = self.width // tile
        return [
            pl.BlockSpec(
                (up.shape[0], self.rows_up, tile), lambda step: (0, step // across, step % across)
            ),
            pl.BlockSpec(
                (tile // self.rows_down, self.rows_down, self.width), lambda step: (step, 1, 0)
            ),
        ]


class Places:
    def __init__(self, latents):
        self.shards = lax.axis_size("shard")
        self.groups = lax.axis_size("seq")
        self.devices = self.shards * self.groups
        self.latents = latents
        assert 2 * latents == self.groups
        self.shard = lax.axis_index("shard")
        self.seq = lax.axis_index("seq")
        self.flat = self.shard * self.groups + self.seq
        self.core = self.shard % 2
        self.slot = self.seq % latents
        self.moves = []
        for turn in range(latents):
            move = []
            for source in range(self.devices):
                pair, core = divmod(source // self.groups, 2)
                half, place = divmod(source % self.groups, latents)
                member = (place + turn) % latents
                target = (2 * pair + half) * self.groups + core * latents + member
                move.append((source, target))
            self.moves.append(move)

    def to_pairs(self, blocks):
        parts = []
        for turn, move in enumerate(self.moves):
            member = (self.slot + turn) % self.latents
            block = lax.dynamic_index_in_dim(blocks, member, 0, keepdims=False)
            parts.append(lax.ppermute(block, AXES, move))
        return parts

    def from_pairs(self, rows):
        tokens = rows.shape[0] // self.latents
        parts = []
        for turn, move in enumerate(self.moves):
            block = rows[turn * tokens : (turn + 1) * tokens]
            parts.append(lax.ppermute(block, AXES, [(b, a) for a, b in move]))
        return parts

    def placed(self, parts):
        if len(parts) == 2:
            straight = self.slot == 0
            return jnp.stack(
                [jnp.where(straight, parts[0], parts[1]), jnp.where(straight, parts[1], parts[0])]
            )
        twice = jnp.stack(parts + parts)
        start = (self.latents - self.slot) % self.latents
        return lax.dynamic_slice_in_dim(twice, start, self.latents, axis=0)

    def across(self, array, mask=1):
        return lax.ppermute(array, "shard", [(s, s ^ mask) for s in range(self.shards)])

    def order(self):
        near = list(range(0, self.shards, 2))
        return near + [each ^ 1 for each in near]

    def arranged(self, matrix):
        width = matrix.shape[1] // self.shards
        return jnp.concatenate(
            [
                lax.dynamic_slice_in_dim(matrix, (self.shard ^ near) * width, width, axis=1)
                for near in self.order()
            ],
            axis=1,
        )

    def restored(self, matrix):
        width = matrix.shape[1] // self.shards
        order = self.order()
        places = jnp.array([order.index(near) for near in range(self.shards)], jnp.int32)
        return jnp.concatenate(
            [
                lax.dynamic_slice_in_dim(matrix, places[self.shard ^ s] * width, width, axis=1)
                for s in range(self.shards)
            ],
            axis=1,
        )

    def along_seq(self, block):
        parts = [block]
        for away in range(self.groups - 1, 0, -1):
            shift = [(q, (q + away) % self.groups) for q in range(self.groups)]
            parts.append(lax.ppermute(block, "seq", shift))
        start = ((self.groups - self.seq) % self.groups) * block.shape[0]
        twice = jnp.concatenate(parts + parts, axis=0)
        return lax.dynamic_slice_in_dim(twice, start, block.shape[0] * self.groups, axis=0)

    def gathered(self, block):
        parts = [block] + [self.across(block, mask) for mask in range(2, self.shards, 2)]
        return parts


class Reduction:
    def __init__(self, at, columns, right):
        self.at, self.columns, self.right = at, columns, right
        self.width = columns.shape[1] // at.shards
        self.received = []

    def piece(self, low, high):
        low, high = low * self.width, high * self.width
        left = self.columns[:, low:high]
        if self.right.ndim == 3:
            total = jnp.einsum("tm,ptn->pmn", left, self.right, preferred_element_type=f32)
        else:
            total = cross_rows(left, self.right)
        if self.received:
            total = total + self.received[0][..., low:high, :].astype(f32)
        return total

    def first(self):
        half = self.at.shards // 2
        return self.piece(half, 2 * half).astype(bf16)

    def send_first(self, block):
        self.received = [self.at.across(block)]

    def middle(self):
        return [self.piece(each, each + 1).astype(bf16) for each in range(1, self.at.shards // 2)]

    def send_middle(self, blocks):
        for each, block in enumerate(blocks):
            self.received.append(self.at.across(block, 2 * (each + 1)))

    def last(self):
        total = self.piece(0, 1)
        for part in self.received[1:]:
            total = total + part.astype(f32)
        return total.astype(bf16)

    def swap_last(self, block):
        groups = self.at.groups
        came = lax.all_to_all(block, "seq", 0, 0, tiled=True)
        return list(came.reshape(groups, -1, block.shape[1]))

    def split_last(self, total):
        at = self.at
        rows = self.width // at.groups

        def block(away):
            begin = ((at.seq + away) % at.groups) * rows
            return lax.dynamic_slice_in_dim(total, begin, rows, axis=total.ndim - 2)

        return [block(away) for away in range(at.groups)]

    def send_last(self, blocks):
        at = self.at
        came = []
        for away in range(1, at.groups):
            shift = [(q, (q + away) % at.groups) for q in range(at.groups)]
            came.append(lax.ppermute(blocks[away], "seq", shift))
        return blocks[:1] + came


def total_of(blocks):
    total = blocks[0].astype(f32)
    for block in blocks[1:]:
        total = total + block.astype(f32)
    return total


def tied(*arrays):
    return lax.optimization_barrier(arrays)


def shards(
    hidden_in,
    condition,
    out_grad,
    ada_weight,
    qkv_weight,
    proj_weight,
    up_weight,
    down_weight,
    ada_bias,
    qv_bias,
    proj_bias,
    up_bias,
    down_bias,
):
    latents, local_len, width = hidden_in.shape
    at = Places(latents)
    pairs = at.shards // 2
    total_latents = pairs * at.groups
    depth = ada_weight.shape[0]

    mlp = FeedForward(up_weight, down_weight)
    near_rows = at.along_seq(jnp.concatenate([qkv_weight, proj_weight], axis=1))

    silu_rows = jax.nn.silu(condition.astype(f32)).astype(bf16)
    silu_rows = silu_rows.reshape(latents, at.shards, at.groups, depth)
    silu_rows = lax.dynamic_index_in_dim(silu_rows, at.seq, 2, keepdims=False)
    silu_rows = silu_rows.transpose(1, 0, 2).reshape(at.shards, latents * depth)
    silu_rows = lax.all_to_all(silu_rows, "shard", 0, 0, tiled=True).reshape(total_latents, depth)
    share = plain(silu_rows, ada_weight)
    wide = share.shape[1]
    share = share.reshape(pairs, at.groups, 2, wide // 2).transpose(0, 2, 1, 3)
    share = share.reshape(at.devices, wide // 2)
    biases = jnp.concatenate([ada_bias, qv_bias, proj_bias, up_bias, down_bias]).astype(f32)
    cuts = [ada_bias.shape[0], qv_bias.shape[0], proj_bias.shape[0], up_bias.shape[0], down_bias.shape[0]]
    sent = jnp.concatenate([share, jnp.broadcast_to(biases, (at.devices, biases.shape[0]))], axis=1)
    sent, near_rows, hidden_in = tied(sent, near_rows, hidden_in)
    came = lax.all_to_all(sent, AXES, 0, 0, tiled=True)
    near_parts = at.gathered(near_rows)
    tokens = at.to_pairs(hidden_in)
    came, *tokens = tied(came, *tokens)
    mine = jnp.sum(came[:, : wide // 2], axis=0)
    other = at.across(mine)
    modulation = jnp.where(
        at.core == 0, jnp.concatenate([mine, other]), jnp.concatenate([other, mine])
    )
    whole = []
    begin = wide // 2
    for cut in cuts:
        whole.append(came[:, begin : begin + cut].reshape(-1))
        begin += cut
    b_ada, b_qv, b_proj, b_up, b_down = whole
    modulation = (modulation + b_ada).reshape(6, width)
    shift_a, scale_a, gate_a, shift_m, scale_m, gate_m = [modulation[member] for member in range(6)]

    tokens = jnp.concatenate(tokens, axis=0).astype(f32)
    normed = modulate(tokens, shift_a, scale_a).astype(bf16)
    normed_cols = at.arranged(normed)
    normed_cols, *near_parts = tied(normed_cols, *near_parts)
    weight = jnp.concatenate(near_parts, axis=0)
    weight = (weight, at.across(weight))
    key_own = project(normed_cols, weight, width, width, jnp.zeros((width,), f32), bf16)
    keys = (key_own, at.across(key_own))
    value_own = project(normed_cols, weight, 2 * width, width, b_qv[width:], bf16)
    values = (value_own, at.across(value_own))
    queries = project(normed_cols, weight, 0, width, b_qv[:width], bf16)
    queries, out_grad = tied(queries, out_grad)
    cotangent = at.to_pairs(out_grad)
    mixed, logs = attend_forward(queries, keys, values)
    mixed_cols = at.arranged(mixed)
    attn_out = project(mixed_cols, weight, 3 * width, width, b_proj, f32)
    middle = tokens + gate_a * attn_out
    normed_two = modulate(middle, shift_m, scale_m).astype(bf16)
    hidden, slope, mlp_out = mlp_forward(normed_two, mlp, b_up, b_down)
    hidden, *cotangent = tied(hidden, *cotangent)
    block_rows = (middle + gate_m * mlp_out).astype(bf16)

    cotangent = jnp.concatenate(cotangent, axis=0).astype(f32)
    grad_gate_m = jnp.sum(cotangent * mlp_out, axis=0)
    grad_mlp = (gate_m * cotangent).astype(bf16)
    grad_bdown = jnp.sum(grad_mlp.astype(f32), axis=0)
    down_sum = Reduction(at, at.arranged(hidden), grad_mlp)
    slope, block, block_rows = tied(slope, down_sum.first(), block_rows)
    down_sum.send_first(block)
    block_out = at.from_pairs(block_rows)
    grad_pre, grad_bup, grad_normed_two = mlp_backward(grad_mlp, mlp, slope)
    grad_pre, grad_normed_two, *down_sum.received = tied(
        grad_pre, grad_normed_two, *down_sum.received
    )
    up_sum = Reduction(at, at.arranged(normed_two), grad_pre)
    grad_normed_two, block, *blocks = tied(grad_normed_two, up_sum.first(), *down_sum.middle())
    down_sum.send_middle(blocks)
    up_sum.send_first(block)
    _, second_back = jax.vjp(modulate, middle, shift_m, scale_m)
    grad_middle, grad_shift_m, grad_scale_m = second_back(grad_normed_two)
    grad_middle = grad_middle + cotangent

    grad_gate_a = jnp.sum(grad_middle * attn_out, axis=0)
    grad_attn = (gate_a * grad_middle).astype(bf16)
    grad_bproj = jnp.sum(grad_attn.astype(f32), axis=0)
    grad_mixed = jnp.concatenate(
        [along_cols(grad_attn, half[:, 3 * width :]).astype(bf16) for half in weight], axis=1
    )
    grad_mixed = at.restored(grad_mixed)
    proj_sum = Reduction(at, mixed_cols, grad_attn)
    grad_mixed, *up_sum.received = tied(grad_mixed, *up_sum.received)
    grad_mixed, block, *blocks = tied(grad_mixed, proj_sum.first(), *up_sum.middle())
    up_sum.send_middle(blocks)
    proj_sum.send_first(block)
    head_pairs = width // (2 * HD)
    cut = head_pairs // 2
    grads = attend_backward(queries, grad_mixed, logs, keys, values, 0, cut, None)
    *grads, proj_sum.received, down_sum.received, block_out = tied(
        *grads, proj_sum.received, down_sum.received, block_out
    )
    *grads, block = tied(*grads, down_sum.last())
    down_came = down_sum.swap_last(block)
    own_grads, other_grads = attend_backward(
        queries, grad_mixed, logs, keys, values, cut, head_pairs - cut, grads
    )
    own_grads, other_grads, down_came, up_sum.received = tied(
        own_grads, other_grads, down_came, up_sum.received
    )
    other_grads, up_block, *blocks = tied(other_grads, up_sum.last(), *proj_sum.middle())
    kv_came = at.across(other_grads)
    up_came = up_sum.swap_last(up_block)
    proj_sum.send_middle(blocks)
    grad_rows = jnp.concatenate([own_grads[:1], own_grads[1:] + kv_came], axis=0)
    qkv_sum = Reduction(at, normed_cols, grad_rows)
    grad_rows, block = tied(grad_rows, qkv_sum.first())
    qkv_sum.send_first(block)
    down_share = total_of(down_came)
    column_sums = jnp.sum(grad_rows.astype(f32), axis=1)
    grad_bqv = jnp.concatenate([column_sums[0], column_sums[2]])
    grad_normed = [unproject(grad_rows, weight[0])]
    grad_normed[0], qkv_sum.received, proj_sum.received = tied(
        grad_normed[0], qkv_sum.received, proj_sum.received
    )
    grad_rows, block, *blocks = tied(grad_rows, proj_sum.last(), *qkv_sum.middle())
    qkv_sum.send_middle(blocks)
    proj_came = proj_sum.swap_last(block)
    grad_normed.append(unproject(grad_rows, weight[1]))
    grad_normed = at.restored(jnp.concatenate(grad_normed, axis=1))
    _, first_back = jax.vjp(modulate, tokens, shift_a, scale_a)
    grad_tokens, grad_shift_a, grad_scale_a = first_back(grad_normed)
    hidden_rows = (grad_tokens + grad_middle).astype(bf16)

    part_mod = jnp.concatenate(
        [grad_shift_a, grad_scale_a, grad_gate_a, grad_shift_m, grad_scale_m, grad_gate_m]
    )
    part_mod, hidden_rows, up_came = tied(part_mod, hidden_rows, up_came)
    mod_came = at.across(part_mod)
    hidden_grad = at.from_pairs(hidden_rows)
    grad_mod = (part_mod + mod_came).astype(bf16)
    half_mod = lax.dynamic_slice_in_dim(grad_mod, at.core * (wide // 2), wide // 2).astype(f32)
    bias_parts = [
        part.reshape(at.devices, -1) for part in (grad_bqv, grad_bproj, grad_bup, grad_bdown)
    ]
    sent = jnp.concatenate(
        [jnp.broadcast_to(half_mod, (at.devices, wide // 2))] + bias_parts, axis=1
    )
    came = lax.all_to_all(sent, AXES, 0, 0, tiled=True)
    came, proj_came, hidden_grad, qkv_sum.received = tied(
        came, proj_came, hidden_grad, qkv_sum.received
    )
    came, block = tied(came, qkv_sum.last())
    qkv_came = qkv_sum.send_last(qkv_sum.split_last(block))
    up_share, proj_share = total_of(up_came), total_of(proj_came)
    every_mod = came[:, : wide // 2].reshape(pairs, 2, at.groups, wide // 2)
    every_mod = every_mod.transpose(0, 2, 1, 3).reshape(total_latents, wide).astype(bf16)
    bias_sums = jnp.sum(came[:, wide // 2 :], axis=0)
    bias_shares = []
    begin = 0
    for part in bias_parts:
        bias_shares.append(bias_sums[begin : begin + part.shape[1]])
        begin += part.shape[1]
    ada_share = cross_rows(silu_rows, every_mod)
    own_bias = ada_bias.shape[0]
    adabias_share = jnp.sum(
        lax.dynamic_slice_in_dim(every_mod, at.flat * own_bias, own_bias, axis=1).astype(f32), axis=0
    )
    grad_silu = along_cols(every_mod, ada_weight).reshape(at.shards, 1, latents * depth)
    sent = jnp.broadcast_to(grad_silu, (at.shards, at.groups, latents * depth))
    came = lax.all_to_all(sent.reshape(at.devices, latents * depth), AXES, 0, 0, tiled=True)
    grad_silu = came.reshape(at.devices, latents, depth).transpose(1, 0, 2).reshape(latents, width)
    _, silu_back = jax.vjp(jax.nn.silu, condition.astype(f32))
    condition_grad = silu_back(grad_silu)[0]
    qkv_share = total_of(qkv_came).transpose(1, 0, 2).reshape(-1, 3 * width)
    return (
        at.placed(block_out),
        at.placed(hidden_grad).astype(f32),
        condition_grad,
        ada_share,
        qkv_share,
        proj_share,
        up_share,
        down_share,
        adabias_share,
        bias_shares[0],
        bias_shares[1],
        bias_shares[2],
        bias_shares[3],
    )


def solution(mesh):
    in_specs = (
        P("shard", "seq", None),
        P("shard", None),
        P("shard", "seq", None),
        P(("shard", "seq"), None),
        P(("shard", "seq"), None),
        P(("shard", "seq"), None),
        P(("shard", "seq"), None),
        P(("shard", "seq"), None),
        P(("shard", "seq")),
        P(("shard", "seq")),
        P(("shard", "seq")),
        P(("shard", "seq")),
        P(("shard", "seq")),
    )
    out_specs = (
        P("shard", "seq", None),
        P("shard", "seq", None),
        P("shard", None),
        P(("shard", "seq"), None),
        P(("shard", "seq"), None),
        P(("shard", "seq"), None),
        P(("shard", "seq"), None),
        P(("shard", "seq"), None),
        P(("shard", "seq")),
        P(("shard", "seq")),
        P(("shard", "seq")),
        P(("shard", "seq")),
        P(("shard", "seq")),
    )
    return jax.shard_map(shards, mesh=mesh, in_specs=in_specs, out_specs=out_specs, check_vma=False)
```

time: 736 us -> 566 us (0.77)
  matrix products: 208 us -> 68.5 us
  waiting for transfers between devices: 281 us -> 171 us
  Pallas kernels: 0 us -> 109 us
  other arithmetic: 83.7 us -> 36.9 us
  starting transfers between devices: 75.4 us -> 92.4 us
  blocking collectives: 11.9 us -> 0 us
    all_gather x4 -> x1, waiting for transfers between devices: 152 us -> 0.01 us  [__init__(): lax.all_gather(jnp.concatenate([cut_up, down], axis=0), AXES, axis=0, til...]
    pallas_call x0 -> x11, Pallas kernels: none -> 109 us  [the longest x2 35.8 us: attend_backward(): call(attend_backward_kernel, 40 * count * count * 2 * HD * steps, grid=(s...]
    dot_general x6 -> x5, matrix products: 85.3 us -> 16.1 us  [piece(): jnp.einsum('tm,ptn->pmn', left, self.right, preferred_element_type=f32)]
    dot_general x6 -> x1, matrix products: 37.8 us -> 0.19 us  [plain(): return jnp.dot(left, right, preferred_element_type=f32)]
    convert_element_type x4 -> x3, other arithmetic: 36.3 us -> 5.68 us  [the longest x1 4.2 us: last(): return total.astype(bf16)]
    all_to_all x0 -> x4, waiting for transfers between devices: none -> 24.9 us  [the longest x3 20.5 us: swap_last(): came = lax.all_to_all(block, 'seq', 0, 0, tiled=True)]
    dot_general x5 -> x3, matrix products: 28.8 us -> 4.54 us  [along_cols(): lax.dot_general(left, right, (((1,), (1,)), ((), ())), preferred_element_...]
    all_to_all x0 -> x4, starting transfers between devices: none -> 16.3 us  [the longest x3 12.6 us: swap_last(): came = lax.all_to_all(block, 'seq', 0, 0, tiled=True)]
  transfers between devices with their start and end apart: 43 -> 47, of which waited for: 14 -> 12; matrix products, arithmetic and copies ran while one was open for 34% -> 15% of each run, Pallas kernels for 0% -> 19%
where the time goes in v2:
time: 566 us; the launch traced here: 558 us
  waiting for transfers between devices  171 us (30%)
  Pallas kernels  109 us (19%)
  starting transfers between devices  92.4 us (16%)
  matrix products  68.5 us (12%)
  local copies, waits for them, and re-layouts  59.1 us (10%)
  other arithmetic  36.9 us (7%)
  between operations  20.9 us (4%)
    ppermute x25, waiting for transfers between devices, across(): lax.ppermute(array, 'shard', [(s, s ^ mask) for s in range(self.shards)])  55.8 us
    dot_general x16, matrix products, cross_rows(): lax.dot_general(left, right, (((0,), (0,)), ((), ())), preferred_element_...  47.7 us
    all_to_all x2, waiting for transfers between devices, shards(): came = lax.all_to_all(sent, AXES, 0, 0, tiled=True)  45.4 us
    pallas_call x2, Pallas kernels, attend_backward(): call(attend_backward_kernel, 40 * count * count * 2 * HD * steps, grid=(s...  35.8 us
    ppermute x25, starting transfers between devices, across(): lax.ppermute(array, 'shard', [(s, s ^ mask) for s in range(self.shards)])  34.5 us
    unnamed x158, local copies, waits for them, and re-layouts  28.7 us
    ppermute x3, waiting for transfers between devices, along_seq(): parts.append(lax.ppermute(block, 'seq', shift))  22 us
    pallas_call x1, Pallas kernels, attend_forward(): call(attend_forward_kernel, 16 * count * count * width, grid=(steps,), in...  20.5 us
  transfers between devices with their start and end apart: 47, of which 12 were waited for; matrix products, arithmetic and copies ran while one was open for 15% of the time, Pallas kernels for 19%

profile of v2, /device:TPU:0, one launch (start us, length us, event | category | flops | bytes accessed | tf_op | source)
XLA Modules:
  0.0 557.9 jit_solution(4342364321346963050)
XLA Ops:
  11.6 5.0 collective-permute-start
  18.5 3.7 all-to-all-start
  22.4 4.4 all-to-all-done
  28.1 22.0 %collective-permute-done.1 = bf16[32,4096]{1,0:T(8,128)(2,1)S(1)} collective-permute-done((bf16[32,4096]{1,0:T(8,128)(2,1)S(1)}, bf16[32,4096]{1,0:T(8,128)(2,1)S(1)}, u32[]{:S(2)}, u32[]{:S(2)}) %collective-permute-start.1) | collective-permute-done | bytes 262176 | tf_op jit(solution)/shard_map/ppermute | solution.py:400
  55.0 2.7 constant_dynamic-slice_fusion.16
  58.8 4.1 all-to-all-start.1
  69.1 15.0 %all-to-all-done.1 = f32[32,1,3520]{2,1,0:T(1,128)S(1)} async-done(((f32[32,1,3520]{2,1,0:T(1,128)}), f32[32,1,3520]{2,1,0:T(1,128)S(1)}, u32[]{:S(2)}, u32[]{:S(2)}) %all-to-all-start.1) | async-done | bytes 450592 | tf_op jit(solution)/shard_map/all_to_all | solution.py:519
  84.2 12.3 %collective-permute-done.4 = bf16[256,1024]{1,0:T(8,128)(2,1)S(1)} collective-permute-done((bf16[256,1024]{1,0:T(8,128)(2,1)S(1)}, bf16[256,1024]{1,0:T(8,128)(2,1)S(1)}, u32[]{:S(2)}, u32[]{:S(2)}) %collective-permute-start.4) | collective-permute-done | bytes 524320 | tf_op jit(solution)/shard_map/ppermute | solution.py:346
  96.5 11.9 %collective-permute-start.5 = (f32[3072]{0:T(1024)S(1)}, f32[3072]{0:T(1024)S(1)}, u32[]{:S(2)}, u32[]{:S(2)}) collective-permute-start(f32[3072]{0:T(1024)S(1)} %slice_reduce_fusion), channel_id=1, source_target_pairs={{0,4},{4,0},{8,12},{12,8},{16,20},{20,16},{24,28},{28,24},{1,5},{5... | collective-permute-start | bytes 36872 | tf_op jit(solution)/shard_map/ppermute | solution.py:368
  110.2 27.7 %collective-permute-done.8 = bf16[128,4096]{1,0:T(8,128)(2,1)} collective-permute-done((bf16[128,4096]{1,0:T(8,128)(2,1)}, bf16[128,4096]{1,0:T(8,128)(2,1)}, u32[]{:S(2)}, u32[]{:S(2)}) %collective-permute-start.8) | collective-permute-done | bytes 1048608 | tf_op jit(solution)/shard_map/ppermute | solution.py:368
  137.9 2.4 constant_dynamic-update-slice_fusion.14
  140.2 2.3 constant_dynamic-update-slice_fusion.13
  142.5 2.3 constant_dynamic-update-slice_fusion.12
  144.8 2.3 constant_dynamic-update-slice_fusion.11.low_ref.weight_ref
  149.4 6.3 %collective-permute-done.9.high_ref.weight_ref = bf16[512,4096]{1,0:T(8,128)(2,1)} collective-permute-done((bf16[512,4096]{1,0:T(8,128)(2,1)}, bf16[512,4096]{1,0:T(8,128)(2,1)}, u32[]{:S(2)}, u32[]{:S(2)}) %collective-permute-start.9) | collective-permute-done | bytes 4194336 | tf_op jit(solution)/shard_map/ppermute | solution.py:368
  155.7 2.7 shard_map.247.refs_0_
  158.9 2.7 shard_map.248.refs_2_
  165.0 2.8 shard_map.246.q_ref
  168.9 5.5 collective-permute-start.12
  175.9 20.5 %shard_map.249 = (bf16[512,1024]{1,0:T(8,128)(2,1)S(1)}, f32[16,1,512]{2,1,0:T(1,128)S(1)}) custom-call(bf16[512,1024]{1,0:T(8,128)(2,1)S(1)} %shard_map.246.q_ref, bf16[512,1024]{1,0:T(8,128)(2,1)S(1)} %shard_map.247.refs_0_, bf16[512,1024]{1,0:T(8,128)(2,1)} %collective-permute-done.10.refs_1_, bf16[512,1024]{1,0:T(8,128)(2,1)S(1)} %shard_map.248.refs_2_, ...), custom_call_target="tpu_custom_call" | custom-call | flops 85899344 | bytes 429496 | tf_op jit(solution)/shard_map/pallas_call | solution.py:134
  198.2 2.9 shard_map.250
  206.3 19.2 %shard_map.251 = (bf16[512,4096]{1,0:T(8,128)(2,1)}, bf16[512,4096]{1,0:T(8,128)(2,1)}, f32[512,1024]{1,0:T(8,128)S(1)}) custom-call(bf16[512,1024]{1,0:T(8,128)(2,1)S(1)} %copy-done.5, bf16[32,256,1024]{2,1,0:T(8,128)(2,1)} %bitcast.157, bf16[32,256,1024]{2,1,0:T(8,128)(2,1)} %bitcast.158, f32[1,4096]{1,0:T(1,128)S(1)} %bitcast.155, ...), custom_call_target="tpu_custom_call" | custom-call | flops 171798688 | bytes 858993 | tf_op jit(solution)/shard_map/pallas_call | solution.py:231
  225.5 3.7 convert_reduce_fusion.2
  230.1 4.4 convolution_convert_fusion.1
  236.8 15.6 %shard_map.252 = (bf16[512,4096]{1,0:T(8,128)(2,1)}, f32[1,4096]{1,0:T(1,128)S(1)}, f32[512,1024]{1,0:T(8,128)S(1)}) custom-call(bf16[512,1024]{1,0:T(8,128)(2,1)S(1)} %copy-done.7, bf16[32,256,1024]{2,1,0:T(8,128)(2,1)} %bitcast.159, bf16[32,256,1024]{2,1,0:T(8,128)(2,1)} %bitcast.160, bf16[512,4096]{1,0:T(8,128)(2,1)} %get-tuple-element.138.slope_ref), custom_call_target="tpu_custom_call" | custom-call | flops 171798688 | bytes 858993 | tf_op jit(solution)/shard_map/pallas_call | solution.py:270
  252.5 3.9 add_convert_fusion.4
  256.4 3.1 add_convert_fusion.3
  259.5 3.3 add_convert_fusion.2
  262.8 4.4 convolution_convert_fusion
  273.5 2.2 fusion.145
  280.8 2.4 multiply_reduce_fusion
  284.0 2.4 convert_reduce_fusion.3
  286.5 2.4 convolution_convert_fusion.4
  295.2 3.1 fusion.4
  298.2 3.0 fusion.5
  301.3 3.1 fusion.6
  304.4 2.2 collective-permute-start.16
  307.3 2.2 fusion.59
  309.5 18.0 %shard_map.253 = (bf16[3,512,1024]{2,1,0:T(8,128)(2,1)}, bf16[2,512,1024]{2,1,0:T(8,128)(2,1)}) custom-call(bf16[512,1024]{1,0:T(8,128)(2,1)S(1)} %shard_map.246.q_ref, bf16[512,1024]{1,0:T(8,128)(2,1)S(1)} %copy-done.13, f32[16,1,512]{2,1,0:T(1,128)S(1)} %get-tuple-element.150.log_ref, bf16[512,1024]{1,0:T(8,128)(2,1)S(1)} %shard_map.247.refs_0_, ...), custom_call_target="tpu_custom_call" | custom-call | flops 107374184 | bytes 536870 | tf_op jit(solution)/shard_map/pallas_call | solution.py:190
  327.5 4.2 add_convert_fusion.1
  331.7 4.2 all-to-all-start.2
  337.3 2.3 collective-permute-start.24
  340.7 17.8 %shard_map.254 = (bf16[3,512,1024]{2,1,0:T(8,128)(2,1)}, bf16[2,512,1024]{2,1,0:T(8,128)(2,1)}) custom-call(bf16[512,1024]{1,0:T(8,128)(2,1)S(1)} %shard_map.246.q_ref, bf16[512,1024]{1,0:T(8,128)(2,1)S(1)} %copy-done.14, f32[16,1,512]{2,1,0:T(1,128)S(1)} %get-tuple-element.150.log_ref, ...), custom_call_target="tpu_custom_call", output_to_operand_aliasing={{0}: (7, {}), {1}: (8, {})} | custom-call | flops 107374184 | bytes 536870 | tf_op jit(solution)/shard_map/pallas_call | solution.py:190
  366.9 17.7 %collective-permute-done.23 = bf16[128,4096]{1,0:T(8,128)(2,1)} collective-permute-done((bf16[128,4096]{1,0:T(8,128)(2,1)}, bf16[128,4096]{1,0:T(8,128)(2,1)}, u32[]{:S(2)}, u32[]{:S(2)}) %collective-permute-start.23) | collective-permute-done | bytes 1048608 | tf_op jit(solution)/shard_map/ppermute | solution.py:368
  384.6 5.8 %fusion.3 = bf16[128,4096]{1,0:T(8,128)(2,1)} fusion(bf16[512,4096]{1,0:T(8,128)(2,1)} %get-tuple-element.143, bf16[128,4096]{1,0:T(8,128)(2,1)} %collective-permute-done.24, bf16[128,4096]{1,0:T(8,128)(2,1)} %collective-permute-done.23, bf16[128,4096]{1,0:T(8,128)(2,1)} %collective-permute-done.22, bf16[512,4096]{1,0:T(8,128)(2,1)} %collective-permute-done.15, ...), kind=kOutput, calls=%fused_computation.25 | convolution fusion | flops 541589504 | bytes 9568260 | tf_op jit(solution)/shard_map/dot_general | solution.py:29
  390.5 4.1 collective-permute-done.25
  396.8 3.6 convert_bitcast_fusion
  400.6 4.9 all-to-all-start.3
  411.4 20.5 %all-to-all-done.3 = bf16[4,32,4096]{2,1,0:T(8,128)(2,1)} async-done(((bf16[4,32,4096]{2,1,0:T(8,128)(2,1)}), bf16[4,32,4096]{2,1,0:T(8,128)(2,1)}, u32[]{:S(2)}, u32[]{:S(2)}) %all-to-all-start.3) | async-done | bytes 1048608 | tf_op jit(solution)/shard_map/all_to_all | solution.py:449
  435.0 3.7 shard_map.255
  438.7 2.9 fusion.33
  441.6 2.8 fusion.32
  444.4 2.9 fusion.31
  447.3 2.3 fusion.37
  449.6 3.5 shard_map.256
  457.8 3.1 fusion.19
  460.9 3.4 all-to-all-start.5
  465.5 5.3 collective-permute-start.31
  477.5 3.6 all-to-all-start.4
  483.9 30.3 %all-to-all-done.4 = f32[32,1,3328]{2,1,0:T(1,128)} async-done(((f32[32,1,3328]{2,1,0:T(1,128)}), f32[32,1,3328]{2,1,0:T(1,128)}, u32[]{:S(2)}, u32[]{:S(2)}) %all-to-all-start.4) | async-done | bytes 426016 | tf_op jit(solution)/shard_map/all_to_all | solution.py:643
  515.4 3.9 fusion.30
  520.5 4.0 all-to-all-start.6
  525.7 3.7 collective-permute-start.38
  539.8 10.2 %collective-permute-done.37 = bf16[3,32,1024]{2,1,0:T(8,128)(2,1)S(1)} collective-permute-done((bf16[3,32,1024]{2,1,0:T(8,128)(2,1)S(1)}, bf16[3,32,1024]{2,1,0:T(8,128)(2,1)S(1)}, u32[]{:S(2)}, u32[]{:S(2)}) %collective-permute-start.37) | collective-permute-done | bytes 196640 | tf_op jit(solution)/shard_map/ppermute | solution.py:467
  (347 shorter events, 106.2 us)
Async XLA Ops:
  7.2 10.5 %copy-start.56 = (bf16[2,1024]{1,0:T(2,128)(2,1)S(1)}, bf16[2,1024]{1,0:T(2,128)(2,1)}, u32[]{:S(2)}) copy-start(bf16[2,1024]{1,0:T(2,128)(2,1)} %param.16) | copy-start | bytes 12292
  7.2 15.0 %copy-start.57 = (bf16[192]{0:T(256)(128)(2,1)S(1)}, bf16[192]{0:T(256)(128)(2,1)}, u32[]{:S(2)}) copy-start(bf16[192]{0:T(256)(128)(2,1)} %param.23) | copy-start | bytes 1156
  7.2 15.0 %copy-start.58 = (bf16[64]{0:T(256)(128)(2,1)S(1)}, bf16[64]{0:T(256)(128)(2,1)}, u32[]{:S(2)}) copy-start(bf16[64]{0:T(256)(128)(2,1)} %param.24) | copy-start | bytes 388
  7.2 15.0 %copy-start.59 = (bf16[32]{0:T(256)(128)(2,1)S(1)}, bf16[32]{0:T(256)(128)(2,1)}, u32[]{:S(2)}) copy-start(bf16[32]{0:T(256)(128)(2,1)} %param.25) | copy-start | bytes 196
  7.2 15.0 %copy-start.60 = (bf16[128]{0:T(256)(128)(2,1)S(1)}, bf16[128]{0:T(256)(128)(2,1)}, u32[]{:S(2)}) copy-start(bf16[128]{0:T(256)(128)(2,1)} %param.26) | copy-start | bytes 772
  7.3 15.0 %copy-start.61 = (bf16[32]{0:T(256)(128)(2,1)S(1)}, bf16[32]{0:T(256)(128)(2,1)}, u32[]{:S(2)}) copy-start(bf16[32]{0:T(256)(128)(2,1)} %param.27) | copy-start | bytes 196
  7.3 19.7 %copy-start.42 = (bf16[32,6144]{1,0:T(8,128)(2,1)S(1)}, bf16[32,6144]{1,0:T(8,128)(2,1)}, u32[]{:S(2)}) copy-start(bf16[32,6144]{1,0:T(8,128)(2,1)} %param.18) | copy-start | bytes 1179652
  7.3 197.8 %all-gather.3.cloned.1.call-start = ((), (), s32[]{:S(2)}) async-start(), calls=%async_computation.7 | async-start | bytes 17301504 | tf_op jit(solution)/shard_map/all_gather | solution.py:289
  11.6 15.7 %collective-permute-start = (bf16[32,4096]{1,0:T(8,128)(2,1)S(1)}, bf16[32,4096]{1,0:T(8,128)(2,1)S(1)}, u32[]{:S(2)}, u32[]{:S(2)}) collective-permute-start(bf16[32,4096]{1,0:T(8,128)(2,1)S(1)} %get-tuple-element.356), channel_id=1, source_target_pairs={{0,3},{1,0},{2,1},{3,2},{4,7},{5,4},{6,5},{7,6},{8,11},{9,8},{10,9... | collective-permute-start | bytes 786440 | tf_op jit(solution)/shard_map/ppermute | solution.py:400
  16.7 33.4 %collective-permute-start.1 = (bf16[32,4096]{1,0:T(8,128)(2,1)S(1)}, bf16[32,4096]{1,0:T(8,128)(2,1)S(1)}, u32[]{:S(2)}, u32[]{:S(2)}) collective-permute-start(bf16[32,4096]{1,0:T(8,128)(2,1)S(1)} %get-tuple-element.356), channel_id=1, source_target_pairs={{0,2},{1,3},{2,0},{3,1},{4,6},{5,7},{6,4},{7,5},{8,10},{9,11},{10,... | collective-permute-start | bytes 786440 | tf_op jit(solution)/shard_map/ppermute | solution.py:400
  16.7 34.1 %collective-permute-start.2 = (bf16[32,4096]{1,0:T(8,128)(2,1)S(1)}, bf16[32,4096]{1,0:T(8,128)(2,1)S(1)}, u32[]{:S(2)}, u32[]{:S(2)}) collective-permute-start(bf16[32,4096]{1,0:T(8,128)(2,1)S(1)} %get-tuple-element.356), channel_id=1, source_target_pairs={{0,1},{1,2},{2,3},{3,0},{4,5},{5,6},{6,7},{7,4},{8,9},{9,10},{10,1... | collective-permute-start | bytes 786440 | tf_op jit(solution)/shard_map/ppermute | solution.py:400
  18.5 8.3 %all-to-all-start = ((bf16[8,1,64]{2,1,0:T(2,128)(2,1)}), bf16[8,1,64]{2,1,0:T(2,128)(2,1)S(1)}, u32[]{:S(2)}, u32[]{:S(2)}) async-start(bf16[8,1,64]{2,1,0:T(2,128)(2,1)} %all_to_all.62), calls=%async_computation | async-start | bytes 8192 | tf_op jit(solution)/shard_map/all_to_all | solution.py:510
  55.0 7.9 %copy-start.44 = (bf16[2,256,1024]{2,1,0:T(8,128)(2,1)S(1)}, bf16[2,256,1024]{2,1,0:T(8,128)(2,1)}, u32[]{:S(2)}) copy-start(bf16[2,256,1024]{2,1,0:T(8,128)(2,1)} %param.15) | copy-start | bytes 3145732
  58.8 25.3 %all-to-all-start.1 = ((f32[32,1,3520]{2,1,0:T(1,128)}), f32[32,1,3520]{2,1,0:T(1,128)S(1)}, u32[]{:S(2)}, u32[]{:S(2)}) async-start(f32[32,1,3520]{2,1,0:T(1,128)} %all_to_all.48), calls=%async_computation.1 | async-start | bytes 917504 | tf_op jit(solution)/shard_map/all_to_all | solution.py:519
  63.0 21.1 %collective-permute-start.3 = (bf16[256,1024]{1,0:T(8,128)(2,1)S(1)}, bf16[256,1024]{1,0:T(8,128)(2,1)S(1)}, u32[]{:S(2)}, u32[]{:S(2)}) collective-permute-start(bf16[256,1024]{1,0:T(8,128)(2,1)S(1)} %get-tuple-element.342), channel_id=1, source_target_pairs={{0,0},{1,1},{2,4},{3,5},{4,2},{5,3},{6,6},{7,7},{8,8},{9,9},{10,12... | collective-permute-start | bytes 1572872 | tf_op jit(solution)/shard_map/ppermute | solution.py:346
  63.7 32.7 %collective-permute-start.4 = (bf16[256,1024]{1,0:T(8,128)(2,1)S(1)}, bf16[256,1024]{1,0:T(8,128)(2,1)S(1)}, u32[]{:S(2)}, u32[]{:S(2)}) collective-permute-start(bf16[256,1024]{1,0:T(8,128)(2,1)S(1)} %get-tuple-element.341), channel_id=1, source_target_pairs={{0,1},{1,0},{2,5},{3,4},{4,3},{5,2},{6,7},{7,6},{8,9},{9,8},{10,13... | collective-permute-start | bytes 1572872 | tf_op jit(solution)/shard_map/ppermute | solution.py:346
  65.6 44.6 %collective-permute-start.6 = (bf16[128,4096]{1,0:T(8,128)(2,1)}, bf16[128,4096]{1,0:T(8,128)(2,1)}, u32[]{:S(2)}, u32[]{:S(2)}) collective-permute-start(bf16[128,4096]{1,0:T(8,128)(2,1)} %constant_dynamic-slice_fusion.16), channel_id=1, source_target_pairs={{0,8},{4,12},{8,0},{12,4},{16,24},{20,28},{24,16},{28,20},{1,9},{5... | collective-permute-start | bytes 3145736 | tf_op jit(solution)/shard_map/ppermute | solution.py:368
  67.0 43.1 %collective-permute-start.7 = (bf16[128,4096]{1,0:T(8,128)(2,1)}, bf16[128,4096]{1,0:T(8,128)(2,1)}, u32[]{:S(2)}, u32[]{:S(2)}) collective-permute-start(bf16[128,4096]{1,0:T(8,128)(2,1)} %constant_dynamic-slice_fusion.16), channel_id=1, source_target_pairs={{0,16},{4,20},{8,24},{12,28},{16,0},{20,4},{24,8},{28,12},{1,17},{... | collective-permute-start | bytes 3145736 | tf_op jit(solution)/shard_map/ppermute | solution.py:368
  68.5 69.4 %collective-permute-start.8 = (bf16[128,4096]{1,0:T(8,128)(2,1)}, bf16[128,4096]{1,0:T(8,128)(2,1)}, u32[]{:S(2)}, u32[]{:S(2)}) collective-permute-start(bf16[128,4096]{1,0:T(8,128)(2,1)} %constant_dynamic-slice_fusion.16), channel_id=1, source_target_pairs={{0,24},{4,28},{8,16},{12,20},{16,8},{20,12},{24,0},{28,4},{1,25},{... | collective-permute-start | bytes 3145736 | tf_op jit(solution)/shard_map/ppermute | solution.py:368
  84.1 24.8 %copy-start.40 = (f32[32,1,3520]{2,0,1:T(8,128)}, f32[32,1,3520]{2,0,1:T(8,128)S(1)}, u32[]{:S(2)}) copy-start(f32[32,1,3520]{2,0,1:T(8,128)S(1)} %copy.168) | copy-start | bytes 1351684
  84.2 25.5 %copy-start.24 = (bf16[256,1024]{1,0:T(8,128)(2,1)}, bf16[256,1024]{1,0:T(8,128)(2,1)S(1)}, u32[]{:S(2)}) copy-start(bf16[256,1024]{1,0:T(8,128)(2,1)S(1)} %collective-permute-done.3) | copy-start | bytes 1572868
  96.4 13.2 %copy-start.27 = (bf16[256,1024]{1,0:T(8,128)(2,1)}, bf16[256,1024]{1,0:T(8,128)(2,1)S(1)}, u32[]{:S(2)}) copy-start(bf16[256,1024]{1,0:T(8,128)(2,1)S(1)} %collective-permute-done.4) | copy-start | bytes 1572868
  96.5 12.7 %collective-permute-start.5 = (f32[3072]{0:T(1024)S(1)}, f32[3072]{0:T(1024)S(1)}, u32[]{:S(2)}, u32[]{:S(2)}) collective-permute-start(f32[3072]{0:T(1024)S(1)} %slice_reduce_fusion), channel_id=1, source_target_pairs={{0,4},{4,0},{8,12},{12,8},{16,20},{20,16},{24,28},{28,24},{1,5},{5... | collective-permute-start | bytes 36872 | tf_op jit(solution)/shard_map/ppermute | solution.py:368
  110.1 48.7 %copy-start.2 = (bf16[512,1024]{1,0:T(8,128)(2,1)}, bf16[512,1024]{1,0:T(8,128)(2,1)S(1)}, u32[]{:S(2)}) copy-start(bf16[512,1024]{1,0:T(8,128)(2,1)S(1)} %dynamic-slice_dynamic-update-slice_fusion.x_ref) | copy-start | bytes 3145732
  147.1 8.6 %collective-permute-start.9 = (bf16[512,4096]{1,0:T(8,128)(2,1)}, bf16[512,4096]{1,0:T(8,128)(2,1)}, u32[]{:S(2)}, u32[]{:S(2)}) collective-permute-start(bf16[512,4096]{1,0:T(8,128)(2,1)} %constant_dynamic-update-slice_fusion.11.low_ref.weight_ref), channel_id=1, source_target_pairs={{0,4},{4,0},{8,12},{12,8},{16,20},{20,16},{24,28},{28,24},{1,5},{5... | collective-permute-start | bytes 12582920 | tf_op jit(solution)/shard_map/ppermute | solution.py:368
  158.5 17.4 %collective-permute-start.10 = (bf16[512,1024]{1,0:T(8,128)(2,1)S(1)}, bf16[512,1024]{1,0:T(8,128)(2,1)}, u32[]{:S(2)}, u32[]{:S(2)}) collective-permute-start(bf16[512,1024]{1,0:T(8,128)(2,1)S(1)} %shard_map.247.refs_0_), channel_id=1, source_target_pairs={{0,4},{4,0},{8,12},{12,8},{16,20},{20,16},{24,28},{28,24},{1,5},{5... | collective-permute-start | bytes 3145736 | tf_op jit(solution)/shard_map/ppermute | solution.py:368
  161.6 14.2 %collective-permute-start.11 = (bf16[512,1024]{1,0:T(8,128)(2,1)S(1)}, bf16[512,1024]{1,0:T(8,128)(2,1)}, u32[]{:S(2)}, u32[]{:S(2)}) collective-permute-start(bf16[512,1024]{1,0:T(8,128)(2,1)S(1)} %shard_map.248.refs_2_), channel_id=1, source_target_pairs={{0,4},{4,0},{8,12},{12,8},{16,20},{20,16},{24,28},{28,24},{1,5},{5... | collective-permute-start | bytes 3145736 | tf_op jit(solution)/shard_map/ppermute | solution.py:368
  168.9 56.6 %collective-permute-start.12 = (bf16[256,1024]{1,0:T(8,128)(2,1)}, bf16[256,1024]{1,0:T(8,128)(2,1)}, u32[]{:S(2)}, u32[]{:S(2)}) collective-permute-start(bf16[256,1024]{1,0:T(8,128)(2,1)} %get-tuple-element.340), channel_id=1, source_target_pairs={{0,0},{1,1},{2,4},{3,5},{4,2},{5,3},{6,6},{7,7},{8,8},{9,9},{10,12... | collective-permute-start | bytes 1572872 | tf_op jit(solution)/shard_map/ppermute | solution.py:346
  174.4 51.1 %collective-permute-start.13 = (bf16[256,1024]{1,0:T(8,128)(2,1)}, bf16[256,1024]{1,0:T(8,128)(2,1)}, u32[]{:S(2)}, u32[]{:S(2)}) collective-permute-start(bf16[256,1024]{1,0:T(8,128)(2,1)} %get-tuple-element.339), channel_id=1, source_target_pairs={{0,1},{1,0},{2,5},{3,4},{4,3},{5,2},{6,7},{7,6},{8,9},{9,8},{10,13... | collective-permute-start | bytes 1572872 | tf_op jit(solution)/shard_map/ppermute | solution.py:346
  206.3 19.2 %copy-start.19 = (f32[512,1024]{1,0:T(8,128)S(1)}, f32[512,1024]{1,0:T(8,128)}, u32[]{:S(2)}) copy-start(f32[512,1024]{1,0:T(8,128)} %copy-done.18) | copy-start | bytes 6291460
  234.4 18.0 %collective-permute-start.14 = (bf16[2048,1024]{1,0:T(8,128)(2,1)}, bf16[2048,1024]{1,0:T(8,128)(2,1)}, u32[]{:S(2)}, u32[]{:S(2)}) collective-permute-start(bf16[2048,1024]{1,0:T(8,128)(2,1)} %convolution_convert_fusion.1), channel_id=1, source_target_pairs={{0,4},{4,0},{8,12},{12,8},{16,20},{20,16},{24,28},{28,24},{1,5},{5... | collective-permute-start | bytes 12582920 | tf_op jit(solution)/shard_map/ppermute | solution.py:368
  267.2 27.2 %collective-permute-start.15 = (bf16[512,4096]{1,0:T(8,128)(2,1)}, bf16[512,4096]{1,0:T(8,128)(2,1)}, u32[]{:S(2)}, u32[]{:S(2)}) collective-permute-start(bf16[512,4096]{1,0:T(8,128)(2,1)} %convolution_convert_fusion), channel_id=1, source_target_pairs={{0,4},{4,0},{8,12},{12,8},{16,20},{20,16},{24,28},{28,24},{1,5},{5... | collective-permute-start | bytes 12582920 | tf_op jit(solution)/shard_map/ppermute | solution.py:368
  275.7 7.6 %copy-start.20 = (f32[512,1024]{1,0:T(8,128)S(1)}, f32[512,1024]{1,0:T(8,128)}, u32[]{:S(2)}) copy-start(f32[512,1024]{1,0:T(8,128)} %copy-done.18) | copy-start | bytes 6291460
  275.7 30.9 %collective-permute-start.20 = (bf16[256,1024]{1,0:T(8,128)(2,1)S(1)}, bf16[256,1024]{1,0:T(8,128)(2,1)}, u32[]{:S(2)}, u32[]{:S(2)}) collective-permute-start(bf16[256,1024]{1,0:T(8,128)(2,1)S(1)} %get-tuple-element.334), channel_id=1, source_target_pairs={{0,0},{1,1},{4,2},{5,3},{2,4},{3,5},{6,6},{7,7},{8,8},{9,9},{12,10... | collective-permute-start | bytes 1572872 | tf_op jit(solution)/shard_map/ppermute | solution.py:354
  277.3 50.1 %collective-permute-start.17 = (bf16[512,1024]{1,0:T(8,128)(2,1)}, bf16[512,1024]{1,0:T(8,128)(2,1)}, u32[]{:S(2)}, u32[]{:S(2)}) collective-permute-start(bf16[512,1024]{1,0:T(8,128)(2,1)} %add_convert_fusion.4), channel_id=1, source_target_pairs={{0,8},{4,12},{8,0},{12,4},{16,24},{20,28},{24,16},{28,20},{1,9},{5... | collective-permute-start | bytes 3145736 | tf_op jit(solution)/shard_map/ppermute | solution.py:368
  278.3 49.1 %collective-permute-start.18 = (bf16[512,1024]{1,0:T(8,128)(2,1)}, bf16[512,1024]{1,0:T(8,128)(2,1)}, u32[]{:S(2)}, u32[]{:S(2)}) collective-permute-start(bf16[512,1024]{1,0:T(8,128)(2,1)} %add_convert_fusion.3), channel_id=1, source_target_pairs={{0,16},{4,20},{8,24},{12,28},{16,0},{20,4},{24,8},{28,12},{1,17},{... | collective-permute-start | bytes 3145736 | tf_op jit(solution)/shard_map/ppermute | solution.py:368
  279.1 48.4 %collective-permute-start.19 = (bf16[512,1024]{1,0:T(8,128)(2,1)}, bf16[512,1024]{1,0:T(8,128)(2,1)}, u32[]{:S(2)}, u32[]{:S(2)}) collective-permute-start(bf16[512,1024]{1,0:T(8,128)(2,1)} %add_convert_fusion.2), channel_id=1, source_target_pairs={{0,24},{4,28},{8,16},{12,20},{16,8},{20,12},{24,0},{28,4},{1,25},{... | collective-permute-start | bytes 3145736 | tf_op jit(solution)/shard_map/ppermute | solution.py:368
  304.4 23.1 %collective-permute-start.16 = (bf16[512,1024]{1,0:T(8,128)(2,1)}, bf16[512,1024]{1,0:T(8,128)(2,1)}, u32[]{:S(2)}, u32[]{:S(2)}) collective-permute-start(bf16[512,1024]{1,0:T(8,128)(2,1)} %convolution_convert_fusion.2), channel_id=1, source_target_pairs={{0,4},{4,0},{8,12},{12,8},{16,20},{20,16},{24,28},{28,24},{1,5},{5... | collective-permute-start | bytes 3145736 | tf_op jit(solution)/shard_map/ppermute | solution.py:368
  306.6 20.9 %collective-permute-start.21 = (bf16[256,1024]{1,0:T(8,128)(2,1)}, bf16[256,1024]{1,0:T(8,128)(2,1)}, u32[]{:S(2)}, u32[]{:S(2)}) collective-permute-start(bf16[256,1024]{1,0:T(8,128)(2,1)} %get-tuple-element.333), channel_id=1, source_target_pairs={{1,0},{0,1},{5,2},{4,3},{3,4},{2,5},{7,6},{6,7},{9,8},{8,9},{13,10... | collective-permute-start | bytes 1572872 | tf_op jit(solution)/shard_map/ppermute | solution.py:354
  331.7 33.1 %all-to-all-start.2 = ((bf16[4,128,1024]{2,1,0:T(8,128)(2,1)}), bf16[4,128,1024]{2,1,0:T(8,128)(2,1)}, u32[]{:S(2)}, u32[]{:S(2)}) async-start(bf16[4,128,1024]{2,1,0:T(8,128)(2,1)} %bitcast.162), calls=%async_computation.2 | async-start | bytes 2097152 | tf_op jit(solution)/shard_map/all_to_all | solution.py:449
  336.0 30.9 %collective-permute-start.22 = (bf16[128,4096]{1,0:T(8,128)(2,1)}, bf16[128,4096]{1,0:T(8,128)(2,1)}, u32[]{:S(2)}, u32[]{:S(2)}) collective-permute-start(bf16[128,4096]{1,0:T(8,128)(2,1)} %fusion.4), channel_id=1, source_target_pairs={{0,8},{4,12},{8,0},{12,4},{16,24},{20,28},{24,16},{28,20},{1,9},{5... | collective-permute-start | bytes 3145736 | tf_op jit(solution)/shard_map/ppermute | solution.py:368
  336.7 47.9 %collective-permute-start.23 = (bf16[128,4096]{1,0:T(8,128)(2,1)}, bf16[128,4096]{1,0:T(8,128)(2,1)}, u32[]{:S(2)}, u32[]{:S(2)}) collective-permute-start(bf16[128,4096]{1,0:T(8,128)(2,1)} %fusion.5), channel_id=1, source_target_pairs={{0,16},{4,20},{8,24},{12,28},{16,0},{20,4},{24,8},{28,12},{1,17},{... | collective-permute-start | bytes 3145736 | tf_op jit(solution)/shard_map/ppermute | solution.py:368
  337.3 47.3 %collective-permute-start.24 = (bf16[128,4096]{1,0:T(8,128)(2,1)}, bf16[128,4096]{1,0:T(8,128)(2,1)}, u32[]{:S(2)}, u32[]{:S(2)}) collective-permute-start(bf16[128,4096]{1,0:T(8,128)(2,1)} %fusion.6), channel_id=1, source_target_pairs={{0,24},{4,28},{8,16},{12,20},{16,8},{20,12},{24,0},{28,4},{1,25},{... | collective-permute-start | bytes 3145736 | tf_op jit(solution)/shard_map/ppermute | solution.py:368
  340.7 17.8 %copy-start.22 = (bf16[512,1024]{1,0:T(8,128)(2,1)S(1)}, bf16[512,1024]{1,0:T(8,128)(2,1)}, u32[]{:S(2)}) copy-start(bf16[512,1024]{1,0:T(8,128)(2,1)} %copy-done.21) | copy-start | bytes 3145732
  390.4 4.2 collective-permute-start.25
  400.5 38.2 %collective-permute-start.26 = (bf16[3,512,1024]{2,1,0:T(8,128)(2,1)}, bf16[3,512,1024]{2,1,0:T(8,128)(2,1)}, u32[]{:S(2)}, u32[]{:S(2)}) collective-permute-start(bf16[3,512,1024]{2,1,0:T(8,128)(2,1)} %convert_bitcast_fusion), channel_id=1, source_target_pairs={{0,4},{4,0},{8,12},{12,8},{16,20},{20,16},{24,28},{28,24},{1,5},{5... | collective-permute-start | bytes 9437192 | tf_op jit(solution)/shard_map/ppermute | solution.py:368
  400.6 31.3 %all-to-all-start.3 = ((bf16[4,32,4096]{2,1,0:T(8,128)(2,1)}), bf16[4,32,4096]{2,1,0:T(8,128)(2,1)}, u32[]{:S(2)}, u32[]{:S(2)}) async-start(bf16[4,32,4096]{2,1,0:T(8,128)(2,1)} %bitcast.161), calls=%async_computation.3 | async-start | bytes 2097152 | tf_op jit(solution)/shard_map/all_to_all | solution.py:449
  405.8 32.8 %collective-permute-start.27 = (bf16[128,1024]{1,0:T(8,128)(2,1)}, bf16[128,1024]{1,0:T(8,128)(2,1)}, u32[]{:S(2)}, u32[]{:S(2)}) collective-permute-start(bf16[128,1024]{1,0:T(8,128)(2,1)} %fusion.38), channel_id=1, source_target_pairs={{0,8},{4,12},{8,0},{12,4},{16,24},{20,28},{24,16},{28,20},{1,9},{5... | collective-permute-start | bytes 786440 | tf_op jit(solution)/shard_map/ppermute | solution.py:368
  407.2 31.5 %collective-permute-start.28 = (bf16[128,1024]{1,0:T(8,128)(2,1)}, bf16[128,1024]{1,0:T(8,128)(2,1)}, u32[]{:S(2)}, u32[]{:S(2)}) collective-permute-start(bf16[128,1024]{1,0:T(8,128)(2,1)} %fusion.39), channel_id=1, source_target_pairs={{0,16},{4,20},{8,24},{12,28},{16,0},{20,4},{24,8},{28,12},{1,17},{... | collective-permute-start | bytes 786440 | tf_op jit(solution)/shard_map/ppermute | solution.py:368
  407.8 30.9 %collective-permute-start.29 = (bf16[128,1024]{1,0:T(8,128)(2,1)}, bf16[128,1024]{1,0:T(8,128)(2,1)}, u32[]{:S(2)}, u32[]{:S(2)}) collective-permute-start(bf16[128,1024]{1,0:T(8,128)(2,1)} %fusion.40), channel_id=1, source_target_pairs={{0,24},{4,28},{8,16},{12,20},{16,8},{20,12},{24,0},{28,4},{1,25},{... | collective-permute-start | bytes 786440 | tf_op jit(solution)/shard_map/ppermute | solution.py:368
  460.9 16.6 %all-to-all-start.5 = ((bf16[4,32,1024]{2,1,0:T(8,128)(2,1)}), bf16[4,32,1024]{2,1,0:T(8,128)(2,1)S(1)}, u32[]{:S(2)}, u32[]{:S(2)}) async-start(bf16[4,32,1024]{2,1,0:T(8,128)(2,1)} %bitcast.42), calls=%async_computation.5 | async-start | bytes 524288 | tf_op jit(solution)/shard_map/all_to_all | solution.py:449
  464.4 10.4 %collective-permute-start.30 = (f32[6144]{0:T(1024)S(1)}, f32[6144]{0:T(1024)S(1)}, u32[]{:S(2)}, u32[]{:S(2)}) collective-permute-start(f32[6144]{0:T(1024)S(1)} %constant_dynamic-update-slice_fusion.22), channel_id=1, source_target_pairs={{0,4},{4,0},{8,12},{12,8},{16,20},{20,16},{24,28},{28,24},{1,5},{5... | collective-permute-start | bytes 73736 | tf_op jit(solution)/shard_map/ppermute | solution.py:368
  465.5 49.8 %collective-permute-start.31 = (bf16[256,1024]{1,0:T(8,128)(2,1)}, bf16[256,1024]{1,0:T(8,128)(2,1)}, u32[]{:S(2)}, u32[]{:S(2)}) collective-permute-start(bf16[256,1024]{1,0:T(8,128)(2,1)} %get-tuple-element.322), channel_id=1, source_target_pairs={{0,0},{1,1},{4,2},{5,3},{2,4},{3,5},{6,6},{7,7},{8,8},{9,9},{12,10... | collective-permute-start | bytes 1572872 | tf_op jit(solution)/shard_map/ppermute | solution.py:354
  470.9 44.4 %collective-permute-start.32 = (bf16[256,1024]{1,0:T(8,128)(2,1)}, bf16[256,1024]{1,0:T(8,128)(2,1)}, u32[]{:S(2)}, u32[]{:S(2)}) collective-permute-start(bf16[256,1024]{1,0:T(8,128)(2,1)} %get-tuple-element.321), channel_id=1, source_target_pairs={{1,0},{0,1},{5,2},{4,3},{3,4},{2,5},{7,6},{6,7},{9,8},{8,9},{13,10... | collective-permute-start | bytes 1572872 | tf_op jit(solution)/shard_map/ppermute | solution.py:354
  472.8 42.5 %collective-permute-start.33 = (bf16[3,128,1024]{2,1,0:T(8,128)(2,1)}, bf16[3,128,1024]{2,1,0:T(8,128)(2,1)}, u32[]{:S(2)}, u32[]{:S(2)}) collective-permute-start(bf16[3,128,1024]{2,1,0:T(8,128)(2,1)} %fusion.33), channel_id=1, source_target_pairs={{0,8},{4,12},{8,0},{12,4},{16,24},{20,28},{24,16},{28,20},{1,9},{5... | collective-permute-start | bytes 2359304 | tf_op jit(solution)/shard_map/ppermute | solution.py:368
  474.2 41.2 %collective-permute-start.34 = (bf16[3,128,1024]{2,1,0:T(8,128)(2,1)}, bf16[3,128,1024]{2,1,0:T(8,128)(2,1)}, u32[]{:S(2)}, u32[]{:S(2)}) collective-permute-start(bf16[3,128,1024]{2,1,0:T(8,128)(2,1)} %fusion.32), channel_id=1, source_target_pairs={{0,16},{4,20},{8,24},{12,28},{16,0},{20,4},{24,8},{28,12},{1,17},{... | collective-permute-start | bytes 2359304 | tf_op jit(solution)/shard_map/ppermute | solution.py:368
  474.8 40.6 %collective-permute-start.35 = (bf16[3,128,1024]{2,1,0:T(8,128)(2,1)}, bf16[3,128,1024]{2,1,0:T(8,128)(2,1)}, u32[]{:S(2)}, u32[]{:S(2)}) collective-permute-start(bf16[3,128,1024]{2,1,0:T(8,128)(2,1)} %fusion.31), channel_id=1, source_target_pairs={{0,24},{4,28},{8,16},{12,20},{16,8},{20,12},{24,0},{28,4},{1,25},{... | collective-permute-start | bytes 2359304 | tf_op jit(solution)/shard_map/ppermute | solution.py:368
  477.5 37.9 %copy-start.35 = (bf16[2,512,1024]{2,1,0:T(8,128)(2,1)S(1)}, bf16[2,512,1024]{2,1,0:T(8,128)(2,1)}, u32[]{:S(2)}) copy-start(bf16[2,512,1024]{2,1,0:T(8,128)(2,1)} %copy-done.33) | copy-start | bytes 6291460
  477.5 37.9 %copy-start.38 = (bf16[1,512,1024]{2,1,0:T(8,128)(2,1)S(1)}, bf16[1,512,1024]{2,1,0:T(8,128)(2,1)}, u32[]{:S(2)}) copy-start(bf16[1,512,1024]{2,1,0:T(8,128)(2,1)} %copy-done.36) | copy-start | bytes 3145732
  477.5 36.8 %all-to-all-start.4 = ((f32[32,1,3328]{2,1,0:T(1,128)}), f32[32,1,3328]{2,1,0:T(1,128)}, u32[]{:S(2)}, u32[]{:S(2)}) async-start(f32[32,1,3328]{2,1,0:T(1,128)} %all_to_all.55), calls=%async_computation.4 | async-start | bytes 851968 | tf_op jit(solution)/shard_map/all_to_all | solution.py:643
  520.5 17.2 %all-to-all-start.6 = ((f32[32,1,64]{2,1,0:T(1,128)}), f32[32,1,64]{2,1,0:T(1,128)S(1)}, u32[]{:S(2)}, u32[]{:S(2)}) async-start(f32[32,1,64]{2,1,0:T(1,128)} %bitcast.52), calls=%async_computation.6 | async-start | bytes 32768 | tf_op jit(solution)/shard_map/all_to_all | solution.py:665
  525.7 14.0 %collective-permute-start.38 = (bf16[3,32,1024]{2,1,0:T(8,128)(2,1)S(1)}, bf16[3,32,1024]{2,1,0:T(8,128)(2,1)S(1)}, u32[]{:S(2)}, u32[]{:S(2)}) collective-permute-start(bf16[3,32,1024]{2,1,0:T(8,128)(2,1)S(1)} %get-tuple-element.344), channel_id=1, source_target_pairs={{0,3},{1,0},{2,1},{3,2},{4,7},{5,4},{6,5},{7,6},{8,11},{9,8},{10,9... | collective-permute-start | bytes 589832 | tf_op jit(solution)/shard_map/ppermute | solution.py:467
  536.0 14.0 %collective-permute-start.37 = (bf16[3,32,1024]{2,1,0:T(8,128)(2,1)S(1)}, bf16[3,32,1024]{2,1,0:T(8,128)(2,1)S(1)}, u32[]{:S(2)}, u32[]{:S(2)}) collective-permute-start(bf16[3,32,1024]{2,1,0:T(8,128)(2,1)S(1)} %get-tuple-element.345), channel_id=1, source_target_pairs={{0,2},{1,3},{2,0},{3,1},{4,6},{5,7},{6,4},{7,5},{8,10},{9,11},{10,... | collective-permute-start | bytes 589832 | tf_op jit(solution)/shard_map/ppermute | solution.py:467
  536.0 14.0 %collective-permute-start.36 = (bf16[3,32,1024]{2,1,0:T(8,128)(2,1)S(1)}, bf16[3,32,1024]{2,1,0:T(8,128)(2,1)S(1)}, u32[]{:S(2)}, u32[]{:S(2)}) collective-permute-start(bf16[3,32,1024]{2,1,0:T(8,128)(2,1)S(1)} %get-tuple-element.343), channel_id=1, source_target_pairs={{0,1},{1,2},{2,3},{3,0},{4,5},{5,6},{6,7},{7,4},{8,9},{9,10},{10,1... | collective-permute-start | bytes 589832 | tf_op jit(solution)/shard_map/ppermute | solution.py:467
  (45 other events, 124.9 us)
Sparse Core Ops, SparseCore 0:
  11.7 163.2 all-gather.2

commit v3 on v2

--- a/solution.py
+++ b/solution.py
@@ -53,56 +53,53 @@
     return lax.dot_general(left, right, (((1,), (1,)), ((), ())), preferred_element_type=f32)
 
 
-def project_kernel(x_ref, low_ref, high_ref, bias_ref, out_ref):
-    half = low_ref.shape[0]
-    total = jnp.dot(x_ref[:, :half], low_ref[...], preferred_element_type=f32)
-    total = total + jnp.dot(x_ref[:, half:], high_ref[...], preferred_element_type=f32)
+def project_kernel(x_ref, *refs):
+    parts, (bias_ref, out_ref) = refs[:-2], refs[-2:]
+    weight = jnp.concatenate([part[...] for part in parts], axis=0)
+    total = jnp.dot(x_ref[...], weight, preferred_element_type=f32)
     out_ref[...] = (total + bias_ref[...]).astype(out_ref.dtype)
 
 
-def project(x, weight, begin, columns, bias, dtype):
-    low, high = weight
+def project(x, parts, begin, columns, bias, dtype):
     rows, depth = x.shape
     tile = 512
     first = begin // tile
-    pick = lambda step: (0, first + step)
+    part_rows = depth // len(parts)
     return call(
         project_kernel,
         2 * rows * depth * columns,
         grid=(columns // tile,),
-        in_specs=[
-            pl.BlockSpec((rows, depth), lambda step: (0, 0)),
-            pl.BlockSpec((depth // 2, tile), pick),
-            pl.BlockSpec((depth // 2, tile), pick),
-            pl.BlockSpec((1, tile), lambda step: (0, step)),
-        ],
+        in_specs=[pl.BlockSpec((rows, depth), lambda step: (0, 0))]
+        + [pl.BlockSpec((part_rows, tile), lambda step: (0, first + step))] * len(parts)
+        + [pl.BlockSpec((1, tile), lambda step: (0, step))],
         out_specs=pl.BlockSpec((rows, tile), lambda step: (0, step)),
         out_shape=jax.ShapeDtypeStruct((rows, columns), dtype),
-    )(x, low, high, bias.reshape(1, -1))
-
-
-def unproject_kernel(rows_ref, weight_ref, out_ref):
-    width = rows_ref.shape[2]
-    total = transposed_dot(rows_ref[0], weight_ref[:, :width])
-    total = total + transposed_dot(rows_ref[1], weight_ref[:, width : 2 * width])
-    out_ref[...] = total + transposed_dot(rows_ref[2], weight_ref[:, 2 * width :])
-
-
-def unproject(rows, weight):
-    _, count, width = rows.shape
-    depth = weight.shape[0]
-    tile = 256
+    )(x, *parts, bias.reshape(1, -1))
+
+
+def unproject_kernel(rows_ref, *refs):
+    parts, out_ref = refs[:-1], refs[-1]
+    weight = jnp.concatenate([part[...] for part in parts], axis=0)
+
+    @pl.when(pl.program_id(0) == 0)
+    def _():
+        out_ref[...] = jnp.zeros(out_ref.shape, f32)
+
+    out_ref[...] += transposed_dot(rows_ref[0], weight)
+
+
+def unproject(rows, parts, first):
+    blocks, count, width = rows.shape
+    part_rows = width // len(parts)
     return call(
         unproject_kernel,
-        6 * count * depth * width,
-        grid=(depth // tile,),
-        in_specs=[
-            pl.BlockSpec((3, count, width), lambda step: (0, 0, 0)),
-            pl.BlockSpec((tile, 3 * width), lambda step: (step, 0)),
-        ],
-        out_specs=pl.BlockSpec((count, tile), lambda step: (0, step)),
-        out_shape=jax.ShapeDtypeStruct((count, depth), f32),
-    )(rows, weight)
+        2 * blocks * count * width * width,
+        grid=(blocks,),
+        in_specs=[pl.BlockSpec((1, count, width), lambda step: (step, 0, 0))]
+        + [pl.BlockSpec((part_rows, width), lambda step: (0, first + step))] * len(parts),
+        out_specs=pl.BlockSpec((count, width), lambda step: (0, 0)),
+        out_shape=jax.ShapeDtypeStruct((count, width), f32),
+    )(rows, *parts)
 
 
 def attend_forward_kernel(q_ref, *refs):
@@ -538,8 +535,7 @@
     normed = modulate(tokens, shift_a, scale_a).astype(bf16)
     normed_cols = at.arranged(normed)
     normed_cols, *near_parts = tied(normed_cols, *near_parts)
-    weight = jnp.concatenate(near_parts, axis=0)
-    weight = (weight, at.across(weight))
+    weight = near_parts + [at.across(part) for part in near_parts]
     key_own = project(normed_cols, weight, width, width, jnp.zeros((width,), f32), bf16)
     keys = (key_own, at.across(key_own))
     value_own = project(normed_cols, weight, 2 * width, width, b_qv[width:], bf16)
@@ -579,10 +575,7 @@
     grad_gate_a = jnp.sum(grad_middle * attn_out, axis=0)
     grad_attn = (gate_a * grad_middle).astype(bf16)
     grad_bproj = jnp.sum(grad_attn.astype(f32), axis=0)
-    grad_mixed = jnp.concatenate(
-        [along_cols(grad_attn, half[:, 3 * width :]).astype(bf16) for half in weight], axis=1
-    )
-    grad_mixed = at.restored(grad_mixed)
+    grad_mixed = at.restored(unproject(grad_attn[None], weight, 3).astype(bf16))
     proj_sum = Reduction(at, mixed_cols, grad_attn)
     grad_mixed, *up_sum.received = tied(grad_mixed, *up_sum.received)
     grad_mixed, block, *blocks = tied(grad_mixed, proj_sum.first(), *up_sum.middle())
@@ -613,15 +606,14 @@
     down_share = total_of(down_came)
     column_sums = jnp.sum(grad_rows.astype(f32), axis=1)
     grad_bqv = jnp.concatenate([column_sums[0], column_sums[2]])
-    grad_normed = [unproject(grad_rows, weight[0])]
-    grad_normed[0], qkv_sum.received, proj_sum.received = tied(
-        grad_normed[0], qkv_sum.received, proj_sum.received
-    )
-    grad_rows, block, *blocks = tied(grad_rows, proj_sum.last(), *qkv_sum.middle())
+    grad_normed = unproject(grad_rows, weight, 0)
+    grad_normed, qkv_sum.received, proj_sum.received = tied(
+        grad_normed, qkv_sum.received, proj_sum.received
+    )
+    grad_normed, block, *blocks = tied(grad_normed, proj_sum.last(), *qkv_sum.middle())
     qkv_sum.send_middle(blocks)
     proj_came = proj_sum.swap_last(block)
-    grad_normed.append(unproject(grad_rows, weight[1]))
-    grad_normed = at.restored(jnp.concatenate(grad_normed, axis=1))
+    grad_normed = at.restored(grad_normed)
     _, first_back = jax.vjp(modulate, tokens, shift_a, scale_a)
     grad_tokens, grad_shift_a, grad_scale_a = first_back(grad_normed)
     hidden_rows = (grad_tokens + grad_middle).astype(bf16)

time: 566 us -> 580 us (1.025)
  other arithmetic: 36.9 us -> 49.3 us
  starting transfers between devices: 92.4 us -> 100 us
  local copies, waits for them, and re-layouts: 59.1 us -> 51.8 us
  Pallas kernels: 109 us -> 116 us
    ppermute x4, starting transfers between devices: 9.51 us -> 16.6 us  [to_pairs(): parts.append(lax.ppermute(block, AXES, move))]
    ppermute x25 -> x28, waiting for transfers between devices: 55.8 us -> 59.5 us  [across(): lax.ppermute(array, 'shard', [(s, s ^ mask) for s in range(self.shards)])]
    unnamed x158 -> x169, local copies, waits for them, and re-layouts: 28.7 us -> 25.3 us
    ppermute x25 -> x28, starting transfers between devices: 34.5 us -> 34.1 us  [across(): lax.ppermute(array, 'shard', [(s, s ^ mask) for s in range(self.shards)])]
  transfers between devices with their start and end apart: 47 -> 50, of which waited for: 12 -> 15; matrix products, arithmetic and copies ran while one was open for 15% -> 14% of each run, Pallas kernels for 19% -> 20%
where the time goes in v3:
time: 580 us; the launch traced here: 572 us
  waiting for transfers between devices  169 us (29%)
  Pallas kernels  116 us (20%)
  starting transfers between devices  100 us (17%)
  matrix products  64.5 us (11%)
  local copies, waits for them, and re-layouts  51.8 us (9%)
  other arithmetic  49.3 us (8%)
  between operations  20.8 us (4%)
    ppermute x28, waiting for transfers between devices, across(): lax.ppermute(array, 'shard', [(s, s ^ mask) for s in range(self.shards)])  59.5 us
    dot_general x16, matrix products, cross_rows(): lax.dot_general(left, right, (((0,), (0,)), ((), ())), preferred_element_...  48 us
    all_to_all x2, waiting for transfers between devices, shards(): came = lax.all_to_all(sent, AXES, 0, 0, tiled=True)  40.9 us
    pallas_call x2, Pallas kernels, attend_backward(): call(attend_backward_kernel, 40 * count * count * 2 * HD * steps, grid=(s...  36 us
    ppermute x28, starting transfers between devices, across(): lax.ppermute(array, 'shard', [(s, s ^ mask) for s in range(self.shards)])  34.1 us
    unnamed x169, local copies, waits for them, and re-layouts  25.3 us
    ppermute x3, waiting for transfers between devices, along_seq(): parts.append(lax.ppermute(block, 'seq', shift))  22 us
    all_to_all x3, waiting for transfers between devices, swap_last(): came = lax.all_to_all(block, 'seq', 0, 0, tiled=True)  20.5 us
  transfers between devices with their start and end apart: 50, of which 15 were waited for; matrix products, arithmetic and copies ran while one was open for 14% of the time, Pallas kernels for 20%

profile of v3, /device:TPU:0, one launch (start us, length us, event | category | flops | bytes accessed | tf_op | source)
XLA Modules:
  0.0 571.6 jit_solution(12568739024299606594)
XLA Ops:
  11.6 5.0 collective-permute-start
  18.5 3.7 all-to-all-start
  22.4 4.4 all-to-all-done
  28.1 22.0 %collective-permute-done.1 = bf16[32,4096]{1,0:T(8,128)(2,1)S(1)} collective-permute-done((bf16[32,4096]{1,0:T(8,128)(2,1)S(1)}, bf16[32,4096]{1,0:T(8,128)(2,1)S(1)}, u32[]{:S(2)}, u32[]{:S(2)}) %collective-permute-start.1) | collective-permute-done | bytes 262176 | tf_op jit(solution)/shard_map/ppermute | solution.py:397
  57.8 4.2 all-to-all-start.1
  63.1 5.4 collective-permute-start.3
  73.7 10.8 %all-to-all-done.1 = f32[32,1,3520]{2,1,0:T(1,128)} async-done(((f32[32,1,3520]{2,1,0:T(1,128)}), f32[32,1,3520]{2,1,0:T(1,128)}, u32[]{:S(2)}, u32[]{:S(2)}) %all-to-all-start.1) | async-done | bytes 450592 | tf_op jit(solution)/shard_map/all_to_all | solution.py:516
  85.6 11.4 %collective-permute-done.4 = bf16[256,1024]{1,0:T(8,128)(2,1)} collective-permute-done((bf16[256,1024]{1,0:T(8,128)(2,1)}, bf16[256,1024]{1,0:T(8,128)(2,1)}, u32[]{:S(2)}, u32[]{:S(2)}) %collective-permute-start.4) | collective-permute-done | bytes 524320 | tf_op jit(solution)/shard_map/ppermute | solution.py:343
  97.0 14.3 %collective-permute-start.5 = (f32[3072]{0:T(1024)S(1)}, f32[3072]{0:T(1024)S(1)}, u32[]{:S(2)}, u32[]{:S(2)}) collective-permute-start(f32[3072]{0:T(1024)S(1)} %slice_reduce_fusion), channel_id=1, source_target_pairs={{0,4},{4,0},{8,12},{12,8},{16,20},{20,16},{24,28},{28,24},{1,5},{5... | collective-permute-start | bytes 36872 | tf_op jit(solution)/shard_map/ppermute | solution.py:365
  117.7 22.5 %collective-permute-done.8.refs_3_ = bf16[128,4096]{1,0:T(8,128)(2,1)} collective-permute-done((bf16[128,4096]{1,0:T(8,128)(2,1)S(1)}, bf16[128,4096]{1,0:T(8,128)(2,1)}, u32[]{:S(2)}, u32[]{:S(2)}) %collective-permute-start.8) | collective-permute-done | bytes 1048608 | tf_op jit(solution)/shard_map/ppermute | solution.py:365
  143.0 3.0 collective-permute-done.10.refs_5_
  148.8 3.5 shard_map.247.refs_0_
  152.4 3.5 shard_map.248.refs_2_
  159.3 2.8 shard_map.246.q_ref
  163.3 5.8 %collective-permute-start.15 = (bf16[256,1024]{1,0:T(8,128)(2,1)}, bf16[256,1024]{1,0:T(8,128)(2,1)}, u32[]{:S(2)}, u32[]{:S(2)}) collective-permute-start(bf16[256,1024]{1,0:T(8,128)(2,1)} %get-tuple-element.340), channel_id=1, source_target_pairs={{0,0},{1,1},{2,4},{3,5},{4,2},{5,3},{6,6},{7,7},{8,8},{9,9},{10,12... | collective-permute-start | bytes 1572872 | tf_op jit(solution)/shard_map/ppermute | solution.py:343
  169.1 3.7 collective-permute-start.16
  172.8 20.3 %shard_map.249 = (bf16[512,1024]{1,0:T(8,128)(2,1)S(1)}, f32[16,1,512]{2,1,0:T(1,128)S(1)}) custom-call(bf16[512,1024]{1,0:T(8,128)(2,1)S(1)} %shard_map.246.q_ref, bf16[512,1024]{1,0:T(8,128)(2,1)} %shard_map.247.refs_0_, bf16[512,1024]{1,0:T(8,128)(2,1)} %collective-permute-done.13.refs_1_, bf16[512,1024]{1,0:T(8,128)(2,1)} %shard_map.248.refs_2_, ...), custom_call_target="tpu_custom_call" | custom-call | flops 85899344 | bytes 429496 | tf_op jit(solution)/shard_map/pallas_call | solution.py:131
  194.9 3.6 shard_map.250
  198.5 2.2 fusion.109
  202.5 19.5 %shard_map.251 = (bf16[512,4096]{1,0:T(8,128)(2,1)}, bf16[512,4096]{1,0:T(8,128)(2,1)}, f32[512,1024]{1,0:T(8,128)S(1)}) custom-call(bf16[512,1024]{1,0:T(8,128)(2,1)S(1)} %add_convert_fusion.6.x_ref, bf16[32,256,1024]{2,1,0:T(8,128)(2,1)} %bitcast.157, bf16[32,256,1024]{2,1,0:T(8,128)(2,1)} %bitcast.158, f32[1,4096]{1,0:T(1,128)S(1)} %bitcast.155, ...), custom_call_target="tpu_custom_call" | custom-call | flops 171798688 | bytes 858993 | tf_op jit(solution)/shard_map/pallas_call | solution.py:228
  222.0 3.7 convert_reduce_fusion.2
  226.8 4.4 convolution_convert_fusion.1
  232.5 15.5 %shard_map.252 = (bf16[512,4096]{1,0:T(8,128)(2,1)}, f32[1,4096]{1,0:T(1,128)S(1)}, f32[512,1024]{1,0:T(8,128)S(1)}) custom-call(bf16[512,1024]{1,0:T(8,128)(2,1)S(1)} %copy-done.12, bf16[32,256,1024]{2,1,0:T(8,128)(2,1)} %bitcast.159, bf16[32,256,1024]{2,1,0:T(8,128)(2,1)} %bitcast.160, bf16[512,4096]{1,0:T(8,128)(2,1)} %get-tuple-element.138.slope_ref), custom_call_target="tpu_custom_call" | custom-call | flops 171798688 | bytes 858993 | tf_op jit(solution)/shard_map/pallas_call | solution.py:267
  248.0 3.9 add_convert_fusion.4
  251.9 3.1 add_convert_fusion.3
  255.0 3.3 add_convert_fusion.2
  258.3 4.4 convolution_convert_fusion
  271.5 2.4 multiply_reduce_fusion
  274.7 2.4 convert_reduce_fusion.3
  277.1 3.9 shard_map.253
  290.5 3.1 fusion.4
  293.6 3.1 fusion.5
  296.6 3.1 fusion.6
  301.0 2.3 fusion.57
  303.3 18.2 %shard_map.254 = (bf16[3,512,1024]{2,1,0:T(8,128)(2,1)}, bf16[2,512,1024]{2,1,0:T(8,128)(2,1)}) custom-call(bf16[512,1024]{1,0:T(8,128)(2,1)S(1)} %copy-done.4, bf16[512,1024]{1,0:T(8,128)(2,1)S(1)} %copy-done.18, f32[16,1,512]{2,1,0:T(1,128)S(1)} %get-tuple-element.150.log_ref, bf16[512,1024]{1,0:T(8,128)(2,1)} %shard_map.247.refs_0_, ...), custom_call_target="tpu_custom_call" | custom-call | flops 107374184 | bytes 536870 | tf_op jit(solution)/shard_map/pallas_call | solution.py:187
  321.5 9.9 %collective-permute-done.21 = bf16[512,1024]{1,0:T(8,128)(2,1)} collective-permute-done((bf16[512,1024]{1,0:T(8,128)(2,1)}, bf16[512,1024]{1,0:T(8,128)(2,1)}, u32[]{:S(2)}, u32[]{:S(2)}) %collective-permute-start.21) | collective-permute-done | bytes 1048608 | tf_op jit(solution)/shard_map/ppermute | solution.py:365
  332.6 4.2 add_convert_fusion.1
  336.7 4.3 all-to-all-start.2
  347.0 17.8 %shard_map.255 = (bf16[3,512,1024]{2,1,0:T(8,128)(2,1)}, bf16[2,512,1024]{2,1,0:T(8,128)(2,1)}) custom-call(bf16[512,1024]{1,0:T(8,128)(2,1)S(1)} %copy-done.5, bf16[512,1024]{1,0:T(8,128)(2,1)S(1)} %copy-done.19, f32[16,1,512]{2,1,0:T(1,128)S(1)} %get-tuple-element.150.log_ref, ...), custom_call_target="tpu_custom_call", output_to_operand_aliasing={{0}: (7, {}), {1}: (8, {})} | custom-call | flops 107374184 | bytes 536870 | tf_op jit(solution)/shard_map/pallas_call | solution.py:187
  371.0 2.1 slice_bitcast_fusion.4
  373.1 16.4 %collective-permute-done.26 = bf16[128,4096]{1,0:T(8,128)(2,1)} collective-permute-done((bf16[128,4096]{1,0:T(8,128)(2,1)}, bf16[128,4096]{1,0:T(8,128)(2,1)}, u32[]{:S(2)}, u32[]{:S(2)}) %collective-permute-start.26) | collective-permute-done | bytes 1048608 | tf_op jit(solution)/shard_map/ppermute | solution.py:365
  389.5 5.9 %fusion.3 = bf16[128,4096]{1,0:T(8,128)(2,1)} fusion(bf16[512,4096]{1,0:T(8,128)(2,1)} %get-tuple-element.143, bf16[128,4096]{1,0:T(8,128)(2,1)} %collective-permute-done.27, bf16[128,4096]{1,0:T(8,128)(2,1)} %collective-permute-done.26, bf16[128,4096]{1,0:T(8,128)(2,1)} %collective-permute-done.25, bf16[512,4096]{1,0:T(8,128)(2,1)} %collective-permute-done.18, ...), kind=kOutput, calls=%fused_computation.9 | convolution fusion | flops 541589504 | bytes 9568260 | tf_op jit(solution)/shard_map/dot_general | solution.py:29
  395.5 4.1 collective-permute-done.28
  402.2 3.7 convert_bitcast_fusion
  406.0 4.9 all-to-all-start.3
  416.7 20.5 %all-to-all-done.3 = bf16[4,32,4096]{2,1,0:T(8,128)(2,1)} async-done(((bf16[4,32,4096]{2,1,0:T(8,128)(2,1)}), bf16[4,32,4096]{2,1,0:T(8,128)(2,1)}, u32[]{:S(2)}, u32[]{:S(2)}) %all-to-all-start.3) | async-done | bytes 1048608 | tf_op jit(solution)/shard_map/all_to_all | solution.py:446
  437.2 2.2 slice_bitcast_fusion
  439.4 2.6 convert_reduce_fusion
  443.4 7.6 %shard_map.256 = f32[512,1024]{1,0:T(8,128)} custom-call(bf16[3,512,1024]{2,1,0:T(8,128)(2,1)} %pad_maximum_fusion.rows_ref, bf16[128,4096]{1,0:T(8,128)(2,1)S(1)} %constant_dynamic-slice_fusion.16.refs_0_, bf16[128,4096]{1,0:T(8,128)(2,1)S(1)} %collective-permute-done.6.refs_1_, bf16[128,4096]{1,0:T(8,128)(2,1)S(1)} %copy-done.2, ...), custom_call_target="tpu_custom_call" | custom-call | flops 64424508 | bytes 322122 | tf_op jit(solution)/shard_map/pallas_call | solution.py:94
  451.1 2.9 fusion.33
  454.0 2.8 fusion.32
  456.8 2.8 fusion.31
  459.6 2.5 fusion.37
  464.4 2.5 fusion.106
  467.5 3.2 fusion.19
  470.8 3.4 all-to-all-start.5
  478.2 5.4 collective-permute-start.34
  490.3 3.6 all-to-all-start.4
  493.9 2.1 convert_add_fusion.3
  496.7 30.0 %all-to-all-done.4 = f32[32,1,3328]{2,1,0:T(1,128)} async-done(((f32[32,1,3328]{2,1,0:T(1,128)}), f32[32,1,3328]{2,1,0:T(1,128)}, u32[]{:S(2)}, u32[]{:S(2)}) %all-to-all-start.4) | async-done | bytes 426016 | tf_op jit(solution)/shard_map/all_to_all | solution.py:635
  527.8 3.9 fusion.30
  533.0 4.3 all-to-all-start.6
  538.5 3.7 collective-permute-start.41
  552.6 10.2 %collective-permute-done.40 = bf16[3,32,1024]{2,1,0:T(8,128)(2,1)S(1)} collective-permute-done((bf16[3,32,1024]{2,1,0:T(8,128)(2,1)S(1)}, bf16[3,32,1024]{2,1,0:T(8,128)(2,1)S(1)}, u32[]{:S(2)}, u32[]{:S(2)}) %collective-permute-start.40) | collective-permute-done | bytes 196640 | tf_op jit(solution)/shard_map/ppermute | solution.py:464
  (348 shorter events, 113.0 us)
Async XLA Ops:
  7.2 15.0 %copy-start.57 = (bf16[192]{0:T(256)(128)(2,1)S(1)}, bf16[192]{0:T(256)(128)(2,1)}, u32[]{:S(2)}) copy-start(bf16[192]{0:T(256)(128)(2,1)} %param.23) | copy-start | bytes 1156
  7.2 15.0 %copy-start.58 = (bf16[64]{0:T(256)(128)(2,1)S(1)}, bf16[64]{0:T(256)(128)(2,1)}, u32[]{:S(2)}) copy-start(bf16[64]{0:T(256)(128)(2,1)} %param.24) | copy-start | bytes 388
  7.2 15.0 %copy-start.59 = (bf16[32]{0:T(256)(128)(2,1)S(1)}, bf16[32]{0:T(256)(128)(2,1)}, u32[]{:S(2)}) copy-start(bf16[32]{0:T(256)(128)(2,1)} %param.25) | copy-start | bytes 196
  7.2 15.0 %copy-start.60 = (bf16[128]{0:T(256)(128)(2,1)S(1)}, bf16[128]{0:T(256)(128)(2,1)}, u32[]{:S(2)}) copy-start(bf16[128]{0:T(256)(128)(2,1)} %param.26) | copy-start | bytes 772
  7.3 15.0 %copy-start.61 = (bf16[32]{0:T(256)(128)(2,1)S(1)}, bf16[32]{0:T(256)(128)(2,1)}, u32[]{:S(2)}) copy-start(bf16[32]{0:T(256)(128)(2,1)} %param.27) | copy-start | bytes 196
  7.3 19.7 %copy-start.41 = (bf16[32,6144]{1,0:T(8,128)(2,1)S(1)}, bf16[32,6144]{1,0:T(8,128)(2,1)}, u32[]{:S(2)}) copy-start(bf16[32,6144]{1,0:T(8,128)(2,1)} %param.18) | copy-start | bytes 1179652
  7.3 195.2 %all-gather.3.cloned.1.call-start = ((), (), s32[]{:S(2)}) async-start(), calls=%async_computation.7 | async-start | bytes 17301504 | tf_op jit(solution)/shard_map/all_gather | solution.py:286
  11.6 15.7 %collective-permute-start = (bf16[32,4096]{1,0:T(8,128)(2,1)S(1)}, bf16[32,4096]{1,0:T(8,128)(2,1)S(1)}, u32[]{:S(2)}, u32[]{:S(2)}) collective-permute-start(bf16[32,4096]{1,0:T(8,128)(2,1)S(1)} %get-tuple-element.356), channel_id=1, source_target_pairs={{0,3},{1,0},{2,1},{3,2},{4,7},{5,4},{6,5},{7,6},{8,11},{9,8},{10,9... | collective-permute-start | bytes 786440 | tf_op jit(solution)/shard_map/ppermute | solution.py:397
  16.7 33.4 %collective-permute-start.1 = (bf16[32,4096]{1,0:T(8,128)(2,1)S(1)}, bf16[32,4096]{1,0:T(8,128)(2,1)S(1)}, u32[]{:S(2)}, u32[]{:S(2)}) collective-permute-start(bf16[32,4096]{1,0:T(8,128)(2,1)S(1)} %get-tuple-element.356), channel_id=1, source_target_pairs={{0,2},{1,3},{2,0},{3,1},{4,6},{5,7},{6,4},{7,5},{8,10},{9,11},{10,... | collective-permute-start | bytes 786440 | tf_op jit(solution)/shard_map/ppermute | solution.py:397
  16.7 34.1 %collective-permute-start.2 = (bf16[32,4096]{1,0:T(8,128)(2,1)S(1)}, bf16[32,4096]{1,0:T(8,128)(2,1)S(1)}, u32[]{:S(2)}, u32[]{:S(2)}) collective-permute-start(bf16[32,4096]{1,0:T(8,128)(2,1)S(1)} %get-tuple-element.356), channel_id=1, source_target_pairs={{0,1},{1,2},{2,3},{3,0},{4,5},{5,6},{6,7},{7,4},{8,9},{9,10},{10,1... | collective-permute-start | bytes 786440 | tf_op jit(solution)/shard_map/ppermute | solution.py:397
  18.5 8.3 %all-to-all-start = ((bf16[8,1,64]{2,1,0:T(2,128)(2,1)}), bf16[8,1,64]{2,1,0:T(2,128)(2,1)S(1)}, u32[]{:S(2)}, u32[]{:S(2)}) async-start(bf16[8,1,64]{2,1,0:T(2,128)(2,1)} %all_to_all.62), calls=%async_computation | async-start | bytes 8192 | tf_op jit(solution)/shard_map/all_to_all | solution.py:507
  57.8 26.7 %all-to-all-start.1 = ((f32[32,1,3520]{2,1,0:T(1,128)}), f32[32,1,3520]{2,1,0:T(1,128)}, u32[]{:S(2)}, u32[]{:S(2)}) async-start(f32[32,1,3520]{2,1,0:T(1,128)} %all_to_all.48), calls=%async_computation.1 | async-start | bytes 917504 | tf_op jit(solution)/shard_map/all_to_all | solution.py:516
  63.1 22.5 %collective-permute-start.3 = (bf16[256,1024]{1,0:T(8,128)(2,1)}, bf16[256,1024]{1,0:T(8,128)(2,1)}, u32[]{:S(2)}, u32[]{:S(2)}) collective-permute-start(bf16[256,1024]{1,0:T(8,128)(2,1)} %get-tuple-element.342), channel_id=1, source_target_pairs={{0,0},{1,1},{2,4},{3,5},{4,2},{5,3},{6,6},{7,7},{8,8},{9,9},{10,12... | collective-permute-start | bytes 1572872 | tf_op jit(solution)/shard_map/ppermute | solution.py:343
  68.5 28.5 %collective-permute-start.4 = (bf16[256,1024]{1,0:T(8,128)(2,1)}, bf16[256,1024]{1,0:T(8,128)(2,1)}, u32[]{:S(2)}, u32[]{:S(2)}) collective-permute-start(bf16[256,1024]{1,0:T(8,128)(2,1)} %get-tuple-element.341), channel_id=1, source_target_pairs={{0,1},{1,0},{2,5},{3,4},{4,3},{5,2},{6,7},{7,6},{8,9},{9,8},{10,13... | collective-permute-start | bytes 1572872 | tf_op jit(solution)/shard_map/ppermute | solution.py:343
  70.2 47.5 %collective-permute-start.6 = (bf16[128,4096]{1,0:T(8,128)(2,1)S(1)}, bf16[128,4096]{1,0:T(8,128)(2,1)S(1)}, u32[]{:S(2)}, u32[]{:S(2)}) collective-permute-start(bf16[128,4096]{1,0:T(8,128)(2,1)S(1)} %constant_dynamic-slice_fusion.16.refs_0_), channel_id=1, source_target_pairs={{0,8},{4,12},{8,0},{12,4},{16,24},{20,28},{24,16},{28,20},{1,9},{5... | collective-permute-start | bytes 3145736 | tf_op jit(solution)/shard_map/ppermute | solution.py:365
  71.7 46.1 %collective-permute-start.7 = (bf16[128,4096]{1,0:T(8,128)(2,1)S(1)}, bf16[128,4096]{1,0:T(8,128)(2,1)S(1)}, u32[]{:S(2)}, u32[]{:S(2)}) collective-permute-start(bf16[128,4096]{1,0:T(8,128)(2,1)S(1)} %constant_dynamic-slice_fusion.16.refs_0_), channel_id=1, source_target_pairs={{0,16},{4,20},{8,24},{12,28},{16,0},{20,4},{24,8},{28,12},{1,17},{... | collective-permute-start | bytes 3145736 | tf_op jit(solution)/shard_map/ppermute | solution.py:365
  73.1 67.1 %collective-permute-start.8 = (bf16[128,4096]{1,0:T(8,128)(2,1)S(1)}, bf16[128,4096]{1,0:T(8,128)(2,1)}, u32[]{:S(2)}, u32[]{:S(2)}) collective-permute-start(bf16[128,4096]{1,0:T(8,128)(2,1)S(1)} %constant_dynamic-slice_fusion.16.refs_0_), channel_id=1, source_target_pairs={{0,24},{4,28},{8,16},{12,20},{16,8},{20,12},{24,0},{28,4},{1,25},{... | collective-permute-start | bytes 3145736 | tf_op jit(solution)/shard_map/ppermute | solution.py:365
  85.6 28.9 %copy-start.39 = (f32[32,1,3520]{2,0,1:T(8,128)}, f32[32,1,3520]{2,0,1:T(8,128)S(1)}, u32[]{:S(2)}) copy-start(f32[32,1,3520]{2,0,1:T(8,128)S(1)} %copy.152) | copy-start | bytes 1351684
  97.0 17.5 %collective-permute-start.5 = (f32[3072]{0:T(1024)S(1)}, f32[3072]{0:T(1024)S(1)}, u32[]{:S(2)}, u32[]{:S(2)}) collective-permute-start(f32[3072]{0:T(1024)S(1)} %slice_reduce_fusion), channel_id=1, source_target_pairs={{0,4},{4,0},{8,12},{12,8},{16,20},{20,16},{24,28},{28,24},{1,5},{5... | collective-permute-start | bytes 36872 | tf_op jit(solution)/shard_map/ppermute | solution.py:365
  117.7 77.2 %copy-start = (bf16[128,4096]{1,0:T(8,128)(2,1)}, bf16[128,4096]{1,0:T(8,128)(2,1)S(1)}, u32[]{:S(2)}) copy-start(bf16[128,4096]{1,0:T(8,128)(2,1)S(1)} %collective-permute-done.7.refs_2_) | copy-start | bytes 3145732
  140.2 2.8 collective-permute-start.9
  140.2 5.8 %collective-permute-start.10 = (bf16[128,4096]{1,0:T(8,128)(2,1)S(1)}, bf16[128,4096]{1,0:T(8,128)(2,1)}, u32[]{:S(2)}, u32[]{:S(2)}) collective-permute-start(bf16[128,4096]{1,0:T(8,128)(2,1)S(1)} %collective-permute-done.6.refs_1_), channel_id=1, source_target_pairs={{0,4},{4,0},{8,12},{12,8},{16,20},{20,16},{24,28},{28,24},{1,5},{5... | collective-permute-start | bytes 3145736 | tf_op jit(solution)/shard_map/ppermute | solution.py:365
  140.8 6.8 %collective-permute-start.11 = (bf16[128,4096]{1,0:T(8,128)(2,1)S(1)}, bf16[128,4096]{1,0:T(8,128)(2,1)}, u32[]{:S(2)}, u32[]{:S(2)}) collective-permute-start(bf16[128,4096]{1,0:T(8,128)(2,1)S(1)} %collective-permute-done.7.refs_2_), channel_id=1, source_target_pairs={{0,4},{4,0},{8,12},{12,8},{16,20},{20,16},{24,28},{28,24},{1,5},{5... | collective-permute-start | bytes 3145736 | tf_op jit(solution)/shard_map/ppermute | solution.py:365
  140.8 6.8 %collective-permute-start.12 = (bf16[128,4096]{1,0:T(8,128)(2,1)}, bf16[128,4096]{1,0:T(8,128)(2,1)}, u32[]{:S(2)}, u32[]{:S(2)}) collective-permute-start(bf16[128,4096]{1,0:T(8,128)(2,1)} %collective-permute-done.8.refs_3_), channel_id=1, source_target_pairs={{0,4},{4,0},{8,12},{12,8},{16,20},{20,16},{24,28},{28,24},{1,5},{5... | collective-permute-start | bytes 3145736 | tf_op jit(solution)/shard_map/ppermute | solution.py:365
  152.2 20.6 %collective-permute-start.13 = (bf16[512,1024]{1,0:T(8,128)(2,1)}, bf16[512,1024]{1,0:T(8,128)(2,1)}, u32[]{:S(2)}, u32[]{:S(2)}) collective-permute-start(bf16[512,1024]{1,0:T(8,128)(2,1)} %shard_map.247.refs_0_), channel_id=1, source_target_pairs={{0,4},{4,0},{8,12},{12,8},{16,20},{20,16},{24,28},{28,24},{1,5},{5... | collective-permute-start | bytes 3145736 | tf_op jit(solution)/shard_map/ppermute | solution.py:365
  155.9 17.0 %collective-permute-start.14 = (bf16[512,1024]{1,0:T(8,128)(2,1)}, bf16[512,1024]{1,0:T(8,128)(2,1)}, u32[]{:S(2)}, u32[]{:S(2)}) collective-permute-start(bf16[512,1024]{1,0:T(8,128)(2,1)} %shard_map.248.refs_2_), channel_id=1, source_target_pairs={{0,4},{4,0},{8,12},{12,8},{16,20},{20,16},{24,28},{28,24},{1,5},{5... | collective-permute-start | bytes 3145736 | tf_op jit(solution)/shard_map/ppermute | solution.py:365
  162.2 30.9 %copy-start.3 = (bf16[512,1024]{1,0:T(8,128)(2,1)}, bf16[512,1024]{1,0:T(8,128)(2,1)S(1)}, u32[]{:S(2)}) copy-start(bf16[512,1024]{1,0:T(8,128)(2,1)S(1)} %shard_map.246.q_ref) | copy-start | bytes 3145732
  163.3 58.7 %collective-permute-start.15 = (bf16[256,1024]{1,0:T(8,128)(2,1)}, bf16[256,1024]{1,0:T(8,128)(2,1)}, u32[]{:S(2)}, u32[]{:S(2)}) collective-permute-start(bf16[256,1024]{1,0:T(8,128)(2,1)} %get-tuple-element.340), channel_id=1, source_target_pairs={{0,0},{1,1},{2,4},{3,5},{4,2},{5,3},{6,6},{7,7},{8,8},{9,9},{10,12... | collective-permute-start | bytes 1572872 | tf_op jit(solution)/shard_map/ppermute | solution.py:343
  169.1 52.9 %collective-permute-start.16 = (bf16[256,1024]{1,0:T(8,128)(2,1)}, bf16[256,1024]{1,0:T(8,128)(2,1)}, u32[]{:S(2)}, u32[]{:S(2)}) collective-permute-start(bf16[256,1024]{1,0:T(8,128)(2,1)} %get-tuple-element.339), channel_id=1, source_target_pairs={{0,1},{1,0},{2,5},{3,4},{4,3},{5,2},{6,7},{7,6},{8,9},{9,8},{10,13... | collective-permute-start | bytes 1572872 | tf_op jit(solution)/shard_map/ppermute | solution.py:343
  202.5 28.7 %copy-start.10 = (bf16[512,1024]{1,0:T(8,128)(2,1)}, bf16[512,1024]{1,0:T(8,128)(2,1)S(1)}, u32[]{:S(2)}) copy-start(bf16[512,1024]{1,0:T(8,128)(2,1)S(1)} %add_convert_fusion.6.x_ref) | copy-start | bytes 3145732
  202.5 19.5 %copy-start.24 = (f32[512,1024]{1,0:T(8,128)S(1)}, f32[512,1024]{1,0:T(8,128)}, u32[]{:S(2)}) copy-start(f32[512,1024]{1,0:T(8,128)} %copy-done.23) | copy-start | bytes 6291460
  231.2 16.9 %collective-permute-start.17 = (bf16[2048,1024]{1,0:T(8,128)(2,1)}, bf16[2048,1024]{1,0:T(8,128)(2,1)}, u32[]{:S(2)}, u32[]{:S(2)}) collective-permute-start(bf16[2048,1024]{1,0:T(8,128)(2,1)} %convolution_convert_fusion.1), channel_id=1, source_target_pairs={{0,4},{4,0},{8,12},{12,8},{16,20},{20,16},{24,28},{28,24},{1,5},{5... | collective-permute-start | bytes 12582920 | tf_op jit(solution)/shard_map/ppermute | solution.py:365
  262.7 26.9 %collective-permute-start.18 = (bf16[512,4096]{1,0:T(8,128)(2,1)}, bf16[512,4096]{1,0:T(8,128)(2,1)}, u32[]{:S(2)}, u32[]{:S(2)}) collective-permute-start(bf16[512,4096]{1,0:T(8,128)(2,1)} %convolution_convert_fusion), channel_id=1, source_target_pairs={{0,4},{4,0},{8,12},{12,8},{16,20},{20,16},{24,28},{28,24},{1,5},{5... | collective-permute-start | bytes 12582920 | tf_op jit(solution)/shard_map/ppermute | solution.py:365
  269.9 29.8 %collective-permute-start.23 = (bf16[256,1024]{1,0:T(8,128)(2,1)S(1)}, bf16[256,1024]{1,0:T(8,128)(2,1)}, u32[]{:S(2)}, u32[]{:S(2)}) collective-permute-start(bf16[256,1024]{1,0:T(8,128)(2,1)S(1)} %get-tuple-element.334), channel_id=1, source_target_pairs={{0,0},{1,1},{4,2},{5,3},{2,4},{3,5},{6,6},{7,7},{8,8},{9,9},{12,10... | collective-permute-start | bytes 1572872 | tf_op jit(solution)/shard_map/ppermute | solution.py:351
  282.9 38.7 %collective-permute-start.20 = (bf16[512,1024]{1,0:T(8,128)(2,1)}, bf16[512,1024]{1,0:T(8,128)(2,1)}, u32[]{:S(2)}, u32[]{:S(2)}) collective-permute-start(bf16[512,1024]{1,0:T(8,128)(2,1)} %add_convert_fusion.4), channel_id=1, source_target_pairs={{0,8},{4,12},{8,0},{12,4},{16,24},{20,28},{24,16},{28,20},{1,9},{5... | collective-permute-start | bytes 3145736 | tf_op jit(solution)/shard_map/ppermute | solution.py:365
  284.3 47.1 %collective-permute-start.21 = (bf16[512,1024]{1,0:T(8,128)(2,1)}, bf16[512,1024]{1,0:T(8,128)(2,1)}, u32[]{:S(2)}, u32[]{:S(2)}) collective-permute-start(bf16[512,1024]{1,0:T(8,128)(2,1)} %add_convert_fusion.3), channel_id=1, source_target_pairs={{0,16},{4,20},{8,24},{12,28},{16,0},{20,4},{24,8},{28,12},{1,17},{... | collective-permute-start | bytes 3145736 | tf_op jit(solution)/shard_map/ppermute | solution.py:365
  285.7 46.9 %collective-permute-start.22 = (bf16[512,1024]{1,0:T(8,128)(2,1)}, bf16[512,1024]{1,0:T(8,128)(2,1)}, u32[]{:S(2)}, u32[]{:S(2)}) collective-permute-start(bf16[512,1024]{1,0:T(8,128)(2,1)} %add_convert_fusion.2), channel_id=1, source_target_pairs={{0,24},{4,28},{8,16},{12,20},{16,8},{20,12},{24,0},{28,4},{1,25},{... | collective-permute-start | bytes 3145736 | tf_op jit(solution)/shard_map/ppermute | solution.py:365
  299.7 32.8 %collective-permute-start.19 = (bf16[512,1024]{1,0:T(8,128)(2,1)}, bf16[512,1024]{1,0:T(8,128)(2,1)}, u32[]{:S(2)}, u32[]{:S(2)}) collective-permute-start(bf16[512,1024]{1,0:T(8,128)(2,1)} %convolution_convert_fusion.2), channel_id=1, source_target_pairs={{0,4},{4,0},{8,12},{12,8},{16,20},{20,16},{24,28},{28,24},{1,5},{5... | collective-permute-start | bytes 3145736 | tf_op jit(solution)/shard_map/ppermute | solution.py:365
  299.7 21.8 %collective-permute-start.24 = (bf16[256,1024]{1,0:T(8,128)(2,1)}, bf16[256,1024]{1,0:T(8,128)(2,1)}, u32[]{:S(2)}, u32[]{:S(2)}) collective-permute-start(bf16[256,1024]{1,0:T(8,128)(2,1)} %get-tuple-element.333), channel_id=1, source_target_pairs={{1,0},{0,1},{5,2},{4,3},{3,4},{2,5},{7,6},{6,7},{9,8},{8,9},{13,10... | collective-permute-start | bytes 1572872 | tf_op jit(solution)/shard_map/ppermute | solution.py:351
  336.7 34.3 %all-to-all-start.2 = ((bf16[4,128,1024]{2,1,0:T(8,128)(2,1)}), bf16[4,128,1024]{2,1,0:T(8,128)(2,1)}, u32[]{:S(2)}, u32[]{:S(2)}) async-start(bf16[4,128,1024]{2,1,0:T(8,128)(2,1)} %bitcast.162), calls=%async_computation.2 | async-start | bytes 2097152 | tf_op jit(solution)/shard_map/all_to_all | solution.py:446
  341.0 32.1 %collective-permute-start.25 = (bf16[128,4096]{1,0:T(8,128)(2,1)}, bf16[128,4096]{1,0:T(8,128)(2,1)}, u32[]{:S(2)}, u32[]{:S(2)}) collective-permute-start(bf16[128,4096]{1,0:T(8,128)(2,1)} %fusion.4), channel_id=1, source_target_pairs={{0,8},{4,12},{8,0},{12,4},{16,24},{20,28},{24,16},{28,20},{1,9},{5... | collective-permute-start | bytes 3145736 | tf_op jit(solution)/shard_map/ppermute | solution.py:365
  342.1 47.4 %collective-permute-start.26 = (bf16[128,4096]{1,0:T(8,128)(2,1)}, bf16[128,4096]{1,0:T(8,128)(2,1)}, u32[]{:S(2)}, u32[]{:S(2)}) collective-permute-start(bf16[128,4096]{1,0:T(8,128)(2,1)} %fusion.5), channel_id=1, source_target_pairs={{0,16},{4,20},{8,24},{12,28},{16,0},{20,4},{24,8},{28,12},{1,17},{... | collective-permute-start | bytes 3145736 | tf_op jit(solution)/shard_map/ppermute | solution.py:365
  343.3 46.2 %collective-permute-start.27 = (bf16[128,4096]{1,0:T(8,128)(2,1)}, bf16[128,4096]{1,0:T(8,128)(2,1)}, u32[]{:S(2)}, u32[]{:S(2)}) collective-permute-start(bf16[128,4096]{1,0:T(8,128)(2,1)} %fusion.6), channel_id=1, source_target_pairs={{0,24},{4,28},{8,16},{12,20},{16,8},{20,12},{24,0},{28,4},{1,25},{... | collective-permute-start | bytes 3145736 | tf_op jit(solution)/shard_map/ppermute | solution.py:365
  395.4 4.2 collective-permute-start.28
  405.9 45.3 %collective-permute-start.29 = (bf16[3,512,1024]{2,1,0:T(8,128)(2,1)}, bf16[3,512,1024]{2,1,0:T(8,128)(2,1)}, u32[]{:S(2)}, u32[]{:S(2)}) collective-permute-start(bf16[3,512,1024]{2,1,0:T(8,128)(2,1)} %convert_bitcast_fusion), channel_id=1, source_target_pairs={{0,4},{4,0},{8,12},{12,8},{16,20},{20,16},{24,28},{28,24},{1,5},{5... | collective-permute-start | bytes 9437192 | tf_op jit(solution)/shard_map/ppermute | solution.py:365
  406.0 31.2 %all-to-all-start.3 = ((bf16[4,32,4096]{2,1,0:T(8,128)(2,1)}), bf16[4,32,4096]{2,1,0:T(8,128)(2,1)}, u32[]{:S(2)}, u32[]{:S(2)}) async-start(bf16[4,32,4096]{2,1,0:T(8,128)(2,1)} %bitcast.161), calls=%async_computation.3 | async-start | bytes 2097152 | tf_op jit(solution)/shard_map/all_to_all | solution.py:446
  411.2 39.9 %collective-permute-start.30 = (bf16[128,1024]{1,0:T(8,128)(2,1)}, bf16[128,1024]{1,0:T(8,128)(2,1)}, u32[]{:S(2)}, u32[]{:S(2)}) collective-permute-start(bf16[128,1024]{1,0:T(8,128)(2,1)} %fusion.38), channel_id=1, source_target_pairs={{0,8},{4,12},{8,0},{12,4},{16,24},{20,28},{24,16},{28,20},{1,9},{5... | collective-permute-start | bytes 786440 | tf_op jit(solution)/shard_map/ppermute | solution.py:365
  412.3 38.8 %collective-permute-start.31 = (bf16[128,1024]{1,0:T(8,128)(2,1)}, bf16[128,1024]{1,0:T(8,128)(2,1)}, u32[]{:S(2)}, u32[]{:S(2)}) collective-permute-start(bf16[128,1024]{1,0:T(8,128)(2,1)} %fusion.39), channel_id=1, source_target_pairs={{0,16},{4,20},{8,24},{12,28},{16,0},{20,4},{24,8},{28,12},{1,17},{... | collective-permute-start | bytes 786440 | tf_op jit(solution)/shard_map/ppermute | solution.py:365
  413.2 37.9 %collective-permute-start.32 = (bf16[128,1024]{1,0:T(8,128)(2,1)}, bf16[128,1024]{1,0:T(8,128)(2,1)}, u32[]{:S(2)}, u32[]{:S(2)}) collective-permute-start(bf16[128,1024]{1,0:T(8,128)(2,1)} %fusion.40), channel_id=1, source_target_pairs={{0,24},{4,28},{8,16},{12,20},{16,8},{20,12},{24,0},{28,4},{1,25},{... | collective-permute-start | bytes 786440 | tf_op jit(solution)/shard_map/ppermute | solution.py:365
  470.8 19.5 %all-to-all-start.5 = ((bf16[4,32,1024]{2,1,0:T(8,128)(2,1)}), bf16[4,32,1024]{2,1,0:T(8,128)(2,1)S(1)}, u32[]{:S(2)}, u32[]{:S(2)}) async-start(bf16[4,32,1024]{2,1,0:T(8,128)(2,1)} %bitcast.173), calls=%async_computation.5 | async-start | bytes 524288 | tf_op jit(solution)/shard_map/all_to_all | solution.py:446
  477.2 11.9 %copy-start.56 = (f32[6144]{0:T(1024)S(1)}, f32[6144]{0:T(1024)}, u32[]{:S(2)}) copy-start(f32[6144]{0:T(1024)} %constant_dynamic-update-slice_fusion.18) | copy-start | bytes 73732
  477.2 10.4 %collective-permute-start.33 = (f32[6144]{0:T(1024)}, f32[6144]{0:T(1024)S(1)}, u32[]{:S(2)}, u32[]{:S(2)}) collective-permute-start(f32[6144]{0:T(1024)} %constant_dynamic-update-slice_fusion.18), channel_id=1, source_target_pairs={{0,4},{4,0},{8,12},{12,8},{16,20},{20,16},{24,28},{28,24},{1,5},{5... | collective-permute-start | bytes 73736 | tf_op jit(solution)/shard_map/ppermute | solution.py:365
  478.2 49.6 %collective-permute-start.34 = (bf16[256,1024]{1,0:T(8,128)(2,1)}, bf16[256,1024]{1,0:T(8,128)(2,1)}, u32[]{:S(2)}, u32[]{:S(2)}) collective-permute-start(bf16[256,1024]{1,0:T(8,128)(2,1)} %get-tuple-element.322), channel_id=1, source_target_pairs={{0,0},{1,1},{4,2},{5,3},{2,4},{3,5},{6,6},{7,7},{8,8},{9,9},{12,10... | collective-permute-start | bytes 1572872 | tf_op jit(solution)/shard_map/ppermute | solution.py:351
  483.6 44.2 %collective-permute-start.35 = (bf16[256,1024]{1,0:T(8,128)(2,1)}, bf16[256,1024]{1,0:T(8,128)(2,1)}, u32[]{:S(2)}, u32[]{:S(2)}) collective-permute-start(bf16[256,1024]{1,0:T(8,128)(2,1)} %get-tuple-element.321), channel_id=1, source_target_pairs={{1,0},{0,1},{5,2},{4,3},{3,4},{2,5},{7,6},{6,7},{9,8},{8,9},{13,10... | collective-permute-start | bytes 1572872 | tf_op jit(solution)/shard_map/ppermute | solution.py:351
  485.6 42.2 %collective-permute-start.36 = (bf16[3,128,1024]{2,1,0:T(8,128)(2,1)}, bf16[3,128,1024]{2,1,0:T(8,128)(2,1)}, u32[]{:S(2)}, u32[]{:S(2)}) collective-permute-start(bf16[3,128,1024]{2,1,0:T(8,128)(2,1)} %fusion.33), channel_id=1, source_target_pairs={{0,8},{4,12},{8,0},{12,4},{16,24},{20,28},{24,16},{28,20},{1,9},{5... | collective-permute-start | bytes 2359304 | tf_op jit(solution)/shard_map/ppermute | solution.py:365
  486.6 41.2 %collective-permute-start.37 = (bf16[3,128,1024]{2,1,0:T(8,128)(2,1)}, bf16[3,128,1024]{2,1,0:T(8,128)(2,1)}, u32[]{:S(2)}, u32[]{:S(2)}) collective-permute-start(bf16[3,128,1024]{2,1,0:T(8,128)(2,1)} %fusion.32), channel_id=1, source_target_pairs={{0,16},{4,20},{8,24},{12,28},{16,0},{20,4},{24,8},{28,12},{1,17},{... | collective-permute-start | bytes 2359304 | tf_op jit(solution)/shard_map/ppermute | solution.py:365
  487.5 40.3 %collective-permute-start.38 = (bf16[3,128,1024]{2,1,0:T(8,128)(2,1)}, bf16[3,128,1024]{2,1,0:T(8,128)(2,1)}, u32[]{:S(2)}, u32[]{:S(2)}) collective-permute-start(bf16[3,128,1024]{2,1,0:T(8,128)(2,1)} %fusion.31), channel_id=1, source_target_pairs={{0,24},{4,28},{8,16},{12,20},{16,8},{20,12},{24,0},{28,4},{1,25},{... | collective-permute-start | bytes 2359304 | tf_op jit(solution)/shard_map/ppermute | solution.py:365
  490.3 37.6 %copy-start.32 = (bf16[2,512,1024]{2,1,0:T(8,128)(2,1)S(1)}, bf16[2,512,1024]{2,1,0:T(8,128)(2,1)}, u32[]{:S(2)}) copy-start(bf16[2,512,1024]{2,1,0:T(8,128)(2,1)} %copy-done.30) | copy-start | bytes 6291460
  490.3 37.6 %copy-start.36 = (bf16[1,512,1024]{2,1,0:T(8,128)(2,1)S(1)}, bf16[1,512,1024]{2,1,0:T(8,128)(2,1)}, u32[]{:S(2)}) copy-start(bf16[1,512,1024]{2,1,0:T(8,128)(2,1)} %copy-done.34) | copy-start | bytes 3145732
  490.3 36.5 %all-to-all-start.4 = ((f32[32,1,3328]{2,1,0:T(1,128)}), f32[32,1,3328]{2,1,0:T(1,128)}, u32[]{:S(2)}, u32[]{:S(2)}) async-start(f32[32,1,3328]{2,1,0:T(1,128)} %all_to_all.55), calls=%async_computation.4 | async-start | bytes 851968 | tf_op jit(solution)/shard_map/all_to_all | solution.py:635
  533.0 17.5 %all-to-all-start.6 = ((f32[32,1,64]{2,1,0:T(1,128)}), f32[32,1,64]{2,1,0:T(1,128)S(1)}, u32[]{:S(2)}, u32[]{:S(2)}) async-start(f32[32,1,64]{2,1,0:T(1,128)} %bitcast.53), calls=%async_computation.6 | async-start | bytes 32768 | tf_op jit(solution)/shard_map/all_to_all | solution.py:657
  538.5 14.0 %collective-permute-start.41 = (bf16[3,32,1024]{2,1,0:T(8,128)(2,1)S(1)}, bf16[3,32,1024]{2,1,0:T(8,128)(2,1)S(1)}, u32[]{:S(2)}, u32[]{:S(2)}) collective-permute-start(bf16[3,32,1024]{2,1,0:T(8,128)(2,1)S(1)} %get-tuple-element.344), channel_id=1, source_target_pairs={{0,3},{1,0},{2,1},{3,2},{4,7},{5,4},{6,5},{7,6},{8,11},{9,8},{10,9... | collective-permute-start | bytes 589832 | tf_op jit(solution)/shard_map/ppermute | solution.py:464
  548.8 13.9 %collective-permute-start.40 = (bf16[3,32,1024]{2,1,0:T(8,128)(2,1)S(1)}, bf16[3,32,1024]{2,1,0:T(8,128)(2,1)S(1)}, u32[]{:S(2)}, u32[]{:S(2)}) collective-permute-start(bf16[3,32,1024]{2,1,0:T(8,128)(2,1)S(1)} %get-tuple-element.345), channel_id=1, source_target_pairs={{0,2},{1,3},{2,0},{3,1},{4,6},{5,7},{6,4},{7,5},{8,10},{9,11},{10,... | collective-permute-start | bytes 589832 | tf_op jit(solution)/shard_map/ppermute | solution.py:464
  548.8 13.9 %collective-permute-start.39 = (bf16[3,32,1024]{2,1,0:T(8,128)(2,1)S(1)}, bf16[3,32,1024]{2,1,0:T(8,128)(2,1)S(1)}, u32[]{:S(2)}, u32[]{:S(2)}) collective-permute-start(bf16[3,32,1024]{2,1,0:T(8,128)(2,1)S(1)} %get-tuple-element.343), channel_id=1, source_target_pairs={{0,1},{1,2},{2,3},{3,0},{4,5},{5,6},{6,7},{7,4},{8,9},{9,10},{10,1... | collective-permute-start | bytes 589832 | tf_op jit(solution)/shard_map/ppermute | solution.py:464
  (48 other events, 173.1 us)
Sparse Core Ops, SparseCore 0:
  11.7 164.1 all-gather.2
